TPU v7x, 32 devices: a whole 2x2x4 slice. The times are simulated.
32 devices in a mesh: groups: 2 (over y), dp: 4 (over z), tensor: 4 (over x, core).
Axes of the slice: x: 2, y: 2, z: 4, core: 2. Of those that a mesh axis runs over, the one named last changes fastest.
Arguments:
- tokens: bfloat16 [2048, 16384], P(('groups', 'dp', 'tensor')), parts along dimension 0, may hold values from -6 to 6
- up_weight: bfloat16 [16384, 26624], P('dp', 'tensor'), may hold values from -0.046875 to 0.046875
- adapter_down: bfloat16 [8, 64, 16384], P('groups', None, ('dp', 'tensor')), parts along dimension 0, may hold values from -0.046875 to 0.046875
- adapter_up: bfloat16 [8, 64, 26624], P('groups', None, 'tensor'), parts along dimension 0, may hold values from -0.75 to 0.75
- grad_out: bfloat16 [2048, 26624], P(('groups', 'dp'), 'tensor'), parts along dimension 0, may hold values from -0.29882812 to 0.29882812
- block_tenant: int32 [16], P('groups'), parts along dimension 0, may hold values from 0 to 3, as said below
- owner_of: int32 [8], P('groups'), parts along dimension 0, may hold values from 0 to 3, as said below
Outputs:
- layer_out: bfloat16 [2048, 26624], P(('groups', 'dp'), 'tensor'), parts along dimension 0
- grad_down: float32 [8, 64, 16384], P('groups', None, ('dp', 'tensor')), parts along dimension 0
- grad_up: float32 [16, 64, 26624], P(('groups', 'dp'), None, 'tensor'), parts along dimension 0
There are 2 independent parts, one for each index of `groups`. A program takes and returns all parts, laid end to end along the dimension named above; an argument that names none is the same for every part. Nothing has to cross between parts.
Inputs may be any that keep to these rules, and one draw needn't show every extreme that they name: `block_tenant`: tenant numbers never fall along the blocks; every tenant names 1 to 3 blocks in a row, and some tenant names exactly 3. `owner_of`: no owner is named by more than 2 tenants; one owner is named by exactly 2.
All inputs are finite; a program needn't handle non-finite values.
Results may differ from a plain program's by a relative error of at most 0.01.
Values may be sent and summed in bfloat16 or wider, within the bound.
No kernel may reach another device: no remote copies, remote signals or barrier semaphores. Data moves between devices by JAX's collectives and lax.ppermute only.
A program may use at most 256 MiB of HBM per device.

v0:
```python
import jax
import jax.numpy as jnp
from jax import lax
from jax.sharding import PartitionSpec as P

ROWS_BLK = 128
OWN_MAX = 2


SCALE = 0.5


def local(tokens, up_weight, adapter_down, adapter_up, grad_out, block_tenant, owner_of):
    dp_count = lax.axis_size("dp")
    dp_index = lax.axis_index("dp")
    tp_index = lax.axis_index("tensor")
    seq_rows, feature_count = tokens.shape
    batch_rows = grad_out.shape[0]
    local_blocks = batch_rows // ROWS_BLK
    all_blocks = local_blocks * dp_count
    column_part = feature_count // dp_count
    slice_cols = adapter_down.shape[2]
    rank_width = adapter_down.shape[1]
    tenants = adapter_down.shape[0]
    gathered = lax.all_gather(tokens, "tensor", axis=0, tiled=True)
    spread = lax.all_to_all(
        gathered.reshape(1, batch_rows, dp_count, column_part),
        "dp",
        split_axis=2,
        concat_axis=0,
        tiled=True,
    )
    all_rows = spread.reshape(dp_count * batch_rows, column_part)
    base_out = lax.psum_scatter(
        jnp.dot(all_rows, up_weight, preferred_element_type=jnp.float32).astype(jnp.bfloat16),
        "dp",
        scatter_dimension=0,
        tiled=True,
    ).astype(jnp.float32)
    slice_start = tp_index * slice_cols
    feature_slice = lax.dynamic_slice_in_dim(all_rows, slice_start, slice_cols, 1).reshape(
        all_blocks, ROWS_BLK, slice_cols
    )
    down_blocks = jnp.take(adapter_down, block_tenant, axis=0)
    proj_part = jnp.einsum(
        "nrd,nkd->nrk", feature_slice, down_blocks, preferred_element_type=jnp.float32
    )
    local_ids = lax.dynamic_slice_in_dim(block_tenant, dp_index * local_blocks, local_blocks, 0)
    up_mine = jnp.take(adapter_up, local_ids, axis=0)
    out_blocks = grad_out.reshape(local_blocks, ROWS_BLK, grad_out.shape[1])
    back_part = jnp.einsum("nrf,nkf->nrk", out_blocks, up_mine, preferred_element_type=jnp.float32)
    back_full = lax.dynamic_update_slice_in_dim(
        jnp.zeros((all_blocks, ROWS_BLK, rank_width), jnp.float32),
        back_part,
        dp_index * local_blocks,
        0,
    )
    proj_sum, back_sum = lax.psum(
        (proj_part.reshape(-1, 2 * rank_width), back_full.reshape(-1, 2 * rank_width)),
        ("dp", "tensor"),
    )
    projected = proj_sum.reshape(all_blocks, ROWS_BLK, rank_width).astype(jnp.bfloat16)
    back_proj = (SCALE * back_sum).reshape(all_blocks, ROWS_BLK, rank_width).astype(jnp.bfloat16)
    proj_mine = lax.dynamic_slice_in_dim(projected, dp_index * local_blocks, local_blocks, 0)
    adapter_term = jnp.einsum(
        "nrk,nkf->nrf", proj_mine, up_mine, preferred_element_type=jnp.float32
    ).reshape(batch_rows, -1)
    layer_out = (base_out + SCALE * adapter_term).astype(jnp.bfloat16)
    down_terms = jnp.einsum(
        "nrk,nrd->nkd", back_proj, feature_slice, preferred_element_type=jnp.float32
    )
    tenant_ids = jnp.arange(tenants, dtype=jnp.int32)
    onehot = (block_tenant[None, :] == tenant_ids[:, None]).astype(jnp.float32)
    inverse = 1.0 / jnp.sum(onehot, axis=1)
    grad_down = (
        jnp.einsum("tn,nkd->tkd", onehot, down_terms, precision=lax.Precision.HIGHEST)
        * inverse[:, None, None]
    )
    up_terms = SCALE * jnp.einsum(
        "nrk,nrf->nkf", proj_mine, out_blocks, preferred_element_type=jnp.float32
    )
    same_owner = owner_of[:, None] == owner_of[None, :]
    earlier = tenant_ids[None, :] < tenant_ids[:, None]
    rank_in = jnp.sum(jnp.logical_and(same_owner, earlier), axis=1)
    slot_of = owner_of * OWN_MAX + rank_in
    own_slots = dp_index * OWN_MAX + jnp.arange(OWN_MAX, dtype=jnp.int32)
    ownership = (slot_of[None, :] == own_slots[:, None]).astype(jnp.float32)
    own_scale = jnp.dot(ownership, inverse, precision=lax.Precision.HIGHEST)
    total_slots = dp_count * OWN_MAX
    local_slots = jnp.take(slot_of, local_ids, axis=0)
    placement = (local_slots[None, :] == jnp.arange(total_slots, dtype=jnp.int32)[:, None]).astype(
        jnp.float32
    )
    buffer = jnp.einsum("sn,nkf->skf", placement, up_terms, precision=lax.Precision.HIGHEST)
    summed = lax.psum_scatter(
        buffer.astype(jnp.bfloat16), "dp", scatter_dimension=0, tiled=True
    ).astype(jnp.float32)
    grad_up = summed * own_scale[:, None, None]
    return (layer_out, grad_down, grad_up)


def solution(mesh):
    placed = (
        P(("groups", "dp", "tensor"), None),
        P("dp", "tensor"),
        P("groups", None, ("dp", "tensor")),
        P("groups", None, "tensor"),
        P(("groups", "dp"), "tensor"),
        P("groups"),
        P("groups"),
    )
    return jax.shard_map(
        local,
        mesh=mesh,
        in_specs=placed,
        out_specs=(
            P(("groups", "dp"), "tensor"),
            P("groups", None, ("dp", "tensor")),
            P(("groups", "dp"), None, "tensor"),
        ),
        check_vma=False,
    )
```

profile of v0, /device:TPU:0, one launch (start us, length us, event | category | flops | bytes accessed | tf_op | source)
XLA Modules:
  0.0 732.6 jit_solution(6067840989318232812)
XLA Ops:
  8.1 0.7 all-gather.2.cloned.1.call-update
  8.7 62.7 %all-gather.2.cloned.1.call-done = bf16[256,16384]{1,0:T(8,128)(2,1)} async-done(((bf16[64,16384]{1,0:T(8,128)(2,1)}), bf16[256,16384]{1,0:T(8,128)(2,1)}) %all-gather.2.cloned.1.call-update) | async-done | bytes 8388624 | tf_op jit(solution)/shard_map/all_gather | solution.py:25
  71.4 11.9 %copy.47 = bf16[256,16384]{0,1:T(8,128)(2,1)} copy(bf16[256,16384]{1,0:T(8,128)(2,1)} %all-gather.2.cloned.1.call-done) | data formatting | bytes 16777216 | tf_op jit(solution)/shard_map/all_gather | solution.py:25
  83.4 11.3 %copy.48 = bf16[1,256,4,4096]{3,1,0,2:T(8,128)(2,1)} copy(bf16[1,256,4,4096]{1,3,2,0:T(8,128)(2,1)} %bitcast.34) | data formatting | bytes 16777216 | tf_op jit(solution)/shard_map/reshape | solution.py:27
  94.7 5.7 all-to-all-start
  100.6 3.8 gather_fusion.1
  104.4 3.4 convolution_bitcast_fusion
  107.8 0.9 copy.51
  108.8 0.8 broadcast_in_dim.47
  109.6 0.7 constant_dynamic-update-slice_fusion
  110.3 1.9 reshape.64
  112.3 0.9 convert_reduce_fusion
  114.5 2.6 gather_fusion
  117.7 168.4 %all-to-all-done = bf16[1,256,4,4096]{3,1,0,2:T(8,128)(2,1)} async-done(((bf16[1,256,4,4096]{3,1,0,2:T(8,128)(2,1)}), bf16[1,256,4,4096]{3,1,0,2:T(8,128)(2,1)}, u32[]{:S(2)}, u32[]{:S(2)}) %all-to-all-start) | async-done | bytes 8388640 | tf_op jit(solution)/shard_map/all_to_all | solution.py:26
  286.1 1.9 constant_dynamic-slice_fusion
  288.0 1.3 copy-done.2
  289.3 1.6 fusion.7
  290.9 1.9 reshape.62
  292.8 60.6 %all-reduce.4 = bf16[512,128]{1,0:T(8,128)(2,1)S(1)} all-reduce(f32[512,128]{1,0:T(8,128)} %reshape.62), channel_id=1, replica_groups=mesh['groups'=2,'dp'=4,'tensor'=4] {'dp','tensor'}, use_global_device_ids=true, to_apply=%region_1.2 | all-reduce | flops 65536 | bytes 393216 | tf_op jit(solution)/shard_map/psum | solution.py:58
  353.4 0.8 convert_element_type.38
  354.2 1.5 convolution_multiply_fusion.1
  355.7 9.7 %convolution_convert_fusion.1 = bf16[8,64,6656]{2,0,1:T(8,128)(2,1)S(1)} fusion(f32[2,64,6656]{2,1,0:T(8,128)S(1)} %convolution_multiply_fusion.1, s32[2]{0:T(128)S(1)} %copy-done.7), kind=kOutput, calls=%fused_computation.4 | convolution fusion | flops 85196816 | bytes 10223624 | tf_op jit(solution)/shard_map/sn,nkf->skf/dot_general | solution.py:94
  365.5 4.8 copy.55
  370.5 65.4 %convolution_convert_fusion = bf16[1024,6656]{1,0:T(8,128)(2,1)} fusion(bf16[1024,4096]{1,0:T(8,128)(2,1)} %bitcast.3, bf16[4096,6656]{1,0:T(8,128)(2,1)} %param.8), kind=kOutput, calls=%fused_computation.3 | convolution fusion | flops 55841390592 | bytes 76546048 | tf_op jit(solution)/shard_map/dot_general | solution.py:35
  436.3 1.2 multiply_convert_fusion
  438.1 2.2 fusion.4
  440.4 1.6 copy.56
  442.0 4.7 convolution_multiply_fusion
  446.6 40.6 %reduce-scatter.5.cloned.1.call-done = bf16[2,64,6656]{2,1,0:T(8,128)(2,1)} async-done(((bf16[8,64,6656]{2,1,0:T(8,128)(2,1)}), bf16[2,64,6656]{2,1,0:T(8,128)(2,1)}) %reduce-scatter.5.cloned.1.call-update) | async-done | bytes 1703952 | tf_op jit(solution)/shard_map/reduce_scatter | solution.py:95
  487.2 3.6 convert_multiply_fusion
  490.9 228.1 %reduce-scatter.3.cloned.1.call-done = bf16[256,6656]{1,0:T(8,128)(2,1)} async-done(((bf16[1024,6656]{1,0:T(8,128)(2,1)}), bf16[256,6656]{1,0:T(8,128)(2,1)}) %reduce-scatter.3.cloned.1.call-update) | async-done | bytes 3407888 | tf_op jit(solution)/shard_map/reduce_scatter | solution.py:34
  718.9 6.5 fusion
  (37 shorter events, 3.4 us)
Async XLA Ops:
  8.0 96.4 %copy-start = (bf16[256,6656]{1,0:T(8,128)(2,1)S(1)}, bf16[256,6656]{1,0:T(8,128)(2,1)}, u32[]{:S(2)}) copy-start(bf16[256,6656]{1,0:T(8,128)(2,1)} %param.11) | copy-start | bytes 10223620
  8.0 63.4 %all-gather.2.cloned.1.call-start = ((), (), s32[]{:S(2)}) async-start(), calls=%async_computation.3 | async-start | bytes 10485760 | tf_op jit(solution)/shard_map/all_gather | solution.py:25
  94.7 5.8 copy-start.6
  94.7 191.4 %all-to-all-start = ((bf16[1,256,4,4096]{3,1,0,2:T(8,128)(2,1)}), bf16[1,256,4,4096]{3,1,0,2:T(8,128)(2,1)}, u32[]{:S(2)}, u32[]{:S(2)}) async-start(bf16[1,256,4,4096]{3,1,0,2:T(8,128)(2,1)} %copy.48), calls=%async_computation | async-start | bytes 16777216 | tf_op jit(solution)/shard_map/all_to_all | solution.py:26
  100.5 335.8 %all-reduce.3.cloned.1.call-start = ((), (), s32[]{:S(2)}) async-start(), calls=%async_computation.5 | async-start | bytes 524288 | tf_op jit(solution)/shard_map/psum | solution.py:58
  112.2 375.0 %reduce-scatter.5.cloned.1.call-start = ((), (), s32[]{:S(2)}) async-start(), calls=%async_computation.6 | async-start | bytes 8519680 | tf_op jit(solution)/shard_map/reduce_scatter | solution.py:95
  286.1 3.2 copy-start.5
  288.0 1.3 copy-start.2
  354.2 1.5 copy-start.7
  370.3 348.6 %reduce-scatter.3.cloned.1.call-start = ((), (), s32[]{:S(2)}) async-start(), calls=%async_computation.4 | async-start | bytes 17039360 | tf_op jit(solution)/shard_map/reduce_scatter | solution.py:34
  436.0 1.7 copy-start.3
  438.1 3.8 copy-start.4
  718.9 6.6 copy-start.1
Sparse Core Ops, SparseCore 0:
  10.4 60.9 all-gather.1
  370.4 116.7 reduce-scatter.4
  489.6 229.2 reduce-scatter.2
Sparse Core Ops, SparseCore 1:
  112.3 235.5 all-reduce.2
where the time goes:
time: 734 us; the launch traced here: 733 us
  waiting for transfers between devices  501 us (68%)
  matrix products  89.2 us (12%)
  blocking collectives  60.6 us (8%)
  local copies, waits for them, and re-layouts  47.1 us (6%)
  between operations  15.3 us (2%)
  other arithmetic  13.7 us (2%)
    reduce_scatter x1, waiting for transfers between devices, local(): lax.psum_scatter(jnp.dot(all_rows, up_weight, preferred_element_type=jnp....  228 us
    all_to_all x1, waiting for transfers between devices, local(): lax.all_to_all(gathered.reshape(1, batch_rows, dp_count, column_part), 'd...  168 us
    dot_general x1, matrix products, local(): jnp.dot(all_rows, up_weight, preferred_element_type=jnp.float32)  65.4 us
    all_gather x1, waiting for transfers between devices, local(): gathered = lax.all_gather(tokens, 'tensor', axis=0, tiled=True)  62.7 us
    psum x1, blocking collectives, local(): lax.psum((proj_part.reshape(-1, 2 * rank_width), back_full.reshape(-1, 2...  60.6 us
    reduce_scatter x1, waiting for transfers between devices, local(): lax.psum_scatter(buffer.astype(jnp.bfloat16), 'dp', scatter_dimension=0,...  40.6 us
  transfers between devices with their start and end apart: 5, of which 4 were waited for; matrix products, arithmetic and copies ran while one was open for 16% of the time, Pallas kernels for 0%

commit v1 on v0

--- a/solution.py
+++ b/solution.py
@@ -1,16 +1,456 @@
+import functools
+
 import jax
 import jax.numpy as jnp
 from jax import lax
+from jax.experimental import pallas as pl
+from jax.experimental.pallas import tpu as pltpu
 from jax.sharding import PartitionSpec as P
 
 ROWS_BLK = 128
 OWN_MAX = 2
-
-
 SCALE = 0.5
+SPLIT = ((0, 2), (2, 5), (5, 9), (9, 13))
+WINDOW = 3
+VMEM = 40 * 1024 * 1024
+ANY = pl.BlockSpec(memory_space=pl.ANY)
+SMEM = pl.BlockSpec(memory_space=pltpu.SMEM)
+
+
+def after(value, *earlier):
+    return lax.optimization_barrier((value, *earlier))[0]
+
+
+def across(value, axis, bit):
+    count = lax.axis_size(axis)
+    return lax.ppermute(value, axis, [(i, i ^ bit) for i in range(count)])
+
+
+def outward(value, hop):
+    last = lax.axis_size("dp") - 1
+    return lax.ppermute(value, "dp", [(hop, hop + 1), (last - hop, last - hop - 1)])
+
+
+def bits_of(count):
+    return [1 << k for k in reversed(range(count.bit_length() - 1))]
+
+
+def gather_rows(rows):
+    held = [(0, rows)]
+    for bit in bits_of(lax.axis_size("tensor")):
+        held = held + [(mask | bit, across(value, "tensor", bit)) for mask, value in held]
+    return held
+
+
+def sum_over_tensor(value):
+    for bit in bits_of(lax.axis_size("tensor")):
+        value = value + across(value, "tensor", bit)
+    return value
+
+
+def tile_of(width):
+    return 512 if width % 512 == 0 else 128
+
+
+def cut(width):
+    tiles = width // tile_of(width)
+    counts = [tiles * (i + 1) // 13 - tiles * i // 13 for i in range(13)]
+    counts = [sum(counts[a:b]) for a, b in SPLIT]
+    edges = [0]
+    for n in counts:
+        edges.append(edges[-1] + n)
+    return list(zip(edges[:-1], counts))
+
+
+def call(kernel, flops, **kwargs):
+    return pl.pallas_call(
+        kernel,
+        compiler_params=pltpu.CompilerParams(vmem_limit_bytes=VMEM),
+        cost_estimate=pl.CostEstimate(flops=flops, bytes_accessed=0, transcendentals=0),
+        **kwargs,
+    )
+
+
+def share_kernel(masks, has_add, deps, index, *refs):
+    blocks, refs = refs[: len(masks)], refs[len(masks) :]
+    weight, refs = refs[0], refs[1:]
+    if has_add:
+        arrived, refs = refs[0], refs[1:]
+    refs = refs[deps:]
+    rows = blocks[0].shape[0]
+    batch = refs[-1]
+
+    @pl.when(pl.program_id(0) == 0)
+    def _():
+        for mask, block in zip(masks, blocks):
+            first = pl.multiple_of((index[0] ^ mask) * rows, rows)
+            batch[pl.ds(first, rows), :] = block[...]
+
+    value = jnp.dot(batch[...], weight[...], preferred_element_type=jnp.float32)
+    refs[0][...] = value.astype(jnp.bfloat16)
+    if has_add:
+        refs[1][...] = (value + arrived[...].astype(jnp.float32)).astype(jnp.bfloat16)
+
+
+def share(index, gathered, weight, piece, arrived=None, deps=()):
+    masks, blocks = zip(*gathered)
+    rows, depth = blocks[0].shape
+    batch_rows = rows * len(blocks)
+    tile = tile_of(weight.shape[1])
+    first, count = piece
+    out = jax.ShapeDtypeStruct((batch_rows, count * tile), jnp.bfloat16)
+    column = pl.BlockSpec((batch_rows, tile), lambda i, s: (0, i))
+    has_add = arrived is not None
+    result = call(
+        functools.partial(share_kernel, masks, has_add, len(deps)),
+        2 * batch_rows * depth * count * tile,
+        out_shape=[out] * (1 + has_add),
+        grid_spec=pltpu.PrefetchScalarGridSpec(
+            num_scalar_prefetch=1,
+            grid=(count,),
+            in_specs=[pl.BlockSpec((rows, depth), lambda i, s: (0, 0))] * len(blocks)
+            + [pl.BlockSpec((depth, tile), lambda i, s: (0, first + i))]
+            + [column] * has_add
+            + [ANY] * len(deps),
+            out_specs=[column] * (1 + has_add),
+            scratch_shapes=[pltpu.VMEM((batch_rows, depth), jnp.bfloat16)],
+        ),
+    )(index, *blocks, weight, *([arrived] if has_add else []), *deps)
+    return result if has_add else result[0]
+
+
+def forward_kernel(masks, batches, index, ids, *refs):
+    blocks, refs = refs[: batches * len(masks)], refs[batches * len(masks) :]
+    down, features, parts = refs[0], refs[1], refs[2:]
+    rows = blocks[0].shape[0]
+    batch_rows = rows * len(masks)
+    local_blocks = batch_rows // ROWS_BLK
+    for d in range(batches):
+        for k, mask in enumerate(masks):
+            first = pl.multiple_of(d * batch_rows + (index[0] ^ mask) * rows, rows)
+            features[pl.ds(first, rows), :] = blocks[d * len(masks) + k][...]
+        for b in range(local_blocks):
+            first = d * batch_rows + b * ROWS_BLK
+            parts[d][b * ROWS_BLK : (b + 1) * ROWS_BLK, :] = lax.dot_general(
+                features[first : first + ROWS_BLK, :],
+                down[ids[d * local_blocks + b]],
+                (((1,), (1,)), ((), ())),
+                preferred_element_type=jnp.float32,
+            )
+
+
+def forward(index, ids, gathered, adapter_down):
+    batches = len(gathered)
+    masks = [mask for mask, _ in gathered[0]]
+    rows = gathered[0][0][1].shape[0]
+    batch_rows = rows * len(masks)
+    rank_width, slice_cols = adapter_down.shape[1:]
+    return call(
+        functools.partial(forward_kernel, masks, batches),
+        2 * batches * batch_rows * slice_cols * rank_width * 4,
+        out_shape=[jax.ShapeDtypeStruct((batches * batch_rows, slice_cols), jnp.bfloat16)]
+        + [jax.ShapeDtypeStruct((batch_rows, rank_width), jnp.float32)] * batches,
+        grid_spec=pltpu.PrefetchScalarGridSpec(
+            num_scalar_prefetch=2,
+            grid=(1,),
+            in_specs=[pl.BlockSpec((rows, slice_cols), lambda i, s, n: (0, s[0]))] * (batches * len(masks))
+            + [pl.BlockSpec(adapter_down.shape, lambda i, s, n: (0, 0, 0))],
+            out_specs=[pl.BlockSpec((batches * batch_rows, slice_cols), lambda i, s, n: (0, 0))]
+            + [pl.BlockSpec((batch_rows, rank_width), lambda i, s, n: (0, 0))] * batches,
+        ),
+    )(index, ids, *[value for d in range(batches) for _, value in gathered[d]], adapter_down)
+
+
+def backward_kernel(ids, grad, up, out):
+    @pl.when(pl.program_id(0) == 0)
+    def _():
+        out[...] = jnp.zeros_like(out)
+
+    for b in range(grad.shape[0] // ROWS_BLK):
+        rows = slice(b * ROWS_BLK, (b + 1) * ROWS_BLK)
+        out[rows, :] += lax.dot_general(
+            grad[rows, :], up[ids[b]], (((1,), (1,)), ((), ())), preferred_element_type=jnp.float32
+        )
+
+
+def backward(ids, grad_out, adapter_up):
+    batch_rows, hidden = grad_out.shape
+    tenants, rank_width, _ = adapter_up.shape
+    tile = tile_of(hidden)
+    return call(
+        backward_kernel,
+        2 * batch_rows * hidden * rank_width * 4,
+        out_shape=jax.ShapeDtypeStruct((batch_rows, rank_width), jnp.float32),
+        grid_spec=pltpu.PrefetchScalarGridSpec(
+            num_scalar_prefetch=1,
+            grid=(hidden // tile,),
+            in_specs=[
+                pl.BlockSpec((batch_rows, tile), lambda i, n: (0, i)),
+                pl.BlockSpec((tenants, rank_width, tile), lambda i, n: (0, 0, i)),
+            ],
+            out_specs=pl.BlockSpec((batch_rows, rank_width), lambda i, n: (0, 0)),
+        ),
+    )(ids, grad_out, adapter_up)
+
+
+def down_kernel(batches, ids, inverse, features, *refs):
+    backs, out = refs[:batches], refs[batches]
+    batch_rows = backs[0].shape[0]
+    local_blocks = batch_rows // ROWS_BLK
+    out[...] = jnp.zeros_like(out)
+    for d in range(batches):
+        for b in range(local_blocks):
+            first = d * batch_rows + b * ROWS_BLK
+            tenant = ids[d * local_blocks + b]
+            out[tenant] += lax.dot_general(
+                backs[d][b * ROWS_BLK : (b + 1) * ROWS_BLK, :],
+                features[first : first + ROWS_BLK, :],
+                (((0,), (0,)), ((), ())),
+                preferred_element_type=jnp.float32,
+            )
+    for n in range(out.shape[0]):
+        out[n] *= inverse[n]
+
+
+def down_gradient(ids, inverse, features, backs, shape):
+    whole = pl.BlockSpec(memory_space=pltpu.VMEM)
+    return call(
+        functools.partial(down_kernel, len(backs)),
+        2 * features.size * backs[0].shape[1] * 4,
+        out_shape=jax.ShapeDtypeStruct(shape, jnp.float32),
+        in_specs=[SMEM, SMEM] + [whole] * (1 + len(backs)),
+        out_specs=whole,
+    )(ids, inverse, features, *backs)
+
+
+def combine_kernel(count, extras, weights, scale, *refs):
+    terms, more, out = refs[:count], refs[count : count + extras], refs[count + extras]
+    parts = [term[0].astype(jnp.float32) for term in terms]
+    for s in range(out.shape[0]):
+        total = sum(part * weights[s, n] for n, part in enumerate(parts))
+        if extras:
+            total += sum(extra[s].astype(jnp.float32) for extra in more) * scale[s]
+        out[s] = total.astype(out.dtype)
+
+
+def combine(weights, terms, dtype, scale=None, extras=()):
+    rank_width, hidden = terms[0].shape[1:]
+    tile = tile_of(hidden)
+    slots = weights.shape[0]
+    if scale is None:
+        scale = jnp.ones((slots,), jnp.float32)
+    return call(
+        functools.partial(combine_kernel, len(terms), len(extras)),
+        4 * slots * rank_width * hidden * len(terms),
+        out_shape=jax.ShapeDtypeStruct((slots, rank_width, hidden), dtype),
+        grid=(hidden // tile,),
+        in_specs=[SMEM, SMEM]
+        + [pl.BlockSpec((1, rank_width, tile), lambda i: (0, 0, i))] * len(terms)
+        + [pl.BlockSpec((slots, rank_width, tile), lambda i: (0, 0, i))] * len(extras),
+        out_specs=pl.BlockSpec((slots, rank_width, tile), lambda i: (0, 0, i)),
+    )(weights, scale, *terms, *extras)
 
 
 def local(tokens, up_weight, adapter_down, adapter_up, grad_out, block_tenant, owner_of):
+    dp_count = 4
+    z = lax.axis_index("dp")
+    t = lax.axis_index("tensor")
+    outer = jnp.logical_or(z == 0, z == 3)
+    feature_count = tokens.shape[1]
+    batch_rows, hidden = grad_out.shape
+    local_blocks = batch_rows // ROWS_BLK
+    depth = feature_count // dp_count
+    tenants, rank_width, slice_cols = adapter_down.shape
+    flat_up = adapter_up.reshape(tenants * rank_width, hidden)
+    pieces = cut(hidden)
+    tile = tile_of(hidden)
+    index = t.reshape(1)
+
+    def block_for(where):
+        return lax.dynamic_slice_in_dim(tokens, where * depth, depth, 1)
+
+    far = lax.ppermute(block_for(z ^ 3), "dp", [(0, 3), (3, 0)])
+    middle = lax.ppermute(block_for(z ^ 3), "dp", [(1, 2), (2, 1)])
+    two = across(block_for(z ^ 2), "dp", 2)
+    one = across(block_for(z ^ 1), "dp", 1)
+    mine = block_for(z)
+    rows_first = gather_rows(jnp.where(outer, far, mine))
+
+    chain = []
+    work = []
+
+    def piece_of(rows, j, arrived=None):
+        out = share(index, rows, up_weight, pieces[j], arrived=arrived, deps=slot_gate[0] + tuple(work[-1:]))
+        out = out if arrived is not None else [out]
+        work.append(out[0])
+        return out
+
+    slot_gate = [()]
+
+    def slot(value):
+        if len(chain) >= WINDOW:
+            slot_gate[0] = (chain[len(chain) - WINDOW],)
+        chain.append(outward(after(value, *slot_gate[0], *work), 0))
+        work.clear()
+        work.append(value)
+        return chain[-1]
+
+    count = len(pieces)
+    first, twos, ones, lates = {}, {}, {}, {}
+    hop0, hop1, hop2 = {}, {}, {}
+
+    def add_two(j):
+        twos[j], total = piece_of(rows_two, j, arrived=hop0[0, j])
+        hop1[1, j] = outward(total, 1)
+
+    def add_one(j):
+        ones[j], total = piece_of(rows_one, j, arrived=hop1[1, j])
+        hop2[2, j] = outward(total, 2)
+
+    def add_late(j):
+        lates[j], total = piece_of(rows_late, j, arrived=hop0[1, j])
+        hop1[2, j] = outward(total, 1)
+
+    (first[0],) = piece_of(rows_first, 0)
+    hop0[0, 0] = slot(first[0])
+    rows_two = gather_rows(after(two, first[0]))
+    (first[1],) = piece_of(rows_first, 1)
+    hop0[0, 1] = slot(first[1])
+    rows_one = gather_rows(after(one, first[1]))
+    (first[2],) = piece_of(rows_first, 2)
+
+    hop0[0, 2] = slot(first[2])
+    rows_late = gather_rows(after(jnp.where(outer, mine, middle), first[2]))
+    (first[3],) = piece_of(rows_first, 3)
+
+    hop0[0, 3] = slot(first[3])
+    add_two(0)
+    add_two(1)
+
+    block_tenant, owner_of = lax.optimization_barrier((block_tenant, owner_of, work[-1]))[:2]
+    tenant_ids = jnp.arange(tenants, dtype=jnp.int32)
+    order = jnp.stack(
+        [jnp.where(outer, z ^ 3, z), z ^ 2, z ^ 1, jnp.where(outer, z, z ^ 3)]
+    )
+    blocks_of = block_tenant.reshape(dp_count, local_blocks)
+    ids = jnp.take(blocks_of, order, axis=0).reshape(-1)
+    own_ids = lax.dynamic_index_in_dim(blocks_of, z, 0, keepdims=False)
+    onehot = (block_tenant[None, :] == tenant_ids[:, None]).astype(jnp.float32)
+    inverse = 1.0 / jnp.sum(onehot, axis=1)
+    gathered = [rows_first, rows_two, rows_one, rows_late]
+    features, *parts = forward(index, ids, gathered, adapter_down)
+    part_own = jnp.where(outer, parts[3], parts[0])
+    part_far = jnp.where(outer, parts[0], parts[3])
+    sums = [across(part_far, "dp", 3), across(parts[1], "dp", 2), across(parts[2], "dp", 1)]
+    work.append(features)
+
+    hop0[1, 0] = slot(twos[0])
+    add_two(2)
+    back_part = backward(after(own_ids, work[-1]), grad_out, adapter_up)
+    work.append(back_part)
+
+    hop0[1, 1] = slot(twos[1])
+    add_two(3)
+    sums = lax.optimization_barrier((*sums, work[-1]))[:3]
+    projected = part_own + sums[0] + sums[1] + sums[2]
+    projected = sum_over_tensor(projected).astype(jnp.bfloat16)
+    back_mine = (SCALE * sum_over_tensor(after(back_part, work[-1]))).astype(jnp.bfloat16)
+
+    up_terms = []
+    for b in range(local_blocks):
+        rows = slice(b * ROWS_BLK, (b + 1) * ROWS_BLK)
+        term = SCALE * lax.dot_general(
+            projected[rows], grad_out[rows], (((0,), (0,)), ((), ())), preferred_element_type=jnp.float32
+        )
+        up_terms.append(term.astype(jnp.bfloat16))
+    work.append(back_mine)
+
+    moved_terms = [slot(up_terms[0])]
+    add_late(0)
+    add_one(0)
+
+    moved_terms.append(slot(up_terms[1]))
+    add_late(1)
+    add_one(1)
+    owner_of = after(owner_of, work[-1])
+    same_owner = owner_of[:, None] == owner_of[None, :]
+    earlier = tenant_ids[None, :] < tenant_ids[:, None]
+    slot_of = owner_of * OWN_MAX + jnp.sum(jnp.logical_and(same_owner, earlier), axis=1)
+    own_slots = z * OWN_MAX + jnp.arange(OWN_MAX, dtype=jnp.int32)
+    ownership = (slot_of[None, :] == own_slots[:, None]).astype(jnp.float32)
+    own_scale = jnp.sum(ownership * inverse[None, :], axis=1)
+    block_slot = jnp.sum(
+        jnp.where(block_tenant[:, None] == tenant_ids[None, :], slot_of[None, :], 0), axis=1
+    ).reshape(dp_count, local_blocks)
+
+    def hits(slots, batch):
+        theirs = lax.dynamic_index_in_dim(block_slot, jnp.clip(batch, 0, 3), 0, keepdims=False)
+        return (slots[:, None] == theirs[None, :]).astype(jnp.float32)
+
+    def slots_at(where):
+        return where * OWN_MAX + jnp.arange(OWN_MAX, dtype=jnp.int32)
+
+    side = jnp.where(z == 1, 1, -1)
+    here = jnp.concatenate([hits(slots_at(z + 2 * side), z), hits(slots_at(z + side), z)], axis=0)
+    there = jnp.concatenate([hits(slots_at(z + 2 * side), z - side), hits(slots_at(z + side), z - side)], axis=0)
+    middle_hits = jnp.concatenate([here, there], axis=1)
+    side2 = jnp.where(z == 2, 1, -1)
+    last_hits = hits(slots_at(z + side2), z)
+    final_hits = jnp.concatenate([hits(own_slots, z), hits(own_slots, z - side)], axis=1) * own_scale[:, None]
+
+    hop0[1, 2] = slot(twos[2])
+    add_one(2)
+
+    hop0[1, 3] = slot(twos[3])
+    own_terms = [term[None] for term in up_terms]
+    outer_terms = [term[None] for term in moved_terms]
+    totals = combine(middle_hits, own_terms + outer_terms, jnp.bfloat16)
+    far_terms = outward(totals[:OWN_MAX], 1)
+    near_terms = outward(totals[OWN_MAX:], 1)
+    work.append(totals)
+    add_one(3)
+
+    hop0[2, 0] = slot(ones[0])
+    add_late(2)
+
+    hop0[2, 1] = slot(ones[1])
+    add_late(3)
+    backs = [across(after(back_mine, work[-1]), "dp", d) for d in (3, 2, 1)]
+
+    hop0[2, 2] = slot(ones[2])
+    own_mask = jnp.broadcast_to(
+        (after(own_ids, work[-1])[:, None] == tenant_ids[None, :])[:, None, :, None],
+        (local_blocks, ROWS_BLK, tenants, rank_width),
+    )
+    wide = jnp.where(
+        own_mask, projected.reshape(local_blocks, ROWS_BLK, 1, rank_width), jnp.zeros((), jnp.bfloat16)
+    ).reshape(batch_rows, tenants * rank_width)
+    bases = []
+    for j, (start, tiles) in enumerate(pieces):
+        total = SCALE * jnp.dot(
+            wide, flat_up[:, start * tile : (start + tiles) * tile], preferred_element_type=jnp.float32
+        )
+        bases.append(total + jnp.where(outer, lates[j], first[j]).astype(jnp.float32))
+        work.append(bases[-1])
+
+    hop0[2, 3] = slot(ones[3])
+    far_terms = after(far_terms, work[-1])
+    last_terms = outward(combine(last_hits, own_terms, jnp.bfloat16, jnp.ones((OWN_MAX,), jnp.float32), [far_terms]), 2)
+    backs = [
+        jnp.where(outer, backs[0], back_mine), backs[1], backs[2], jnp.where(outer, back_mine, backs[0])
+    ]
+    grad_down = down_gradient(ids, inverse, features, backs, adapter_down.shape)
+    grad_up = combine(final_hits, own_terms + outer_terms, jnp.float32, own_scale, [near_terms, last_terms])
+
+    layer_out = jnp.zeros((batch_rows, hidden), jnp.bfloat16)
+    for j, (start, tiles) in enumerate(pieces):
+        total = bases[j] + hop2[2, j].astype(jnp.float32) + hop1[2, j].astype(jnp.float32)
+        total = total + hop0[2, j].astype(jnp.float32)
+        layer_out = lax.dynamic_update_slice(layer_out, total.astype(jnp.bfloat16), (0, start * tile))
+    return (layer_out, grad_down, grad_up)
+
+
+def local_plain(tokens, up_weight, adapter_down, adapter_up, grad_out, block_tenant, owner_of):
     dp_count = lax.axis_size("dp")
     dp_index = lax.axis_index("dp")
     tp_index = lax.axis_index("tensor")
@@ -110,7 +550,7 @@
         P("groups"),
     )
     return jax.shard_map(
-        local,
+        local if mesh.shape["dp"] == 4 else local_plain,
         mesh=mesh,
         in_specs=placed,
         out_specs=(

time: 734 us -> 445 us (0.61)
  waiting for transfers between devices: 501 us -> 105 us
  Pallas kernels: 0 us -> 156 us
  starting transfers between devices: 6.1 us -> 134 us
  matrix products: 89.2 us -> 6.07 us
  blocking collectives: 60.6 us -> 0 us
  local copies, waits for them, and re-layouts: 47.1 us -> 23.6 us
  between operations: 15.3 us -> 1.76 us
    reduce_scatter x2 -> x0, waiting for transfers between devices: 269 us -> none  [the longest x1 228 us: local(): lax.psum_scatter(jnp.dot(all_rows, up_weight, preferred_element_type=jnp....]
    all_to_all x1 -> x0, waiting for transfers between devices: 168 us -> none  [local(): lax.all_to_all(gathered.reshape(1, batch_rows, dp_count, column_part), 'd...]
    pallas_call x0 -> x22, Pallas kernels: none -> 156 us  [the longest x16 128 us: share(): call(functools.partial(share_kernel, masks, has_add, len(deps)), 2 * batc...]
    ppermute x0 -> x55, starting transfers between devices: none -> 134 us  [the longest x29 89.4 us: outward(): lax.ppermute(value, 'dp', [(hop, hop + 1), (last - hop, last - hop - 1)])]
    ppermute x0 -> x55, waiting for transfers between devices: none -> 105 us  [the longest x29 55.8 us: outward(): lax.ppermute(value, 'dp', [(hop, hop + 1), (last - hop, last - hop - 1)])]
    dot_general x9 -> x6, matrix products: 89.2 us -> 6.07 us  [the longest x4 5.24 us: local(): jnp.dot(wide, flat_up[:, start * tile:(start + tiles) * tile], preferred_...]
    all_gather x1 -> x0, waiting for transfers between devices: 62.7 us -> none  [local(): gathered = lax.all_gather(tokens, 'tensor', axis=0, tiled=True)]
    psum x1 -> x0, blocking collectives: 60.6 us -> none  [local(): lax.psum((proj_part.reshape(-1, 2 * rank_width), back_full.reshape(-1, 2...]
  transfers between devices with their start and end apart: 5 -> 55, of which waited for: 4 -> 12; matrix products, arithmetic and copies ran while one was open for 16% -> 6% of each run, Pallas kernels for 0% -> 33%
where the time goes in v1:
time: 445 us; the launch traced here: 442 us
  Pallas kernels  156 us (35%)
  starting transfers between devices  134 us (30%)
  waiting for transfers between devices  105 us (24%)
  local copies, waits for them, and re-layouts  23.6 us (5%)
  other arithmetic  15.7 us (4%)
  matrix products  6.07 us (1%)
    pallas_call x16, Pallas kernels, share(): call(functools.partial(share_kernel, masks, has_add, len(deps)), 2 * batc...  128 us
    ppermute x29, starting transfers between devices, outward(): lax.ppermute(value, 'dp', [(hop, hop + 1), (last - hop, last - hop - 1)])  89.4 us
    ppermute x29, waiting for transfers between devices, outward(): lax.ppermute(value, 'dp', [(hop, hop + 1), (last - hop, last - hop - 1)])  55.8 us
    ppermute x24, waiting for transfers between devices, across(): return lax.ppermute(value, axis, [(i, i ^ bit) for i in range(count)])  37.4 us
    ppermute x24, starting transfers between devices, across(): return lax.ppermute(value, axis, [(i, i ^ bit) for i in range(count)])  37 us
    pallas_call x3, Pallas kernels, combine(): call(functools.partial(combine_kernel, len(terms), len(extras)), 4 * slot...  18.5 us
    unnamed x148, local copies, waits for them, and re-layouts  17 us
    ppermute x1, waiting for transfers between devices, local(): far = lax.ppermute(block_for(z ^ 3), 'dp', [(0, 3), (3, 0)])  12 us
  transfers between devices with their start and end apart: 55, of which 12 were waited for; matrix products, arithmetic and copies ran while one was open for 6% of the time, Pallas kernels for 33%

profile of v1, /device:TPU:0, one launch (start us, length us, event | category | flops | bytes accessed | tf_op | source)
XLA Modules:
  0.0 442.0 jit_solution(16518985099636032639)
XLA Ops:
  2.4 7.0 %collective-permute-start.1 = (bf16[64,4096]{1,0:T(8,128)(2,1)S(1)}, bf16[64,4096]{1,0:T(8,128)(2,1)S(1)}, u32[]{:S(2)}, u32[]{:S(2)}) collective-permute-start(bf16[64,4096]{1,0:T(8,128)(2,1)S(1)} %constant_dynamic-slice_fusion.4), channel_id=1, source_target_pairs={{0,12},{12,0},{1,13},{13,1},{2,14},{14,2},{3,15},{15,3},{16,28},{2... | collective-permute-start | bytes 1572872 | tf_op jit(solution)/shard_map/ppermute | solution.py:272
  9.4 12.0 %collective-permute-done.1 = bf16[64,4096]{1,0:T(8,128)(2,1)S(1)} collective-permute-done((bf16[64,4096]{1,0:T(8,128)(2,1)S(1)}, bf16[64,4096]{1,0:T(8,128)(2,1)S(1)}, u32[]{:S(2)}, u32[]{:S(2)}) %collective-permute-start.1) | collective-permute-done | bytes 524320 | tf_op jit(solution)/shard_map/ppermute | solution.py:272
  25.6 11.6 %collective-permute-done.2.refs_1_ = bf16[64,4096]{1,0:T(8,128)(2,1)S(1)} collective-permute-done((bf16[64,4096]{1,0:T(8,128)(2,1)S(1)}, bf16[64,4096]{1,0:T(8,128)(2,1)S(1)}, u32[]{:S(2)}, u32[]{:S(2)}) %collective-permute-start.2) | collective-permute-done | bytes 524320 | tf_op jit(solution)/shard_map/ppermute | solution.py:26
  37.7 10.9 %collective-permute-start = (bf16[64,4096]{1,0:T(8,128)(2,1)}, bf16[64,4096]{1,0:T(8,128)(2,1)S(1)}, u32[]{:S(2)}, u32[]{:S(2)}) collective-permute-start(bf16[64,4096]{1,0:T(8,128)(2,1)} %get-tuple-element.120), channel_id=1, source_target_pairs={{0,8},{4,12},{8,0},{12,4},{1,9},{5,13},{9,1},{13,5},{2,10},{6,14},... | collective-permute-start | bytes 1572872 | tf_op jit(solution)/shard_map/ppermute | solution.py:26
  49.9 5.2 %shard_map.94.refs_5_ = bf16[256,1024]{1,0:T(8,128)(2,1)S(1)} custom-call(s32[1]{0:T(128)} %bitcast.index, bf16[64,4096]{1,0:T(8,128)(2,1)S(1)} %get-tuple-element.122.refs_0_, bf16[64,4096]{1,0:T(8,128)(2,1)S(1)} %collective-permute-done.2.refs_1_, bf16[64,4096]{1,0:T(8,128)(2,1)S(1)} %collective-permute-done.3.refs_2_, ...), custom_call_target="tpu_custom_call" | custom-call | flops 2147483648 | tf_op jit(solution)/shard_map/pallas_call | solution.py:104
  55.1 17.6 %collective-permute-done.refs_0_.refs_4_ = bf16[64,4096]{1,0:T(8,128)(2,1)S(1)} collective-permute-done((bf16[64,4096]{1,0:T(8,128)(2,1)}, bf16[64,4096]{1,0:T(8,128)(2,1)S(1)}, u32[]{:S(2)}, u32[]{:S(2)}) %collective-permute-start) | collective-permute-done | bytes 524320 | tf_op jit(solution)/shard_map/ppermute | solution.py:26
  75.7 7.2 %shard_map.95.refs_5_ = bf16[256,1536]{1,0:T(8,128)(2,1)S(1)} custom-call(s32[1]{0:T(128)} %bitcast.index, bf16[64,4096]{1,0:T(8,128)(2,1)S(1)} %get-tuple-element.122.refs_0_, bf16[64,4096]{1,0:T(8,128)(2,1)S(1)} %collective-permute-done.2.refs_1_, bf16[64,4096]{1,0:T(8,128)(2,1)S(1)} %collective-permute-done.3.refs_2_, ...), custom_call_target="tpu_custom_call" | custom-call | flops 3221225472 | tf_op jit(solution)/shard_map/pallas_call | solution.py:104
  86.4 9.6 %shard_map.96.refs_5_ = bf16[256,2048]{1,0:T(8,128)(2,1)} custom-call(s32[1]{0:T(128)} %bitcast.index, bf16[64,4096]{1,0:T(8,128)(2,1)S(1)} %get-tuple-element.122.refs_0_, bf16[64,4096]{1,0:T(8,128)(2,1)S(1)} %collective-permute-done.2.refs_1_, bf16[64,4096]{1,0:T(8,128)(2,1)S(1)} %collective-permute-done.3.refs_2_, ...), custom_call_target="tpu_custom_call" | custom-call | flops 4294967296 | tf_op jit(solution)/shard_map/pallas_call | solution.py:104
  99.2 8.7 %shard_map.97.refs_7_ = bf16[256,2048]{1,0:T(8,128)(2,1)S(1)} custom-call(s32[1]{0:T(128)} %bitcast.index, bf16[64,4096]{1,0:T(8,128)(2,1)S(1)} %get-tuple-element.122.refs_0_, bf16[64,4096]{1,0:T(8,128)(2,1)S(1)} %collective-permute-done.2.refs_1_, bf16[64,4096]{1,0:T(8,128)(2,1)S(1)} %collective-permute-done.3.refs_2_, bf16[64,4096]{1,0:T(8,128)(2,1)S(1)} %copy-done.12, ...), custom_call_target="tpu_custom_call" | custom-call | flops 4294967296 | tf_op jit(solution)/shard_map/pallas_call | solution.py:104
  110.2 5.6 %shard_map.98 = (bf16[256,1024]{1,0:T(8,128)(2,1)}, bf16[256,1024]{1,0:T(8,128)(2,1)S(1)}) custom-call(s32[1]{0:T(128)} %bitcast.index, bf16[64,4096]{1,0:T(8,128)(2,1)S(1)} %collective-permute-done.refs_0_.refs_4_, bf16[64,4096]{1,0:T(8,128)(2,1)S(1)} %collective-permute-done.5.refs_1_.refs_5_, bf16[64,4096]{1,0:T(8,128)(2,1)S(1)} %collective-permute-done.6.refs_2_.refs_6_, ...), custom_call_target="tpu_custom_call" | custom-call | flops 2147483648 | tf_op jit(solution)/shard_map/pallas_call | solution.py:104
  122.2 8.3 %shard_map.99 = (bf16[256,1536]{1,0:T(8,128)(2,1)}, bf16[256,1536]{1,0:T(8,128)(2,1)}) custom-call(s32[1]{0:T(128)} %bitcast.index, bf16[64,4096]{1,0:T(8,128)(2,1)S(1)} %collective-permute-done.refs_0_.refs_4_, bf16[64,4096]{1,0:T(8,128)(2,1)S(1)} %collective-permute-done.5.refs_1_.refs_5_, bf16[64,4096]{1,0:T(8,128)(2,1)S(1)} %collective-permute-done.6.refs_2_.refs_6_, ...), custom_call_target="tpu_custom_call" | custom-call | flops 3221225472 | tf_op jit(solution)/shard_map/pallas_call | solution.py:104
  151.1 9.7 %shard_map.100 = (bf16[256,2048]{1,0:T(8,128)(2,1)S(1)}, bf16[256,2048]{1,0:T(8,128)(2,1)}) custom-call(s32[1]{0:T(128)} %bitcast.index, bf16[64,4096]{1,0:T(8,128)(2,1)S(1)} %copy-done.16, bf16[64,4096]{1,0:T(8,128)(2,1)S(1)} %copy-done.19, bf16[64,4096]{1,0:T(8,128)(2,1)S(1)} %copy-done.22, bf16[64,4096]{1,0:T(8,128)(2,1)S(1)} %copy-done.25, ...), custom_call_target="tpu_custom_call" | custom-call | flops 4294967296 | tf_op jit(solution)/shard_map/pallas_call | solution.py:104
  162.0 9.6 %shard_map.104 = (bf16[256,2048]{1,0:T(8,128)(2,1)S(1)}, bf16[256,2048]{1,0:T(8,128)(2,1)S(1)}) custom-call(s32[1]{0:T(128)} %bitcast.index, bf16[64,4096]{1,0:T(8,128)(2,1)S(1)} %copy-done.16, bf16[64,4096]{1,0:T(8,128)(2,1)S(1)} %copy-done.19, bf16[64,4096]{1,0:T(8,128)(2,1)S(1)} %copy-done.22, bf16[64,4096]{1,0:T(8,128)(2,1)S(1)} %copy-done.25, ...), custom_call_target="tpu_custom_call" | custom-call | flops 4294967296 | tf_op jit(solution)/shard_map/pallas_call | solution.py:104
  194.2 5.7 %shard_map.105 = (bf16[256,1024]{1,0:T(8,128)(2,1)S(1)}, bf16[256,1024]{1,0:T(8,128)(2,1)}) custom-call(s32[1]{0:T(128)} %bitcast.index, bf16[64,4096]{1,0:T(8,128)(2,1)S(1)} %get-tuple-element.74.refs_12_.refs_0_, bf16[64,4096]{1,0:T(8,128)(2,1)S(1)} %collective-permute-done.18.refs_13_.refs_1_, ...), custom_call_target="tpu_custom_call" | custom-call | flops 2147483648 | tf_op jit(solution)/shard_map/pallas_call | solution.py:104
  199.9 6.3 %collective-permute-start.35 = (bf16[64,6656]{1,0:T(8,128)(2,1)S(1)}, bf16[64,6656]{1,0:T(8,128)(2,1)}, u32[]{:S(2)}, u32[]{:S(2)}) collective-permute-start(bf16[64,6656]{1,0:T(8,128)(2,1)S(1)} %fusion.refs_7_), channel_id=1, source_target_pairs={{0,4},{12,8},{1,5},{13,9},{2,6},{14,10},{3,7},{15,11},{16,20},{28,... | collective-permute-start | bytes 2555912 | tf_op jit(solution)/shard_map/ppermute | solution.py:31
  206.3 6.3 %shard_map.106 = (bf16[256,1024]{1,0:T(8,128)(2,1)S(1)}, bf16[256,1024]{1,0:T(8,128)(2,1)}) custom-call(s32[1]{0:T(128)} %bitcast.index, bf16[64,4096]{1,0:T(8,128)(2,1)S(1)} %collective-permute-done.10.refs_0_.refs_8_, bf16[64,4096]{1,0:T(8,128)(2,1)} %collective-permute-done.11.refs_1_.refs_9_, bf16[64,4096]{1,0:T(8,128)(2,1)} %collective-permute-done.12.refs_2_.refs_10_, ...), custom_call_target="tpu_custom_call" | custom-call | flops 2147483648 | tf_op jit(solution)/shard_map/pallas_call | solution.py:104
  215.3 7.7 %shard_map.107 = (bf16[256,1536]{1,0:T(8,128)(2,1)S(1)}, bf16[256,1536]{1,0:T(8,128)(2,1)S(1)}) custom-call(s32[1]{0:T(128)} %bitcast.index, bf16[64,4096]{1,0:T(8,128)(2,1)S(1)} %get-tuple-element.74.refs_12_.refs_0_, bf16[64,4096]{1,0:T(8,128)(2,1)S(1)} %collective-permute-done.18.refs_13_.refs_1_, bf16[64,4096]{1,0:T(8,128)(2,1)S(1)} %copy-done.5, ...), custom_call_target="tpu_custom_call" | custom-call | flops 3221225472 | tf_op jit(solution)/shard_map/pallas_call | solution.py:104
  223.8 6.3 %collective-permute-start.31 = (bf16[64,6656]{1,0:T(8,128)(2,1)S(1)}, bf16[64,6656]{1,0:T(8,128)(2,1)}, u32[]{:S(2)}, u32[]{:S(2)}) collective-permute-start(bf16[64,6656]{1,0:T(8,128)(2,1)S(1)} %fusion.1.refs_7_), channel_id=1, source_target_pairs={{0,4},{12,8},{1,5},{13,9},{2,6},{14,10},{3,7},{15,11},{16,20},{28,... | collective-permute-start | bytes 2555912 | tf_op jit(solution)/shard_map/ppermute | solution.py:31
  230.1 7.9 %shard_map.108 = (bf16[256,1536]{1,0:T(8,128)(2,1)S(1)}, bf16[256,1536]{1,0:T(8,128)(2,1)S(1)}) custom-call(s32[1]{0:T(128)} %bitcast.index, bf16[64,4096]{1,0:T(8,128)(2,1)S(1)} %collective-permute-done.10.refs_0_.refs_8_, bf16[64,4096]{1,0:T(8,128)(2,1)} %collective-permute-done.11.refs_1_.refs_9_, ...), custom_call_target="tpu_custom_call" | custom-call | flops 3221225472 | tf_op jit(solution)/shard_map/pallas_call | solution.py:104
  243.5 9.3 %shard_map.102 = (bf16[256,2048]{1,0:T(8,128)(2,1)S(1)}, bf16[256,2048]{1,0:T(8,128)(2,1)S(1)}) custom-call(s32[1]{0:T(128)} %bitcast.index, bf16[64,4096]{1,0:T(8,128)(2,1)S(1)} %collective-permute-done.10.refs_0_.refs_8_, bf16[64,4096]{1,0:T(8,128)(2,1)} %collective-permute-done.11.refs_1_.refs_9_, ...), custom_call_target="tpu_custom_call" | custom-call | flops 4294967296 | tf_op jit(solution)/shard_map/pallas_call | solution.py:104
  256.0 7.6 %shard_map.109.refs_7_ = bf16[4,64,6656]{2,1,0:T(8,128)(2,1)S(1)} custom-call(f32[4,4]{1,0:T(4,128)S(1)} %add_convert_fusion.5.weights, f32[4]{0:T(128)S(1)} %broadcast_19_scale.2.scale, bf16[1,64,6656]{2,1,0:T(8,128)(2,1)S(1)} %bitcast.36, bf16[1,64,6656]{2,1,0:T(8,128)(2,1)S(1)} %bitcast.39, bf16[1,64,6656]{2,1,0:T(8,128)(2,1)} %bitcast.17.refs_2_, ...), custom_call_target="tpu_custom_call" | custom-call | flops 27262976 | tf_op jit(solution)/shard_map/pallas_call | solution.py:242
  269.3 9.4 %shard_map.110 = (bf16[256,2048]{1,0:T(8,128)(2,1)S(1)}, bf16[256,2048]{1,0:T(8,128)(2,1)S(1)}) custom-call(s32[1]{0:T(128)} %bitcast.index, bf16[64,4096]{1,0:T(8,128)(2,1)S(1)} %collective-permute-done.10.refs_0_.refs_8_, bf16[64,4096]{1,0:T(8,128)(2,1)} %collective-permute-done.11.refs_1_.refs_9_, ...), custom_call_target="tpu_custom_call" | custom-call | flops 4294967296 | tf_op jit(solution)/shard_map/pallas_call | solution.py:104
  280.2 10.7 %collective-permute-done.44.refs_5_ = bf16[256,2048]{1,0:T(8,128)(2,1)S(1)} collective-permute-done((bf16[256,2048]{1,0:T(8,128)(2,1)S(1)}, bf16[256,2048]{1,0:T(8,128)(2,1)S(1)}, u32[]{:S(2)}, u32[]{:S(2)}) %collective-permute-start.44) | collective-permute-done | bytes 1048608 | tf_op jit(solution)/shard_map/ppermute | solution.py:31
  295.4 9.0 %shard_map.112 = (bf16[256,2048]{1,0:T(8,128)(2,1)S(1)}, bf16[256,2048]{1,0:T(8,128)(2,1)S(1)}) custom-call(s32[1]{0:T(128)} %bitcast.index, bf16[64,4096]{1,0:T(8,128)(2,1)S(1)} %get-tuple-element.74.refs_12_.refs_0_, bf16[64,4096]{1,0:T(8,128)(2,1)S(1)} %collective-permute-done.18.refs_13_.refs_1_, bf16[64,4096]{1,0:T(8,128)(2,1)S(1)} %copy-done.6, ...), custom_call_target="tpu_custom_call" | custom-call | flops 4294967296 | tf_op jit(solution)/shard_map/pallas_call | solution.py:104
  304.5 11.7 %collective-permute-start.50 = (bf16[256,64]{1,0:T(8,128)(2,1)S(1)}, bf16[256,64]{1,0:T(8,128)(2,1)S(1)}, u32[]{:S(2)}, u32[]{:S(2)}) collective-permute-start(bf16[256,64]{1,0:T(8,128)(2,1)S(1)} %copy-done.66), channel_id=1, source_target_pairs={{0,8},{4,12},{8,0},{12,4},{1,9},{5,13},{9,1},{13,5},{2,10},{6,14},... | collective-permute-start | bytes 98312 | tf_op jit(solution)/shard_map/ppermute | solution.py:26
  316.2 8.8 %shard_map.111 = (bf16[256,2048]{1,0:T(8,128)(2,1)S(1)}, bf16[256,2048]{1,0:T(8,128)(2,1)S(1)}) custom-call(s32[1]{0:T(128)} %bitcast.index, bf16[64,4096]{1,0:T(8,128)(2,1)S(1)} %get-tuple-element.74.refs_12_.refs_0_, bf16[64,4096]{1,0:T(8,128)(2,1)S(1)} %collective-permute-done.18.refs_13_.refs_1_, bf16[64,4096]{1,0:T(8,128)(2,1)S(1)} %copy-done.6, ...), custom_call_target="tpu_custom_call" | custom-call | flops 4294967296 | tf_op jit(solution)/shard_map/pallas_call | solution.py:104
  329.4 7.6 %collective-permute-start.45 = (bf16[256,2048]{1,0:T(8,128)(2,1)S(1)}, bf16[256,2048]{1,0:T(8,128)(2,1)}, u32[]{:S(2)}, u32[]{:S(2)}) collective-permute-start(bf16[256,2048]{1,0:T(8,128)(2,1)S(1)} %get-tuple-element.111), channel_id=1, source_target_pairs={{0,4},{12,8},{1,5},{13,9},{2,6},{14,10},{3,7},{15,11},{16,20},{28,... | collective-permute-start | bytes 3145736 | tf_op jit(solution)/shard_map/ppermute | solution.py:31
  339.7 21.5 %collective-permute-start.41 = (bf16[256,1536]{1,0:T(8,128)(2,1)S(1)}, bf16[256,1536]{1,0:T(8,128)(2,1)}, u32[]{:S(2)}, u32[]{:S(2)}) collective-permute-start(bf16[256,1536]{1,0:T(8,128)(2,1)S(1)} %copy-done.45), channel_id=1, source_target_pairs={{0,4},{12,8},{1,5},{13,9},{2,6},{14,10},{3,7},{15,11},{16,20},{28,... | collective-permute-start | bytes 2359304 | tf_op jit(solution)/shard_map/ppermute | solution.py:31
  374.5 8.2 %collective-permute-start.48 = (bf16[256,2048]{1,0:T(8,128)(2,1)S(1)}, bf16[256,2048]{1,0:T(8,128)(2,1)S(1)}, u32[]{:S(2)}, u32[]{:S(2)}) collective-permute-start(bf16[256,2048]{1,0:T(8,128)(2,1)S(1)} %get-tuple-element.114), channel_id=1, source_target_pairs={{0,4},{12,8},{1,5},{13,9},{2,6},{14,10},{3,7},{15,11},{16,20},{28,... | collective-permute-start | bytes 3145736 | tf_op jit(solution)/shard_map/ppermute | solution.py:31
  390.3 11.6 %collective-permute-done.46 = bf16[256,2048]{1,0:T(8,128)(2,1)S(1)} collective-permute-done((bf16[256,2048]{1,0:T(8,128)(2,1)S(1)}, bf16[256,2048]{1,0:T(8,128)(2,1)S(1)}, u32[]{:S(2)}, u32[]{:S(2)}) %collective-permute-start.46) | collective-permute-done | bytes 1048608 | tf_op jit(solution)/shard_map/ppermute | solution.py:31
  403.6 29.7 %collective-permute-done.54.refs_5_ = bf16[2,64,6656]{2,1,0:T(8,128)(2,1)S(1)} collective-permute-done((bf16[2,64,6656]{2,1,0:T(8,128)(2,1)S(1)}, bf16[2,64,6656]{2,1,0:T(8,128)(2,1)S(1)}, u32[]{:S(2)}, u32[]{:S(2)}) %collective-permute-start.54) | collective-permute-done | bytes 1703968 | tf_op jit(solution)/shard_map/ppermute | solution.py:31
  433.3 8.7 %shard_map.115 = f32[2,64,6656]{2,1,0:T(8,128)} custom-call(f32[2,4]{1,0:T(2,128)S(1)} %add_select_fusion.weights, f32[2]{0:T(128)S(1)} %fusion.30.scale, bf16[1,64,6656]{2,1,0:T(8,128)(2,1)S(1)} %bitcast.38, bf16[1,64,6656]{2,1,0:T(8,128)(2,1)S(1)} %bitcast.41, bf16[1,64,6656]{2,1,0:T(8,128)(2,1)} %bitcast.17.refs_2_, ...), custom_call_target="tpu_custom_call" | custom-call | flops 13631488 | tf_op jit(solution)/shard_map/pallas_call | solution.py:242
  (296 shorter events, 123.0 us)
Async XLA Ops:
  37.7 35.0 %collective-permute-start = (bf16[64,4096]{1,0:T(8,128)(2,1)}, bf16[64,4096]{1,0:T(8,128)(2,1)S(1)}, u32[]{:S(2)}, u32[]{:S(2)}) collective-permute-start(bf16[64,4096]{1,0:T(8,128)(2,1)} %get-tuple-element.120), channel_id=1, source_target_pairs={{0,8},{4,12},{8,0},{12,4},{1,9},{5,13},{9,1},{13,5},{2,10},{6,14},... | collective-permute-start | bytes 1572872 | tf_op jit(solution)/shard_map/ppermute | solution.py:26
  49.8 33.2 %collective-permute-start.10 = (bf16[64,4096]{1,0:T(8,128)(2,1)}, bf16[64,4096]{1,0:T(8,128)(2,1)S(1)}, u32[]{:S(2)}, u32[]{:S(2)}) collective-permute-start(bf16[64,4096]{1,0:T(8,128)(2,1)} %get-tuple-element.121), channel_id=1, source_target_pairs={{0,4},{4,0},{8,12},{12,8},{1,5},{5,1},{9,13},{13,9},{2,6},{6,2},{1... | collective-permute-start | bytes 1572872 | tf_op jit(solution)/shard_map/ppermute | solution.py:26
  83.0 48.1 %collective-permute-start.12 = (bf16[64,4096]{1,0:T(8,128)(2,1)S(1)}, bf16[64,4096]{1,0:T(8,128)(2,1)}, u32[]{:S(2)}, u32[]{:S(2)}) collective-permute-start(bf16[64,4096]{1,0:T(8,128)(2,1)S(1)} %collective-permute-done.10.refs_0_.refs_8_), channel_id=1, source_target_pairs={{0,1},{1,0},{2,3},{3,2},{4,5},{5,4},{6,7},{7,6},{8,9},{9,8},{10,11... | collective-permute-start | bytes 1572872 | tf_op jit(solution)/shard_map/ppermute | solution.py:26
  83.6 38.1 %collective-permute-start.8 = (bf16[256,1536]{1,0:T(8,128)(2,1)S(1)}, bf16[256,1536]{1,0:T(8,128)(2,1)S(1)}, u32[]{:S(2)}, u32[]{:S(2)}) collective-permute-start(bf16[256,1536]{1,0:T(8,128)(2,1)S(1)} %shard_map.95.refs_5_), channel_id=1, source_target_pairs={{0,4},{12,8},{1,5},{13,9},{2,6},{14,10},{3,7},{15,11},{16,20},{28,... | collective-permute-start | bytes 2359304 | tf_op jit(solution)/shard_map/ppermute | solution.py:31
  107.9 40.4 %collective-permute-start.14 = (bf16[256,2048]{1,0:T(8,128)(2,1)}, bf16[256,2048]{1,0:T(8,128)(2,1)}, u32[]{:S(2)}, u32[]{:S(2)}) collective-permute-start(bf16[256,2048]{1,0:T(8,128)(2,1)} %shard_map.96.refs_5_), channel_id=1, source_target_pairs={{0,4},{12,8},{1,5},{13,9},{2,6},{14,10},{3,7},{15,11},{16,20},{28,... | collective-permute-start | bytes 3145736 | tf_op jit(solution)/shard_map/ppermute | solution.py:31
  131.2 30.9 %collective-permute-start.24 = (bf16[256,2048]{1,0:T(8,128)(2,1)}, bf16[256,2048]{1,0:T(8,128)(2,1)}, u32[]{:S(2)}, u32[]{:S(2)}) collective-permute-start(bf16[256,2048]{1,0:T(8,128)(2,1)} %copy-done.26), channel_id=1, source_target_pairs={{0,4},{12,8},{1,5},{13,9},{2,6},{14,10},{3,7},{15,11},{16,20},{28,... | collective-permute-start | bytes 3145736 | tf_op jit(solution)/shard_map/ppermute | solution.py:31
  133.6 66.3 %collective-permute-start.28 = (bf16[256,1024]{1,0:T(8,128)(2,1)}, bf16[256,1024]{1,0:T(8,128)(2,1)}, u32[]{:S(2)}, u32[]{:S(2)}) collective-permute-start(bf16[256,1024]{1,0:T(8,128)(2,1)} %copy-done.57), channel_id=1, source_target_pairs={{4,8},{8,4},{5,9},{9,5},{6,10},{10,6},{7,11},{11,7},{20,24},{24,20... | collective-permute-start | bytes 1572872 | tf_op jit(solution)/shard_map/ppermute | solution.py:31
  146.5 25.2 %collective-permute-start.21 = (f32[256,64]{1,0:T(8,128)S(1)}, f32[256,64]{1,0:T(8,128)S(1)}, u32[]{:S(2)}, u32[]{:S(2)}) collective-permute-start(f32[256,64]{1,0:T(8,128)S(1)} %broadcast_select_fusion.5), channel_id=1, source_target_pairs={{0,12},{4,8},{8,4},{12,0},{1,13},{5,9},{9,5},{13,1},{2,14},{6,10},... | collective-permute-start | bytes 196616 | tf_op jit(solution)/shard_map/ppermute | solution.py:26
  180.0 43.8 %collective-permute-start.32 = (bf16[256,1536]{1,0:T(8,128)(2,1)}, bf16[256,1536]{1,0:T(8,128)(2,1)}, u32[]{:S(2)}, u32[]{:S(2)}) collective-permute-start(bf16[256,1536]{1,0:T(8,128)(2,1)} %get-tuple-element.93), channel_id=1, source_target_pairs={{4,8},{8,4},{5,9},{9,5},{6,10},{10,6},{7,11},{11,7},{20,24},{24,20... | collective-permute-start | bytes 2359304 | tf_op jit(solution)/shard_map/ppermute | solution.py:31
  182.4 31.4 %collective-permute-start.16 = (bf16[256,1536]{1,0:T(8,128)(2,1)}, bf16[256,1536]{1,0:T(8,128)(2,1)}, u32[]{:S(2)}, u32[]{:S(2)}) collective-permute-start(bf16[256,1536]{1,0:T(8,128)(2,1)} %get-tuple-element.71.refs_7_), channel_id=1, source_target_pairs={{0,4},{12,8},{1,5},{13,9},{2,6},{14,10},{3,7},{15,11},{16,20},{28,... | collective-permute-start | bytes 2359304 | tf_op jit(solution)/shard_map/ppermute | solution.py:31
  186.7 54.0 %collective-permute-start.15 = (bf16[256,2048]{1,0:T(8,128)(2,1)}, bf16[256,2048]{1,0:T(8,128)(2,1)}, u32[]{:S(2)}, u32[]{:S(2)}) collective-permute-start(bf16[256,2048]{1,0:T(8,128)(2,1)} %get-tuple-element.68), channel_id=1, source_target_pairs={{4,8},{8,4},{5,9},{9,5},{6,10},{10,6},{7,11},{11,7},{20,24},{24,20... | collective-permute-start | bytes 3145736 | tf_op jit(solution)/shard_map/ppermute | solution.py:31
  192.6 75.1 %collective-permute-start.36 = (bf16[256,2048]{1,0:T(8,128)(2,1)}, bf16[256,2048]{1,0:T(8,128)(2,1)}, u32[]{:S(2)}, u32[]{:S(2)}) collective-permute-start(bf16[256,2048]{1,0:T(8,128)(2,1)} %copy-done.53), channel_id=1, source_target_pairs={{4,8},{8,4},{5,9},{9,5},{6,10},{10,6},{7,11},{11,7},{20,24},{24,20... | collective-permute-start | bytes 3145736 | tf_op jit(solution)/shard_map/ppermute | solution.py:31
  199.9 54.7 %collective-permute-start.35 = (bf16[64,6656]{1,0:T(8,128)(2,1)S(1)}, bf16[64,6656]{1,0:T(8,128)(2,1)}, u32[]{:S(2)}, u32[]{:S(2)}) collective-permute-start(bf16[64,6656]{1,0:T(8,128)(2,1)S(1)} %fusion.refs_7_), channel_id=1, source_target_pairs={{0,4},{12,8},{1,5},{13,9},{2,6},{14,10},{3,7},{15,11},{16,20},{28,... | collective-permute-start | bytes 2555912 | tf_op jit(solution)/shard_map/ppermute | solution.py:31
  213.8 90.6 %collective-permute-start.29 = (bf16[256,1024]{1,0:T(8,128)(2,1)}, bf16[256,1024]{1,0:T(8,128)(2,1)}, u32[]{:S(2)}, u32[]{:S(2)}) collective-permute-start(bf16[256,1024]{1,0:T(8,128)(2,1)} %get-tuple-element.88), channel_id=1, source_target_pairs={{8,12},{4,0},{9,13},{5,1},{10,14},{6,2},{11,15},{7,3},{24,28},{20,... | collective-permute-start | bytes 1572872 | tf_op jit(solution)/shard_map/ppermute | solution.py:31
  223.8 32.2 %collective-permute-start.31 = (bf16[64,6656]{1,0:T(8,128)(2,1)S(1)}, bf16[64,6656]{1,0:T(8,128)(2,1)}, u32[]{:S(2)}, u32[]{:S(2)}) collective-permute-start(bf16[64,6656]{1,0:T(8,128)(2,1)S(1)} %fusion.1.refs_7_), channel_id=1, source_target_pairs={{0,4},{12,8},{1,5},{13,9},{2,6},{14,10},{3,7},{15,11},{16,20},{28,... | collective-permute-start | bytes 2555912 | tf_op jit(solution)/shard_map/ppermute | solution.py:31
  240.7 38.1 %collective-permute-start.40 = (bf16[256,2048]{1,0:T(8,128)(2,1)}, bf16[256,2048]{1,0:T(8,128)(2,1)S(1)}, u32[]{:S(2)}, u32[]{:S(2)}) collective-permute-start(bf16[256,2048]{1,0:T(8,128)(2,1)} %copy-done.42), channel_id=1, source_target_pairs={{0,4},{12,8},{1,5},{13,9},{2,6},{14,10},{3,7},{15,11},{16,20},{28,... | collective-permute-start | bytes 3145736 | tf_op jit(solution)/shard_map/ppermute | solution.py:31
  254.6 36.3 %collective-permute-start.44 = (bf16[256,2048]{1,0:T(8,128)(2,1)S(1)}, bf16[256,2048]{1,0:T(8,128)(2,1)S(1)}, u32[]{:S(2)}, u32[]{:S(2)}) collective-permute-start(bf16[256,2048]{1,0:T(8,128)(2,1)S(1)} %copy-done.52), channel_id=1, source_target_pairs={{0,4},{12,8},{1,5},{13,9},{2,6},{14,10},{3,7},{15,11},{16,20},{28,... | collective-permute-start | bytes 3145736 | tf_op jit(solution)/shard_map/ppermute | solution.py:31
  265.6 74.1 %collective-permute-start.53 = (bf16[2,64,6656]{2,1,0:T(8,128)(2,1)}, bf16[2,64,6656]{2,1,0:T(8,128)(2,1)S(1)}, u32[]{:S(2)}, u32[]{:S(2)}) collective-permute-start(bf16[2,64,6656]{2,1,0:T(8,128)(2,1)} %get-tuple-element.117), channel_id=1, source_target_pairs={{4,8},{8,4},{5,9},{9,5},{6,10},{10,6},{7,11},{11,7},{20,24},{24,20... | collective-permute-start | bytes 5111816 | tf_op jit(solution)/shard_map/ppermute | solution.py:31
  267.7 36.8 %collective-permute-start.30 = (bf16[256,1024]{1,0:T(8,128)(2,1)}, bf16[256,1024]{1,0:T(8,128)(2,1)}, u32[]{:S(2)}, u32[]{:S(2)}) collective-permute-start(bf16[256,1024]{1,0:T(8,128)(2,1)} %get-tuple-element.89), channel_id=1, source_target_pairs={{4,8},{8,4},{5,9},{9,5},{6,10},{10,6},{7,11},{11,7},{20,24},{24,20... | collective-permute-start | bytes 1572872 | tf_op jit(solution)/shard_map/ppermute | solution.py:31
  278.8 46.3 %collective-permute-start.38 = (bf16[256,1536]{1,0:T(8,128)(2,1)}, bf16[256,1536]{1,0:T(8,128)(2,1)S(1)}, u32[]{:S(2)}, u32[]{:S(2)}) collective-permute-start(bf16[256,1536]{1,0:T(8,128)(2,1)} %copy-done.56), channel_id=1, source_target_pairs={{8,12},{4,0},{9,13},{5,1},{10,14},{6,2},{11,15},{7,3},{24,28},{20,... | collective-permute-start | bytes 2359304 | tf_op jit(solution)/shard_map/ppermute | solution.py:31
  291.0 35.4 %collective-permute-start.37 = (bf16[256,1024]{1,0:T(8,128)(2,1)S(1)}, bf16[256,1024]{1,0:T(8,128)(2,1)S(1)}, u32[]{:S(2)}, u32[]{:S(2)}) collective-permute-start(bf16[256,1024]{1,0:T(8,128)(2,1)S(1)} %copy-done.47), channel_id=1, source_target_pairs={{0,4},{12,8},{1,5},{13,9},{2,6},{14,10},{3,7},{15,11},{16,20},{28,... | collective-permute-start | bytes 1572872 | tf_op jit(solution)/shard_map/ppermute | solution.py:31
  304.5 24.9 %collective-permute-start.50 = (bf16[256,64]{1,0:T(8,128)(2,1)S(1)}, bf16[256,64]{1,0:T(8,128)(2,1)S(1)}, u32[]{:S(2)}, u32[]{:S(2)}) collective-permute-start(bf16[256,64]{1,0:T(8,128)(2,1)S(1)} %copy-done.66), channel_id=1, source_target_pairs={{0,8},{4,12},{8,0},{12,4},{1,9},{5,13},{9,1},{13,5},{2,10},{6,14},... | collective-permute-start | bytes 98312 | tf_op jit(solution)/shard_map/ppermute | solution.py:26
  325.1 46.6 %collective-permute-start.42 = (bf16[256,2048]{1,0:T(8,128)(2,1)S(1)}, bf16[256,2048]{1,0:T(8,128)(2,1)}, u32[]{:S(2)}, u32[]{:S(2)}) collective-permute-start(bf16[256,2048]{1,0:T(8,128)(2,1)S(1)} %get-tuple-element.107), channel_id=1, source_target_pairs={{8,12},{4,0},{9,13},{5,1},{10,14},{6,2},{11,15},{7,3},{24,28},{20,... | collective-permute-start | bytes 3145736 | tf_op jit(solution)/shard_map/ppermute | solution.py:31
  326.4 48.1 %collective-permute-start.43 = (bf16[256,2048]{1,0:T(8,128)(2,1)S(1)}, bf16[256,2048]{1,0:T(8,128)(2,1)}, u32[]{:S(2)}, u32[]{:S(2)}) collective-permute-start(bf16[256,2048]{1,0:T(8,128)(2,1)S(1)} %get-tuple-element.108), channel_id=1, source_target_pairs={{4,8},{8,4},{5,9},{9,5},{6,10},{10,6},{7,11},{11,7},{20,24},{24,20... | collective-permute-start | bytes 3145736 | tf_op jit(solution)/shard_map/ppermute | solution.py:31
  329.4 53.3 %collective-permute-start.45 = (bf16[256,2048]{1,0:T(8,128)(2,1)S(1)}, bf16[256,2048]{1,0:T(8,128)(2,1)}, u32[]{:S(2)}, u32[]{:S(2)}) collective-permute-start(bf16[256,2048]{1,0:T(8,128)(2,1)S(1)} %get-tuple-element.111), channel_id=1, source_target_pairs={{0,4},{12,8},{1,5},{13,9},{2,6},{14,10},{3,7},{15,11},{16,20},{28,... | collective-permute-start | bytes 3145736 | tf_op jit(solution)/shard_map/ppermute | solution.py:31
  338.1 32.8 %collective-permute-start.39 = (bf16[256,1536]{1,0:T(8,128)(2,1)S(1)}, bf16[256,1536]{1,0:T(8,128)(2,1)}, u32[]{:S(2)}, u32[]{:S(2)}) collective-permute-start(bf16[256,1536]{1,0:T(8,128)(2,1)S(1)} %copy-done.55), channel_id=1, source_target_pairs={{4,8},{8,4},{5,9},{9,5},{6,10},{10,6},{7,11},{11,7},{20,24},{24,20... | collective-permute-start | bytes 2359304 | tf_op jit(solution)/shard_map/ppermute | solution.py:31
  339.7 34.1 %collective-permute-start.41 = (bf16[256,1536]{1,0:T(8,128)(2,1)S(1)}, bf16[256,1536]{1,0:T(8,128)(2,1)}, u32[]{:S(2)}, u32[]{:S(2)}) collective-permute-start(bf16[256,1536]{1,0:T(8,128)(2,1)S(1)} %copy-done.45), channel_id=1, source_target_pairs={{0,4},{12,8},{1,5},{13,9},{2,6},{14,10},{3,7},{15,11},{16,20},{28,... | collective-permute-start | bytes 2359304 | tf_op jit(solution)/shard_map/ppermute | solution.py:31
  370.9 32.6 %collective-permute-start.52 = (bf16[2,64,6656]{2,1,0:T(8,128)(2,1)S(1)}, bf16[2,64,6656]{2,1,0:T(8,128)(2,1)S(1)}, u32[]{:S(2)}, u32[]{:S(2)}) collective-permute-start(bf16[2,64,6656]{2,1,0:T(8,128)(2,1)S(1)} %copy-done.61), channel_id=1, source_target_pairs={{4,8},{8,4},{5,9},{9,5},{6,10},{10,6},{7,11},{11,7},{20,24},{24,20... | collective-permute-start | bytes 5111816 | tf_op jit(solution)/shard_map/ppermute | solution.py:31
  371.7 30.2 %collective-permute-start.46 = (bf16[256,2048]{1,0:T(8,128)(2,1)S(1)}, bf16[256,2048]{1,0:T(8,128)(2,1)S(1)}, u32[]{:S(2)}, u32[]{:S(2)}) collective-permute-start(bf16[256,2048]{1,0:T(8,128)(2,1)S(1)} %get-tuple-element.112), channel_id=1, source_target_pairs={{8,12},{4,0},{9,13},{5,1},{10,14},{6,2},{11,15},{7,3},{24,28},{20,... | collective-permute-start | bytes 3145736 | tf_op jit(solution)/shard_map/ppermute | solution.py:31
  373.8 28.2 %collective-permute-start.47 = (bf16[256,2048]{1,0:T(8,128)(2,1)S(1)}, bf16[256,2048]{1,0:T(8,128)(2,1)S(1)}, u32[]{:S(2)}, u32[]{:S(2)}) collective-permute-start(bf16[256,2048]{1,0:T(8,128)(2,1)S(1)} %get-tuple-element.113), channel_id=1, source_target_pairs={{4,8},{8,4},{5,9},{9,5},{6,10},{10,6},{7,11},{11,7},{20,24},{24,20... | collective-permute-start | bytes 3145736 | tf_op jit(solution)/shard_map/ppermute | solution.py:31
  374.5 27.5 %collective-permute-start.48 = (bf16[256,2048]{1,0:T(8,128)(2,1)S(1)}, bf16[256,2048]{1,0:T(8,128)(2,1)S(1)}, u32[]{:S(2)}, u32[]{:S(2)}) collective-permute-start(bf16[256,2048]{1,0:T(8,128)(2,1)S(1)} %get-tuple-element.114), channel_id=1, source_target_pairs={{0,4},{12,8},{1,5},{13,9},{2,6},{14,10},{3,7},{15,11},{16,20},{28,... | collective-permute-start | bytes 3145736 | tf_op jit(solution)/shard_map/ppermute | solution.py:31
  382.7 50.6 %collective-permute-start.54 = (bf16[2,64,6656]{2,1,0:T(8,128)(2,1)S(1)}, bf16[2,64,6656]{2,1,0:T(8,128)(2,1)S(1)}, u32[]{:S(2)}, u32[]{:S(2)}) collective-permute-start(bf16[2,64,6656]{2,1,0:T(8,128)(2,1)S(1)} %shard_map.114), channel_id=1, source_target_pairs={{8,12},{4,0},{9,13},{5,1},{10,14},{6,2},{11,15},{7,3},{24,28},{20,... | collective-permute-start | bytes 5111816 | tf_op jit(solution)/shard_map/ppermute | solution.py:31
  (97 other events, 1260.3 us)

commit v2 on v1

v2 whole, which is shorter than its diff:
```python
import functools

import jax
import jax.numpy as jnp
from jax import lax
from jax.experimental import pallas as pl
from jax.experimental.pallas import tpu as pltpu
from jax.sharding import PartitionSpec as P

ROWS_BLK = 128
OWN_MAX = 2
SCALE = 0.5
SPLIT = ((0, 2), (2, 5), (5, 9), (9, 13))
WINDOW = 2
VMEM = 60 * 1024 * 1024
ANY = pl.BlockSpec(memory_space=pl.ANY)
SMEM = pl.BlockSpec(memory_space=pltpu.SMEM)


class Held:
    def __init__(self, now):
        self.now = now


def tie(*held):
    distinct = list({id(one): one for one in held}.values())
    for one, now in zip(distinct, lax.optimization_barrier(tuple(one.now for one in distinct))):
        one.now = now


def after(value, *earlier):
    return lax.optimization_barrier((value, *earlier))[0]


def across(value, axis, bit):
    count = lax.axis_size(axis)
    return lax.ppermute(value, axis, [(i, i ^ bit) for i in range(count)])


def outward(value, hop):
    last = lax.axis_size("dp") - 1
    return lax.ppermute(value, "dp", [(hop, hop + 1), (last - hop, last - hop - 1)])


def bits_of(count):
    return [1 << k for k in reversed(range(count.bit_length() - 1))]


def gather_rows(rows):
    held = [(0, rows)]
    for bit in bits_of(lax.axis_size("tensor")):
        held = held + [(mask | bit, across(value, "tensor", bit)) for mask, value in held]
    return held


def sum_over_tensor(value):
    for bit in bits_of(lax.axis_size("tensor")):
        value = value + across(value, "tensor", bit)
    return value


def tile_of(width):
    return 512 if width % 512 == 0 else 128


def cut(width):
    tiles = width // tile_of(width)
    counts = [tiles * (i + 1) // 13 - tiles * i // 13 for i in range(13)]
    counts = [sum(counts[a:b]) for a, b in SPLIT]
    edges = [0]
    for n in counts:
        edges.append(edges[-1] + n)
    return list(zip(edges[:-1], counts))


def call(kernel, flops, **kwargs):
    return pl.pallas_call(
        kernel,
        compiler_params=pltpu.CompilerParams(vmem_limit_bytes=VMEM),
        cost_estimate=pl.CostEstimate(flops=flops // 6, bytes_accessed=0, transcendentals=0),
        **kwargs,
    )


def share_kernel(masks, has_add, deps, index, *refs):
    blocks, refs = refs[: len(masks)], refs[len(masks) :]
    weight, refs = refs[0], refs[1:]
    if has_add:
        arrived, refs = refs[0], refs[1:]
    out = refs[deps]
    batch = blocks[0]
    if len(masks) > 1:
        batch = refs[deps + 1]
        rows = blocks[0].shape[0]

        @pl.when(pl.program_id(0) == 0)
        def _():
            for mask, block in zip(masks, blocks):
                first = pl.multiple_of((index[0] ^ mask) * rows, rows)
                batch[pl.ds(first, rows), :] = block[...]

    value = jnp.dot(batch[...], weight[...], preferred_element_type=jnp.float32)
    if has_add:
        value = value + arrived[...].astype(jnp.float32)
    out[...] = value.astype(jnp.bfloat16)


def share(index, gathered, weight, piece, arrived=None, deps=()):
    masks, blocks = zip(*gathered)
    rows, depth = blocks[0].shape
    batch_rows = rows * len(blocks)
    tile = tile_of(weight.shape[1])
    first, count = piece
    column = pl.BlockSpec((batch_rows, tile), lambda i, s: (0, i))
    has_add = arrived is not None
    return call(
        functools.partial(share_kernel, masks, has_add, len(deps)),
        2 * batch_rows * depth * count * tile,
        out_shape=jax.ShapeDtypeStruct((batch_rows, count * tile), jnp.bfloat16),
        grid_spec=pltpu.PrefetchScalarGridSpec(
            num_scalar_prefetch=1,
            grid=(count,),
            in_specs=[pl.BlockSpec((rows, depth), lambda i, s: (0, 0))] * len(blocks)
            + [pl.BlockSpec((depth, tile), lambda i, s: (0, first + i))]
            + [column] * has_add
            + [ANY] * len(deps),
            out_specs=column,
            scratch_shapes=[pltpu.VMEM((batch_rows, depth), jnp.bfloat16)] * (len(blocks) > 1),
        ),
    )(index, *blocks, weight, *([arrived] if has_add else []), *deps)


def forward_kernel(count, deps, ids, *refs):
    blocks, down, outs = refs[:count], refs[count], refs[count + 1 + deps :]
    slices, _, _, width = down.shape
    for d in range(count):
        outs[d][...] = sum(
            lax.dot_general(
                blocks[d][:, n * width : (n + 1) * width],
                down[n, ids[d]],
                (((1,), (1,)), ((), ())),
                preferred_element_type=jnp.float32,
            )
            for n in range(slices)
        )


def forward(ids, blocks, down, deps):
    rows = blocks[0].shape[0]
    rank_width = down.shape[2]
    whole = pl.BlockSpec(memory_space=pltpu.VMEM)
    return call(
        functools.partial(forward_kernel, len(blocks), len(deps)),
        2 * len(blocks) * blocks[0].size * rank_width * 4,
        out_shape=[jax.ShapeDtypeStruct((rows, rank_width), jnp.float32)] * len(blocks),
        in_specs=[SMEM] + [whole] * (len(blocks) + 1) + [ANY] * len(deps),
        out_specs=[whole] * len(blocks),
    )(ids, *blocks, down, *deps)


def backward_kernel(ids, grad, up, out):
    @pl.when(pl.program_id(0) == 0)
    def _():
        out[...] = jnp.zeros_like(out)

    for b in range(grad.shape[0] // ROWS_BLK):
        rows = slice(b * ROWS_BLK, (b + 1) * ROWS_BLK)
        out[rows, :] += lax.dot_general(
            grad[rows, :], up[ids[b]], (((1,), (1,)), ((), ())), preferred_element_type=jnp.float32
        )


def backward(ids, grad_out, adapter_up):
    batch_rows, hidden = grad_out.shape
    tenants, rank_width, _ = adapter_up.shape
    tile = tile_of(hidden)
    return call(
        backward_kernel,
        2 * batch_rows * hidden * rank_width * 4,
        out_shape=jax.ShapeDtypeStruct((batch_rows, rank_width), jnp.float32),
        grid_spec=pltpu.PrefetchScalarGridSpec(
            num_scalar_prefetch=1,
            grid=(hidden // tile,),
            in_specs=[
                pl.BlockSpec((batch_rows, tile), lambda i, n: (0, i)),
                pl.BlockSpec((tenants, rank_width, tile), lambda i, n: (0, 0, i)),
            ],
            out_specs=pl.BlockSpec((batch_rows, rank_width), lambda i, n: (0, 0)),
        ),
    )(ids, grad_out, adapter_up)


def down_kernel(masks, index, ids, inverse, *refs):
    out = refs[-1]
    out[...] = jnp.zeros_like(out)
    at = 0
    backs, refs = refs[: len(masks)], refs[len(masks) :]
    local_blocks = backs[0].shape[0] // ROWS_BLK
    for d, parts in enumerate(masks):
        for mask in parts:
            rows = refs[at].shape[0]
            first = 0 if len(parts) == 1 else pl.multiple_of((index[0] ^ mask) * rows, rows)
            step = min(rows, ROWS_BLK)
            for k in range(0, rows, step):
                tenant = ids[d * local_blocks + (first + k) // ROWS_BLK]
                out[tenant] += lax.dot_general(
                    backs[d][pl.ds(first + k, step), :],
                    refs[at][k : k + step, :],
                    (((0,), (0,)), ((), ())),
                    preferred_element_type=jnp.float32,
                )
            at += 1
    for n in range(out.shape[0]):
        out[n] *= inverse[n]


def down_gradient(index, ids, inverse, gathered, backs, shape):
    masks = [[mask for mask, _ in parts] for parts in gathered]
    arrays = [value for parts in gathered for _, value in parts]
    slice_cols = shape[2]
    return call(
        functools.partial(down_kernel, masks),
        8 * shape[1] * slice_cols * sum(value.shape[0] for value in arrays),
        out_shape=jax.ShapeDtypeStruct(shape, jnp.float32),
        grid_spec=pltpu.PrefetchScalarGridSpec(
            num_scalar_prefetch=2,
            grid=(1,),
            in_specs=[SMEM]
            + [pl.BlockSpec(back.shape, lambda i, s, n: (0, 0)) for back in backs]
            + [pl.BlockSpec((value.shape[0], slice_cols), lambda i, s, n: (0, s[0])) for value in arrays],
            out_specs=pl.BlockSpec(shape, lambda i, s, n: (0, 0, 0)),
        ),
    )(index, ids, inverse, *backs, *arrays)


def combine_kernel(count, extras, weights, scale, *refs):
    terms, more, out = refs[:count], refs[count : count + extras], refs[count + extras]
    parts = [term[0].astype(jnp.float32) for term in terms]
    for s in range(out.shape[0]):
        total = sum(part * weights[s, n] for n, part in enumerate(parts))
        if extras:
            total += sum(extra[s].astype(jnp.float32) for extra in more) * scale[s]
        out[s] = total.astype(out.dtype)


def combine(weights, terms, dtype, scale=None, extras=()):
    rank_width, hidden = terms[0].shape[1:]
    tile = tile_of(hidden)
    slots = weights.shape[0]
    if scale is None:
        scale = jnp.ones((slots,), jnp.float32)
    return call(
        functools.partial(combine_kernel, len(terms), len(extras)),
        4 * slots * rank_width * hidden * len(terms),
        out_shape=jax.ShapeDtypeStruct((slots, rank_width, hidden), dtype),
        grid=(hidden // tile,),
        in_specs=[SMEM, SMEM]
        + [pl.BlockSpec((1, rank_width, tile), lambda i: (0, 0, i))] * len(terms)
        + [pl.BlockSpec((slots, rank_width, tile), lambda i: (0, 0, i))] * len(extras),
        out_specs=pl.BlockSpec((slots, rank_width, tile), lambda i: (0, 0, i)),
    )(weights, scale, *terms, *extras)


def local(tokens, up_weight, adapter_down, adapter_up, grad_out, block_tenant, owner_of):
    dp_count = 4
    z = lax.axis_index("dp")
    t = lax.axis_index("tensor")
    outer = jnp.logical_or(z == 0, z == 3)
    part_rows, feature_count = tokens.shape
    batch_rows, hidden = grad_out.shape
    local_blocks = batch_rows // ROWS_BLK
    depth = feature_count // dp_count
    tenants, rank_width, slice_cols = adapter_down.shape
    flat_up = adapter_up.reshape(tenants * rank_width, hidden)
    pieces = cut(hidden)
    tile = tile_of(hidden)
    index = t.reshape(1)

    def block_for(where):
        return lax.dynamic_slice_in_dim(tokens, where * depth, depth, 1)

    def first_hop(value):
        return lax.ppermute(value, "dp", [(0, 1), (3, 2)])

    def middle_hop(value):
        return lax.ppermute(value, "dp", [(1, 2), (2, 1)])

    def last_hop(value):
        return lax.ppermute(value, "dp", [(1, 0), (2, 3)])

    def first_and_last_hop(value):
        return lax.ppermute(value, "dp", [(0, 1), (3, 2), (1, 0), (2, 3)])

    def gather(value):
        return [(0, lax.all_gather(value, "tensor", axis=0, tiled=True))]

    down_all = lax.all_gather(adapter_down, "tensor", axis=0)
    far = lax.ppermute(block_for(z ^ 3), "dp", [(0, 3), (3, 0)])
    two = across(block_for(z ^ 2), "dp", 2)
    one = across(block_for(z ^ 1), "dp", 1)
    far, two, one = lax.optimization_barrier((far, two, one))
    middle = middle_hop(after(block_for(z ^ 3), far))
    mine = block_for(z)
    first_part = jnp.where(outer, far, mine)
    rows_first = gather_rows(first_part)

    chain = []
    work, earlier_work, pinned = [], [], []
    slot_gate = []

    def slot(value, hop=first_hop):
        k = len(chain)
        slot_gate[:] = chain[max(k - WINDOW, 0) : max(k - WINDOW + 1, 0)]
        with jax.named_scope(f"send{k}"):
            tie(value, *slot_gate, *pinned, *earlier_work)
            chain.append(Held(hop(value.now)))
        earlier_work[:] = work[-1:]
        pinned.clear()
        return chain[-1]

    def pin(arrived):
        pinned.append(arrived)

    def do(value):
        work.append(Held(value))
        return work[-1]

    def late_use(value):
        held = Held(value)
        tie(held, *work[-1:])
        return held.now

    def piece_of(name, rows, j, arrived=None):
        arrived = arrived if arrived is None else arrived.now
        deps = [held.now for held in (*slot_gate, *work[-1:])]
        with jax.named_scope(f"{name}{j}"):
            return do(share(index, rows, up_weight, pieces[j], arrived=arrived, deps=deps))

    firsts, twos, ones, lates = {}, {}, {}, {}
    step0, step1, step2, mid1, mid2 = {}, {}, {}, {}, {}

    def add_two(j):
        twos[j] = piece_of("two", rows_two, j, step0[j])
        with jax.named_scope(f"mid_two{j}"):
            mid1[j] = Held(middle_hop(twos[j].now))

    def add_late(j):
        lates[j] = piece_of("late", rows_late, j, step1[j])
        with jax.named_scope(f"mid_late{j}"):
            mid2[j] = Held(middle_hop(lates[j].now))

    def add_one(j):
        ones[j] = piece_of("one", rows_one, j, mid1[j])

    firsts[0] = piece_of("first", rows_first, 0)
    with jax.named_scope("two_rows"):
        two = late_use(two)
        rows_two = gather(two)

    step0[0] = slot(firsts[0])
    firsts[1] = piece_of("first", rows_first, 1)
    with jax.named_scope("one_rows"):
        one = late_use(one)
        rows_one = gather(one)
    with jax.named_scope("late_rows"):
        late_part = jnp.where(outer, mine, late_use(middle))
        rows_late = gather(late_part)
    block_tenant = late_use(block_tenant)

    step0[1] = slot(firsts[1])
    firsts[2] = piece_of("first", rows_first, 2)

    tenant_ids = jnp.arange(tenants, dtype=jnp.int32)
    order = jnp.stack([jnp.where(outer, z ^ 3, z), z ^ 2, z ^ 1, jnp.where(outer, z, z ^ 3)])
    blocks_of = block_tenant.reshape(dp_count, local_blocks)
    ids = jnp.take(blocks_of, order, axis=0)
    row_ids = lax.dynamic_index_in_dim(ids, t * part_rows // ROWS_BLK, 1, keepdims=False)
    ids = ids.reshape(-1)
    own_ids = lax.dynamic_index_in_dim(blocks_of, z, 0, keepdims=False)
    with jax.named_scope("forward"):
        parts = jnp.stack(forward(row_ids, [first_part, two, one, late_part], down_all, (firsts[2].now,)))
        by_batch = jnp.where((order[None, :] == jnp.arange(dp_count)[:, None])[:, :, None, None], parts, 0.0)
        by_batch = do(jnp.sum(by_batch, axis=1)).now
        projected = lax.psum_scatter(by_batch, "dp", scatter_dimension=0, tiled=True)[0]

    step0[2] = slot(firsts[2])
    firsts[3] = piece_of("first", rows_first, 3)
    add_two(0)

    step0[3] = slot(firsts[3])
    with jax.named_scope("projected"):
        projected = late_use(projected).astype(jnp.bfloat16)
        projected = lax.all_gather(projected, "tensor", axis=0, tiled=True)
    add_two(1)
    projected = late_use(projected)
    up_terms = []
    for b in range(local_blocks):
        rows = slice(b * ROWS_BLK, (b + 1) * ROWS_BLK)
        term = SCALE * lax.dot_general(
            projected[rows], grad_out[rows], (((0,), (0,)), ((), ())), preferred_element_type=jnp.float32
        )
        up_terms.append(do(term.astype(jnp.bfloat16)))

    moved_terms = [slot(up_terms[0])]
    add_two(2)
    pin(mid1[0])

    moved_terms.append(slot(up_terms[1]))
    add_two(3)
    pin(mid1[1])
    owner_of = late_use(owner_of)
    onehot = (block_tenant[None, :] == tenant_ids[:, None]).astype(jnp.float32)
    inverse = 1.0 / jnp.sum(onehot, axis=1)
    same_owner = owner_of[:, None] == owner_of[None, :]
    earlier = tenant_ids[None, :] < tenant_ids[:, None]
    slot_of = owner_of * OWN_MAX + jnp.sum(jnp.logical_and(same_owner, earlier), axis=1)
    own_slots = z * OWN_MAX + jnp.arange(OWN_MAX, dtype=jnp.int32)
    ownership = (slot_of[None, :] == own_slots[:, None]).astype(jnp.float32)
    own_scale = jnp.sum(ownership * inverse[None, :], axis=1)
    block_slot = jnp.sum(
        jnp.where(block_tenant[:, None] == tenant_ids[None, :], slot_of[None, :], 0), axis=1
    ).reshape(dp_count, local_blocks)

    def hits(slots, batch):
        theirs = lax.dynamic_index_in_dim(block_slot, jnp.clip(batch, 0, 3), 0, keepdims=False)
        return (slots[:, None] == theirs[None, :]).astype(jnp.float32)

    def slots_at(where):
        return where * OWN_MAX + jnp.arange(OWN_MAX, dtype=jnp.int32)

    side = jnp.where(z == 1, 1, -1)
    far_hits = jnp.concatenate([hits(slots_at(z + 2 * side), z), hits(slots_at(z + 2 * side), z - side)], axis=1)
    near_hits = jnp.concatenate([hits(slots_at(z + side), z), hits(slots_at(z + side), z - side)], axis=1)
    last_hits = hits(slots_at(jnp.where(z == 2, 3, 0)), z)
    own_hits = jnp.concatenate([hits(own_slots, z), hits(own_slots, z - side)], axis=1) * own_scale[:, None]

    add_one(0)

    step1[0] = slot(twos[0])
    pin(mid1[2])
    add_one(1)
    back_part = do(backward(late_use(own_ids), grad_out, adapter_up))
    with jax.named_scope("back_mine"):
        back_mine = (SCALE * lax.psum(back_part.now, "tensor")).astype(jnp.bfloat16)

    step1[1] = slot(twos[1])

    def terms():
        return [held.now[None] for held in (*up_terms, *moved_terms)]

    with jax.named_scope("far_terms"):
        far_sums = do(combine(far_hits, terms(), jnp.bfloat16))
        far_terms = Held(middle_hop(far_sums.now))
    pin(mid1[3])
    with jax.named_scope("backs"):
        backs = lax.all_gather(late_use(back_mine), "dp", axis=0)

    step2[0] = slot(ones[0], first_and_last_hop)
    add_late(0)
    add_one(2)

    step2[1] = slot(ones[1], first_and_last_hop)
    add_late(1)
    pin(far_terms)
    with jax.named_scope("last_terms"):
        last_sums = do(
            combine(last_hits, terms()[:local_blocks], jnp.bfloat16, jnp.ones((OWN_MAX,), jnp.float32), [far_terms.now])
        )
        last_terms = Held(last_hop(last_sums.now))

    step1[2] = slot(twos[2])
    with jax.named_scope("near_terms"):
        near_sums = do(combine(near_hits, terms(), jnp.bfloat16))
        near_terms = Held(middle_hop(near_sums.now))
    pin(mid2[0])
    add_one(3)

    step1[3] = slot(twos[3])
    pin(mid2[1])
    backs = late_use(backs)
    backs = [lax.dynamic_index_in_dim(backs, order[n], 0, keepdims=False) for n in range(dp_count)]
    grad_down = do(
        down_gradient(
            index, ids, inverse, [rows_first, rows_two, rows_one, rows_late], backs, adapter_down.shape
        )
    )
    pin(last_terms)

    step2[2] = slot(ones[2], first_and_last_hop)
    add_late(2)
    pin(near_terms)

    step2[3] = slot(ones[3], first_and_last_hop)
    add_late(3)
    grad_up = combine(own_hits, terms(), jnp.float32, own_scale, [near_terms.now, last_terms.now])
    own_mask = jnp.broadcast_to(
        (late_use(own_ids)[:, None] == tenant_ids[None, :])[:, None, :, None],
        (local_blocks, ROWS_BLK, tenants, rank_width),
    )
    wide = jnp.where(
        own_mask, projected.reshape(local_blocks, ROWS_BLK, 1, rank_width), jnp.zeros((), jnp.bfloat16)
    ).reshape(batch_rows, tenants * rank_width)
    layer_out = jnp.zeros((batch_rows, hidden), jnp.bfloat16)
    for j, (start, tiles) in enumerate(pieces):
        total = SCALE * jnp.dot(
            wide, flat_up[:, start * tile : (start + tiles) * tile], preferred_element_type=jnp.float32
        )
        total = total + jnp.where(outer, lates[j].now, firsts[j].now).astype(jnp.float32)
        total = total + mid2[j].now.astype(jnp.float32)
        total = total + step2[j].now.astype(jnp.float32)
        layer_out = lax.dynamic_update_slice(layer_out, total.astype(jnp.bfloat16), (0, start * tile))
    return (layer_out, grad_down.now, grad_up)


def local_plain(tokens, up_weight, adapter_down, adapter_up, grad_out, block_tenant, owner_of):
    dp_count = lax.axis_size("dp")
    dp_index = lax.axis_index("dp")
    tp_index = lax.axis_index("tensor")
    seq_rows, feature_count = tokens.shape
    batch_rows = grad_out.shape[0]
    local_blocks = batch_rows // ROWS_BLK
    all_blocks = local_blocks * dp_count
    column_part = feature_count // dp_count
    slice_cols = adapter_down.shape[2]
    rank_width = adapter_down.shape[1]
    tenants = adapter_down.shape[0]
    gathered = lax.all_gather(tokens, "tensor", axis=0, tiled=True)
    spread = lax.all_to_all(
        gathered.reshape(1, batch_rows, dp_count, column_part),
        "dp",
        split_axis=2,
        concat_axis=0,
        tiled=True,
    )
    all_rows = spread.reshape(dp_count * batch_rows, column_part)
    base_out = lax.psum_scatter(
        jnp.dot(all_rows, up_weight, preferred_element_type=jnp.float32).astype(jnp.bfloat16),
        "dp",
        scatter_dimension=0,
        tiled=True,
    ).astype(jnp.float32)
    slice_start = tp_index * slice_cols
    feature_slice = lax.dynamic_slice_in_dim(all_rows, slice_start, slice_cols, 1).reshape(
        all_blocks, ROWS_BLK, slice_cols
    )
    down_blocks = jnp.take(adapter_down, block_tenant, axis=0)
    proj_part = jnp.einsum(
        "nrd,nkd->nrk", feature_slice, down_blocks, preferred_element_type=jnp.float32
    )
    local_ids = lax.dynamic_slice_in_dim(block_tenant, dp_index * local_blocks, local_blocks, 0)
    up_mine = jnp.take(adapter_up, local_ids, axis=0)
    out_blocks = grad_out.reshape(local_blocks, ROWS_BLK, grad_out.shape[1])
    back_part = jnp.einsum("nrf,nkf->nrk", out_blocks, up_mine, preferred_element_type=jnp.float32)
    back_full = lax.dynamic_update_slice_in_dim(
        jnp.zeros((all_blocks, ROWS_BLK, rank_width), jnp.float32),
        back_part,
        dp_index * local_blocks,
        0,
    )
    proj_sum, back_sum = lax.psum(
        (proj_part.reshape(-1, 2 * rank_width), back_full.reshape(-1, 2 * rank_width)),
        ("dp", "tensor"),
    )
    projected = proj_sum.reshape(all_blocks, ROWS_BLK, rank_width).astype(jnp.bfloat16)
    back_proj = (SCALE * back_sum).reshape(all_blocks, ROWS_BLK, rank_width).astype(jnp.bfloat16)
    proj_mine = lax.dynamic_slice_in_dim(projected, dp_index * local_blocks, local_blocks, 0)
    adapter_term = jnp.einsum(
        "nrk,nkf->nrf", proj_mine, up_mine, preferred_element_type=jnp.float32
    ).reshape(batch_rows, -1)
    layer_out = (base_out + SCALE * adapter_term).astype(jnp.bfloat16)
    down_terms = jnp.einsum(
        "nrk,nrd->nkd", back_proj, feature_slice, preferred_element_type=jnp.float32
    )
    tenant_ids = jnp.arange(tenants, dtype=jnp.int32)
    onehot = (block_tenant[None, :] == tenant_ids[:, None]).astype(jnp.float32)
    inverse = 1.0 / jnp.sum(onehot, axis=1)
    grad_down = (
        jnp.einsum("tn,nkd->tkd", onehot, down_terms, precision=lax.Precision.HIGHEST)
        * inverse[:, None, None]
    )
    up_terms = SCALE * jnp.einsum(
        "nrk,nrf->nkf", proj_mine, out_blocks, preferred_element_type=jnp.float32
    )
    same_owner = owner_of[:, None] == owner_of[None, :]
    earlier = tenant_ids[None, :] < tenant_ids[:, None]
    rank_in = jnp.sum(jnp.logical_and(same_owner, earlier), axis=1)
    slot_of = owner_of * OWN_MAX + rank_in
    own_slots = dp_index * OWN_MAX + jnp.arange(OWN_MAX, dtype=jnp.int32)
    ownership = (slot_of[None, :] == own_slots[:, None]).astype(jnp.float32)
    own_scale = jnp.dot(ownership, inverse, precision=lax.Precision.HIGHEST)
    total_slots = dp_count * OWN_MAX
    local_slots = jnp.take(slot_of, local_ids, axis=0)
    placement = (local_slots[None, :] == jnp.arange(total_slots, dtype=jnp.int32)[:, None]).astype(
        jnp.float32
    )
    buffer = jnp.einsum("sn,nkf->skf", placement, up_terms, precision=lax.Precision.HIGHEST)
    summed = lax.psum_scatter(
        buffer.astype(jnp.bfloat16), "dp", scatter_dimension=0, tiled=True
    ).astype(jnp.float32)
    grad_up = summed * own_scale[:, None, None]
    return (layer_out, grad_down, grad_up)


def solution(mesh):
    placed = (
        P(("groups", "dp", "tensor"), None),
        P("dp", "tensor"),
        P("groups", None, ("dp", "tensor")),
        P("groups", None, "tensor"),
        P(("groups", "dp"), "tensor"),
        P("groups"),
        P("groups"),
    )
    return jax.shard_map(
        local if mesh.shape["dp"] == 4 else local_plain,
        mesh=mesh,
        in_specs=placed,
        out_specs=(
            P(("groups", "dp"), "tensor"),
            P("groups", None, ("dp", "tensor")),
            P(("groups", "dp"), None, "tensor"),
        ),
        check_vma=False,
    )
```

time: 445 us -> 506 us (1.14)
  Pallas kernels: 156 us -> 196 us
  blocking collectives: 0 us -> 31.8 us
  starting transfers between devices: 134 us -> 103 us
  between operations: 1.76 us -> 14.7 us
  local copies, waits for them, and re-layouts: 23.6 us -> 12.5 us
  waiting for transfers between devices: 105 us -> 116 us
    ppermute x24 -> x5, starting transfers between devices: 37 us -> 2.2 us  [across(): return lax.ppermute(value, axis, [(i, i ^ bit) for i in range(count)])]
    all_gather x0 -> x2, blocking collectives: none -> 31.8 us  [the longest x1 26.6 us: local(): backs = lax.all_gather(late_use(back_mine), 'dp', axis=0)]
    pallas_call x3 -> x4, Pallas kernels: 18.5 us -> 36.1 us  [combine(): call(functools.partial(combine_kernel, len(terms), len(extras)), 4 * slot...]
    pallas_call x16, Pallas kernels: 128 us -> 142 us  [share(): call(functools.partial(share_kernel, masks, has_add, len(deps)), 2 * batc...]
    psum x0 -> x1, waiting for transfers between devices: none -> 13.4 us  [local(): back_mine = (SCALE * lax.psum(back_part.now, 'tensor')).astype(jnp.bfloat16)]
    unnamed x148 -> x80, local copies, waits for them, and re-layouts: 17 us -> 6.7 us
    pallas_call x1, Pallas kernels: 4.01 us -> 10.3 us  [backward(): call(backward_kernel, 2 * batch_rows * hidden * rank_width * 4, out_shape...]
    ppermute x30 -> x26, starting transfers between devices: 90.1 us -> 94.1 us  [the longest x10 52.2 us: first_hop(): return lax.ppermute(value, 'dp', [(0, 1), (3, 2)])]
  transfers between devices with their start and end apart: 55 -> 38, of which waited for: 12 -> 12; matrix products, arithmetic and copies ran while one was open for 6% -> 6% of each run, Pallas kernels for 33% -> 37%
where the time goes in v2:
time: 506 us; the launch traced here: 503 us
  Pallas kernels  196 us (39%)
  waiting for transfers between devices  116 us (23%)
  starting transfers between devices  103 us (20%)
  blocking collectives  31.8 us (6%)
  other arithmetic  19.6 us (4%)
  between operations  14.7 us (3%)
  local copies, waits for them, and re-layouts  12.5 us (2%)
  matrix products  8.85 us (2%)
    pallas_call x16, Pallas kernels, share(): call(functools.partial(share_kernel, masks, has_add, len(deps)), 2 * batc...  142 us
    ppermute x10, starting transfers between devices, first_hop(): return lax.ppermute(value, 'dp', [(0, 1), (3, 2)])  52.2 us
    pallas_call x4, Pallas kernels, combine(): call(functools.partial(combine_kernel, len(terms), len(extras)), 4 * slot...  36.1 us
    ppermute x5, waiting for transfers between devices, across(): return lax.ppermute(value, axis, [(i, i ^ bit) for i in range(count)])  35.8 us
    ppermute x4, waiting for transfers between devices, first_and_last_hop(): return lax.ppermute(value, 'dp', [(0, 1), (3, 2), (1, 0), (2, 3)])  34.9 us
    all_gather x1, blocking collectives, local(): backs = lax.all_gather(late_use(back_mine), 'dp', axis=0)  26.6 us
    ppermute x4, starting transfers between devices, first_and_last_hop(): return lax.ppermute(value, 'dp', [(0, 1), (3, 2), (1, 0), (2, 3)])  24.8 us
    ppermute x10, waiting for transfers between devices, first_hop(): return lax.ppermute(value, 'dp', [(0, 1), (3, 2)])  18.2 us
  transfers between devices with their start and end apart: 38, of which 12 were waited for; matrix products, arithmetic and copies ran while one was open for 6% of the time, Pallas kernels for 37%

profile of v2, /device:TPU:0, one launch (start us, length us, event | category | flops | bytes accessed | tf_op | source)
XLA Modules:
  0.0 503.2 jit_solution(6486020360389581753)
XLA Ops:
  9.5 7.0 %collective-permute-start = (bf16[64,4096]{1,0:T(8,128)(2,1)S(1)}, bf16[64,4096]{1,0:T(8,128)(2,1)S(1)}, u32[]{:S(2)}, u32[]{:S(2)}) collective-permute-start(bf16[64,4096]{1,0:T(8,128)(2,1)S(1)} %get-tuple-element.75), channel_id=1, source_target_pairs={{0,12},{12,0},{1,13},{13,1},{2,14},{14,2},{3,15},{15,3},{16,28},{2... | collective-permute-start | bytes 1572872 | tf_op jit(solution)/shard_map/ppermute | solution.py:298
  17.1 12.2 %collective-permute-done = bf16[64,4096]{1,0:T(8,128)(2,1)S(1)} collective-permute-done((bf16[64,4096]{1,0:T(8,128)(2,1)S(1)}, bf16[64,4096]{1,0:T(8,128)(2,1)S(1)}, u32[]{:S(2)}, u32[]{:S(2)}) %collective-permute-start) | collective-permute-done | bytes 524320 | tf_op jit(solution)/shard_map/ppermute | solution.py:298
  29.3 21.5 %collective-permute-done.1.refs_1_ = bf16[64,4096]{1,0:T(8,128)(2,1)S(1)} collective-permute-done((bf16[64,4096]{1,0:T(8,128)(2,1)S(1)}, bf16[64,4096]{1,0:T(8,128)(2,1)S(1)}, u32[]{:S(2)}, u32[]{:S(2)}) %collective-permute-start.1) | collective-permute-done | bytes 524320 | tf_op jit(solution)/shard_map/ppermute | solution.py:37
  54.0 12.4 %collective-permute-done.4.refs_1_.refs_5_ = bf16[64,4096]{1,0:T(8,128)(2,1)S(1)} collective-permute-done((bf16[64,4096]{1,0:T(8,128)(2,1)S(1)}, bf16[64,4096]{1,0:T(8,128)(2,1)S(1)}, u32[]{:S(2)}, u32[]{:S(2)}) %collective-permute-start.4) | collective-permute-done | bytes 524320 | tf_op jit(solution)/shard_map/ppermute | solution.py:37
  69.0 6.2 %first0.1.refs_5_ = bf16[256,1024]{1,0:T(8,128)(2,1)} custom-call(s32[1]{0:T(128)} %bitcast.index, bf16[64,4096]{1,0:T(8,128)(2,1)} %copy-done.1, bf16[64,4096]{1,0:T(8,128)(2,1)} %copy-done.4, bf16[64,4096]{1,0:T(8,128)(2,1)} %copy-done.5, bf16[64,4096]{1,0:T(8,128)(2,1)} %copy-done.6, bf16[4096,6656]{1,0:T(8,128)(2,1)} %refs_1_.23), custom_call_target="tpu_custom_call" | custom-call | flops 357913952 | tf_op jit(solution)/shard_map/first0/pallas_call | solution.py:116
  76.3 8.8 %first1.1.refs_5_ = bf16[256,1536]{1,0:T(8,128)(2,1)} custom-call(s32[1]{0:T(128)} %bitcast.index, bf16[64,4096]{1,0:T(8,128)(2,1)} %copy-done.1, bf16[64,4096]{1,0:T(8,128)(2,1)} %copy-done.4, bf16[64,4096]{1,0:T(8,128)(2,1)} %copy-done.5, bf16[64,4096]{1,0:T(8,128)(2,1)} %copy-done.6, bf16[4096,6656]{1,0:T(8,128)(2,1)} %refs_1_.23, ...), custom_call_target="tpu_custom_call" | custom-call | flops 536870912 | tf_op jit(solution)/shard_map/first1/pallas_call | solution.py:116
  86.5 10.4 %first2.1.refs_5_ = bf16[256,2048]{1,0:T(8,128)(2,1)} custom-call(s32[1]{0:T(128)} %bitcast.index, bf16[64,4096]{1,0:T(8,128)(2,1)} %copy-done.1, bf16[64,4096]{1,0:T(8,128)(2,1)} %copy-done.4, bf16[64,4096]{1,0:T(8,128)(2,1)} %copy-done.5, bf16[64,4096]{1,0:T(8,128)(2,1)} %copy-done.6, bf16[4096,6656]{1,0:T(8,128)(2,1)} %refs_1_.23, ...), custom_call_target="tpu_custom_call" | custom-call | flops 715827904 | tf_op jit(solution)/shard_map/first2/pallas_call | solution.py:116
  104.8 8.9 %collective-permute-start.7 = (bf16[256,1024]{1,0:T(8,128)(2,1)}, bf16[256,1024]{1,0:T(8,128)(2,1)S(1)}, u32[]{:S(2)}, u32[]{:S(2)}) collective-permute-start(bf16[256,1024]{1,0:T(8,128)(2,1)} %first0.1.refs_5_), channel_id=1, source_target_pairs={{0,4},{12,8},{1,5},{13,9},{2,6},{14,10},{3,7},{15,11},{16,20},{28,... | collective-permute-start | bytes 1572872 | tf_op jit(solution)/shard_map/send0/ppermute | solution.py:283
  115.0 13.1 %collective-permute-done.7.refs_5_.refs_2_.refs_3_ = bf16[256,1024]{1,0:T(8,128)(2,1)S(1)} collective-permute-done((bf16[256,1024]{1,0:T(8,128)(2,1)}, bf16[256,1024]{1,0:T(8,128)(2,1)S(1)}, u32[]{:S(2)}, u32[]{:S(2)}) %collective-permute-start.7) | collective-permute-done | bytes 524320 | tf_op jit(solution)/shard_map/send0/ppermute | solution.py:283
  133.4 10.5 %first3.1.refs_4_ = bf16[256,2048]{1,0:T(8,128)(2,1)} custom-call(s32[1]{0:T(128)} %bitcast.index, bf16[64,4096]{1,0:T(8,128)(2,1)} %copy-done.1, bf16[64,4096]{1,0:T(8,128)(2,1)} %copy-done.4, bf16[64,4096]{1,0:T(8,128)(2,1)} %copy-done.5, bf16[64,4096]{1,0:T(8,128)(2,1)} %copy-done.6, bf16[4096,6656]{1,0:T(8,128)(2,1)} %refs_1_.23, ...), custom_call_target="tpu_custom_call" | custom-call | flops 715827904 | tf_op jit(solution)/shard_map/first3/pallas_call | solution.py:116
  150.2 6.3 %two0.1.refs_4_ = bf16[256,1024]{1,0:T(8,128)(2,1)} custom-call(s32[1]{0:T(128)} %bitcast.index, bf16[256,4096]{1,0:T(8,128)(2,1)} %all-gather.9.cloned.1.call-done.refs_0_.refs_8_, bf16[4096,6656]{1,0:T(8,128)(2,1)} %refs_1_.23, bf16[256,1024]{1,0:T(8,128)(2,1)} %copy-done.16, bf16[256,1024]{1,0:T(8,128)(2,1)} %copy-done.16, bf16[256,2048]{1,0:T(8,128)(2,1)} %first3.1.refs_4_), custom_call_target="tpu_custom_call" | custom-call | flops 357913952 | tf_op jit(solution)/shard_map/two0/pallas_call | solution.py:116
  158.7 8.6 %two1.1 = bf16[256,1536]{1,0:T(8,128)(2,1)} custom-call(s32[1]{0:T(128)} %bitcast.index, bf16[256,4096]{1,0:T(8,128)(2,1)} %all-gather.9.cloned.1.call-done.refs_0_.refs_8_, bf16[4096,6656]{1,0:T(8,128)(2,1)} %refs_1_.23, bf16[256,1536]{1,0:T(8,128)(2,1)} %copy-done.23, bf16[256,1536]{1,0:T(8,128)(2,1)} %copy-done.23, bf16[256,1024]{1,0:T(8,128)(2,1)} %two0.1.refs_4_), custom_call_target="tpu_custom_call" | custom-call | flops 536870912 | tf_op jit(solution)/shard_map/two1/pallas_call | solution.py:116
  182.1 10.2 %two2.1.refs_4_ = bf16[256,2048]{1,0:T(8,128)(2,1)} custom-call(s32[1]{0:T(128)} %bitcast.index, bf16[256,4096]{1,0:T(8,128)(2,1)} %all-gather.9.cloned.1.call-done.refs_0_.refs_8_, bf16[4096,6656]{1,0:T(8,128)(2,1)} %refs_1_.23, bf16[256,2048]{1,0:T(8,128)(2,1)} %collective-permute-done.9.refs_2_.refs_3_, ...), custom_call_target="tpu_custom_call" | custom-call | flops 715827904 | tf_op jit(solution)/shard_map/two2/pallas_call | solution.py:116
  194.0 10.2 %two3.1.refs_4_ = bf16[256,2048]{1,0:T(8,128)(2,1)} custom-call(s32[1]{0:T(128)} %bitcast.index, bf16[256,4096]{1,0:T(8,128)(2,1)} %all-gather.9.cloned.1.call-done.refs_0_.refs_8_, bf16[4096,6656]{1,0:T(8,128)(2,1)} %refs_1_.23, bf16[256,2048]{1,0:T(8,128)(2,1)} %collective-permute-done.12.refs_2_.refs_3_, ...), custom_call_target="tpu_custom_call" | custom-call | flops 715827904 | tf_op jit(solution)/shard_map/two3/pallas_call | solution.py:116
  218.1 8.7 %one1.1 = bf16[256,1536]{1,0:T(8,128)(2,1)} custom-call(s32[1]{0:T(128)} %bitcast.index, bf16[256,4096]{1,0:T(8,128)(2,1)} %all-gather.11.cloned.1.call-done.refs_0_.refs_9_, bf16[4096,6656]{1,0:T(8,128)(2,1)} %refs_1_.23, bf16[256,1536]{1,0:T(8,128)(2,1)} %collective-permute-done.11.refs_2_, bf16[64,6656]{1,0:T(8,128)(2,1)} %copy-done.3, ...), custom_call_target="tpu_custom_call" | custom-call | flops 536870912 | tf_op jit(solution)/shard_map/one1/pallas_call | solution.py:116
  226.8 10.3 %shard_map.94 = f32[256,64]{1,0:T(8,128)} custom-call(s32[2]{0:T(128)} %fusion.28.ids, bf16[256,6656]{1,0:T(8,128)(2,1)} %grad.1, bf16[4,64,6656]{2,1,0:T(8,128)(2,1)} %up.1), custom_call_target="tpu_custom_call" | custom-call | flops 145402544 | tf_op jit(solution)/shard_map/pallas_call | solution.py:177
  242.1 8.6 %far_terms.1.refs_4_ = bf16[2,64,6656]{2,1,0:T(8,128)(2,1)} custom-call(f32[2,4]{1,0:T(2,128)} %add_convert_fusion.4.weights, f32[2]{0:T(128)} %broadcast_16_scale.2.scale, bf16[1,64,6656]{2,1,0:T(8,128)(2,1)} %bitcast.55, bf16[1,64,6656]{2,1,0:T(8,128)(2,1)} %bitcast.51, bf16[1,64,6656]{2,1,0:T(8,128)(2,1)} %bitcast.59, bf16[1,64,6656]{2,1,0:T(8,128)(2,1)} %bitcast.66), custom_call_target="tpu_custom_call" | custom-call | flops 2271914 | tf_op jit(solution)/shard_map/far_terms/pallas_call | solution.py:252
  251.4 6.3 %collective-permute-start.21 = (bf16[256,1536]{1,0:T(8,128)(2,1)}, bf16[256,1536]{1,0:T(8,128)(2,1)S(1)}, u32[]{:S(2)}, u32[]{:S(2)}) collective-permute-start(bf16[256,1536]{1,0:T(8,128)(2,1)} %two1.1), channel_id=1, source_target_pairs={{0,4},{12,8},{1,5},{13,9},{2,6},{14,10},{3,7},{15,11},{16,20},{28,... | collective-permute-start | bytes 2359304 | tf_op jit(solution)/shard_map/send7/ppermute | solution.py:283
  257.8 13.4 %all-reduce.3.cloned.1.call-done = f32[256,64]{1,0:T(8,128)} async-done(((f32[256,64]{1,0:T(8,128)}), f32[256,64]{1,0:T(8,128)}) %all-reduce.3.cloned.1.call-update) | async-done | bytes 65552 | tf_op jit(solution)/shard_map/back_mine/psum | solution.py:444
  278.5 8.8 %last_terms.1 = bf16[2,64,6656]{2,1,0:T(8,128)(2,1)} custom-call(f32[2,2]{1,0:T(2,128)} %get-tuple-element.162.weights, f32[2]{0:T(128)} %broadcast_16_scale.2.scale, bf16[1,64,6656]{2,1,0:T(8,128)(2,1)} %bitcast.56, bf16[1,64,6656]{2,1,0:T(8,128)(2,1)} %bitcast.52, bf16[2,64,6656]{2,1,0:T(8,128)(2,1)} %copy-done.29), custom_call_target="tpu_custom_call" | custom-call | flops 1135957 | tf_op jit(solution)/shard_map/last_terms/pallas_call | solution.py:252
  288.7 8.6 %near_terms.1.refs_4_ = bf16[2,64,6656]{2,1,0:T(8,128)(2,1)} custom-call(f32[2,4]{1,0:T(2,128)} %add_convert_fusion.5.weights, f32[2]{0:T(128)} %broadcast_16_scale.2.scale, bf16[1,64,6656]{2,1,0:T(8,128)(2,1)} %bitcast.57, bf16[1,64,6656]{2,1,0:T(8,128)(2,1)} %bitcast.53, bf16[1,64,6656]{2,1,0:T(8,128)(2,1)} %bitcast.60, bf16[1,64,6656]{2,1,0:T(8,128)(2,1)} %bitcast.67), custom_call_target="tpu_custom_call" | custom-call | flops 2271914 | tf_op jit(solution)/shard_map/near_terms/pallas_call | solution.py:252
  299.2 18.7 %collective-permute-start.18 = (bf16[256,1024]{1,0:T(8,128)(2,1)S(1)}, bf16[256,1024]{1,0:T(8,128)(2,1)}, u32[]{:S(2)}, u32[]{:S(2)}) collective-permute-start(bf16[256,1024]{1,0:T(8,128)(2,1)S(1)} %copy-done.25), channel_id=1, source_target_pairs={{0,4},{12,8},{4,0},{8,12},{1,5},{13,9},{5,1},{9,13},{2,6},{14,10},... | collective-permute-start | bytes 1572872 | tf_op jit(solution)/shard_map/send8/ppermute | solution.py:292
  324.9 10.4 %one2.1.refs_4_ = bf16[256,2048]{1,0:T(8,128)(2,1)} custom-call(s32[1]{0:T(128)} %bitcast.index, bf16[256,4096]{1,0:T(8,128)(2,1)} %all-gather.11.cloned.1.call-done.refs_0_.refs_9_, bf16[4096,6656]{1,0:T(8,128)(2,1)} %refs_1_.23, bf16[256,2048]{1,0:T(8,128)(2,1)} %collective-permute-done.15.refs_2_, bf16[256,1024]{1,0:T(8,128)(2,1)} %copy-done.15, ...), custom_call_target="tpu_custom_call" | custom-call | flops 715827904 | tf_op jit(solution)/shard_map/one2/pallas_call | solution.py:116
  335.2 17.7 %collective-permute-done.18.refs_3_ = bf16[256,1024]{1,0:T(8,128)(2,1)} collective-permute-done((bf16[256,1024]{1,0:T(8,128)(2,1)S(1)}, bf16[256,1024]{1,0:T(8,128)(2,1)}, u32[]{:S(2)}, u32[]{:S(2)}) %collective-permute-start.18) | collective-permute-done | bytes 524320 | tf_op jit(solution)/shard_map/send8/ppermute | solution.py:292
  355.2 14.9 %collective-permute-start.26 = (bf16[256,2048]{1,0:T(8,128)(2,1)S(1)}, bf16[256,2048]{1,0:T(8,128)(2,1)}, u32[]{:S(2)}, u32[]{:S(2)}) collective-permute-start(bf16[256,2048]{1,0:T(8,128)(2,1)S(1)} %copy-done.18), channel_id=1, source_target_pairs={{0,4},{12,8},{1,5},{13,9},{2,6},{14,10},{3,7},{15,11},{16,20},{28,... | collective-permute-start | bytes 3145736 | tf_op jit(solution)/shard_map/send11/ppermute | solution.py:283
  370.9 8.7 %late1.1 = bf16[256,1536]{1,0:T(8,128)(2,1)} custom-call(s32[1]{0:T(128)} %bitcast.index, bf16[256,4096]{1,0:T(8,128)(2,1)} %all-gather.7.cloned.1.call-done.refs_0_.refs_10_, bf16[4096,6656]{1,0:T(8,128)(2,1)} %refs_1_.23, bf16[256,1536]{1,0:T(8,128)(2,1)} %copy-done.22, bf16[256,1536]{1,0:T(8,128)(2,1)} %copy-done.22, bf16[256,2048]{1,0:T(8,128)(2,1)} %one2.1.refs_4_), custom_call_target="tpu_custom_call" | custom-call | flops 536870912 | tf_op jit(solution)/shard_map/late1/pallas_call | solution.py:116
  382.1 26.6 %all-gather.1 = bf16[1024,64]{1,0:T(8,128)(2,1)S(1)} all-gather(bf16[256,64]{1,0:T(8,128)(2,1)S(1)} %multiply_convert_fusion), channel_id=3, replica_groups=mesh['groups'=2,'dp'=4,'tensor'=4] {'dp'}, dimensions={0}, use_global_device_ids=true | all-gather | bytes 163840 | tf_op jit(solution)/shard_map/backs/all_gather | solution.py:456
  408.7 10.2 %one3.1 = bf16[256,2048]{1,0:T(8,128)(2,1)} custom-call(s32[1]{0:T(128)} %bitcast.index, bf16[256,4096]{1,0:T(8,128)(2,1)} %all-gather.11.cloned.1.call-done.refs_0_.refs_9_, bf16[4096,6656]{1,0:T(8,128)(2,1)} %refs_1_.23, bf16[256,2048]{1,0:T(8,128)(2,1)} %collective-permute-done.17.refs_2_, bf16[256,1024]{1,0:T(8,128)(2,1)} %collective-permute-done.18.refs_3_, ...), custom_call_target="tpu_custom_call" | custom-call | flops 715827904 | tf_op jit(solution)/shard_map/one3/pallas_call | solution.py:116
  424.5 10.3 %late2.1.refs_4_ = bf16[256,2048]{1,0:T(8,128)(2,1)} custom-call(s32[1]{0:T(128)} %bitcast.index, bf16[256,4096]{1,0:T(8,128)(2,1)} %all-gather.7.cloned.1.call-done.refs_0_.refs_10_, bf16[4096,6656]{1,0:T(8,128)(2,1)} %refs_1_.23, bf16[256,2048]{1,0:T(8,128)(2,1)} %copy-done.19, bf16[256,2048]{1,0:T(8,128)(2,1)} %copy-done.19, f32[4,64,1024]{2,1,0:T(8,128)} %shard_map.95.refs_4_), custom_call_target="tpu_custom_call" | custom-call | flops 715827904 | tf_op jit(solution)/shard_map/late2/pallas_call | solution.py:116
  436.6 10.2 %late3.1 = bf16[256,2048]{1,0:T(8,128)(2,1)} custom-call(s32[1]{0:T(128)} %bitcast.index, bf16[256,4096]{1,0:T(8,128)(2,1)} %all-gather.7.cloned.1.call-done.refs_0_.refs_10_, bf16[4096,6656]{1,0:T(8,128)(2,1)} %refs_1_.23, bf16[256,2048]{1,0:T(8,128)(2,1)} %collective-permute-done.26.refs_2_.refs_3_, ...), custom_call_target="tpu_custom_call" | custom-call | flops 715827904 | tf_op jit(solution)/shard_map/late3/pallas_call | solution.py:116
  461.3 10.0 %shard_map.96 = f32[2,64,6656]{2,1,0:T(8,128)} custom-call(f32[2,4]{1,0:T(2,128)} %add_select_fusion.weights, f32[2]{0:T(128)} %copy-done.33, bf16[1,64,6656]{2,1,0:T(8,128)(2,1)} %bitcast.58, bf16[1,64,6656]{2,1,0:T(8,128)(2,1)} %bitcast.54, bf16[1,64,6656]{2,1,0:T(8,128)(2,1)} %bitcast.61, bf16[1,64,6656]{2,1,0:T(8,128)(2,1)} %bitcast.68, ...), custom_call_target="tpu_custom_call" | custom-call | flops 2271914 | tf_op jit(solution)/shard_map/pallas_call | solution.py:252
  480.6 12.4 %collective-permute-done.31 = bf16[256,2048]{1,0:T(8,128)(2,1)} collective-permute-done((bf16[256,2048]{1,0:T(8,128)(2,1)}, bf16[256,2048]{1,0:T(8,128)(2,1)}, u32[]{:S(2)}, u32[]{:S(2)}) %collective-permute-start.31) | collective-permute-done | bytes 1048608 | tf_op jit(solution)/shard_map/send13/ppermute | solution.py:292
  (202 shorter events, 127.6 us)
Async XLA Ops:
  7.2 91.7 %all-gather.13.cloned.1.call-start = ((), (), s32[]{:S(2)}) async-start(), calls=%async_computation.6 | async-start | bytes 2621440 | tf_op jit(solution)/shard_map/all_gather | solution.py:297
  7.9 142.3 %all-gather.9.cloned.1.call-start = ((), (), s32[]{:S(2)}) async-start(), calls=%async_computation.3 | async-start | bytes 2621440 | tf_op jit(solution)/shard_map/two_rows/all_gather | solution.py:295
  16.4 34.4 %collective-permute-start.1 = (bf16[64,4096]{1,0:T(8,128)(2,1)S(1)}, bf16[64,4096]{1,0:T(8,128)(2,1)S(1)}, u32[]{:S(2)}, u32[]{:S(2)}) collective-permute-start(bf16[64,4096]{1,0:T(8,128)(2,1)S(1)} %get-tuple-element.148), channel_id=1, source_target_pairs={{0,8},{4,12},{8,0},{12,4},{1,9},{5,13},{9,1},{13,5},{2,10},{6,14},... | collective-permute-start | bytes 1572872 | tf_op jit(solution)/shard_map/ppermute | solution.py:37
  16.5 34.3 %collective-permute-start.2 = (bf16[64,4096]{1,0:T(8,128)(2,1)S(1)}, bf16[64,4096]{1,0:T(8,128)(2,1)S(1)}, u32[]{:S(2)}, u32[]{:S(2)}) collective-permute-start(bf16[64,4096]{1,0:T(8,128)(2,1)S(1)} %get-tuple-element.147), channel_id=1, source_target_pairs={{0,4},{4,0},{8,12},{12,8},{1,5},{5,1},{9,13},{13,9},{2,6},{6,2},{1... | collective-permute-start | bytes 1572872 | tf_op jit(solution)/shard_map/ppermute | solution.py:37
  75.3 82.6 %reduce-scatter.2.cloned.1.call-start = ((), (), s32[]{:S(2)}) async-start(), calls=%async_computation.2 | async-start | bytes 163840 | tf_op jit(solution)/shard_map/forward/reduce_scatter | solution.py:384
  104.2 107.7 %all-gather.11.cloned.1.call-start = ((), (), s32[]{:S(2)}) async-start(), calls=%async_computation.4 | async-start | bytes 2621440 | tf_op jit(solution)/shard_map/one_rows/all_gather | solution.py:295
  104.7 166.5 %all-reduce.3.cloned.1.call-start = ((), (), s32[]{:S(2)}) async-start(), calls=%async_computation.5 | async-start | bytes 262144 | tf_op jit(solution)/shard_map/back_mine/psum | solution.py:444
  104.8 23.3 %collective-permute-start.7 = (bf16[256,1024]{1,0:T(8,128)(2,1)}, bf16[256,1024]{1,0:T(8,128)(2,1)S(1)}, u32[]{:S(2)}, u32[]{:S(2)}) collective-permute-start(bf16[256,1024]{1,0:T(8,128)(2,1)} %first0.1.refs_5_), channel_id=1, source_target_pairs={{0,4},{12,8},{1,5},{13,9},{2,6},{14,10},{3,7},{15,11},{16,20},{28,... | collective-permute-start | bytes 1572872 | tf_op jit(solution)/shard_map/send0/ppermute | solution.py:283
  113.7 31.2 %collective-permute-start.8 = (bf16[256,1536]{1,0:T(8,128)(2,1)S(1)}, bf16[256,1536]{1,0:T(8,128)(2,1)S(1)}, u32[]{:S(2)}, u32[]{:S(2)}) collective-permute-start(bf16[256,1536]{1,0:T(8,128)(2,1)S(1)} %copy-done.13), channel_id=1, source_target_pairs={{0,4},{12,8},{1,5},{13,9},{2,6},{14,10},{3,7},{15,11},{16,20},{28,... | collective-permute-start | bytes 2359304 | tf_op jit(solution)/shard_map/send1/ppermute | solution.py:283
  128.1 47.9 %collective-permute-start.9 = (bf16[256,2048]{1,0:T(8,128)(2,1)S(1)}, bf16[256,2048]{1,0:T(8,128)(2,1)}, u32[]{:S(2)}, u32[]{:S(2)}) collective-permute-start(bf16[256,2048]{1,0:T(8,128)(2,1)S(1)} %copy-done.10), channel_id=1, source_target_pairs={{0,4},{12,8},{1,5},{13,9},{2,6},{14,10},{3,7},{15,11},{16,20},{28,... | collective-permute-start | bytes 3145736 | tf_op jit(solution)/shard_map/send2/ppermute | solution.py:283
  144.8 49.2 %collective-permute-start.12 = (bf16[256,2048]{1,0:T(8,128)(2,1)}, bf16[256,2048]{1,0:T(8,128)(2,1)}, u32[]{:S(2)}, u32[]{:S(2)}) collective-permute-start(bf16[256,2048]{1,0:T(8,128)(2,1)} %first3.1.refs_4_), channel_id=1, source_target_pairs={{0,4},{12,8},{1,5},{13,9},{2,6},{14,10},{3,7},{15,11},{16,20},{28,... | collective-permute-start | bytes 3145736 | tf_op jit(solution)/shard_map/send3/ppermute | solution.py:283
  156.5 37.6 %collective-permute-start.13 = (bf16[256,1024]{1,0:T(8,128)(2,1)}, bf16[256,1024]{1,0:T(8,128)(2,1)}, u32[]{:S(2)}, u32[]{:S(2)}) collective-permute-start(bf16[256,1024]{1,0:T(8,128)(2,1)} %two0.1.refs_4_), channel_id=1, source_target_pairs={{4,8},{8,4},{5,9},{9,5},{6,10},{10,6},{7,11},{11,7},{20,24},{24,20... | collective-permute-start | bytes 1572872 | tf_op jit(solution)/shard_map/mid_two0/ppermute | solution.py:286
  167.3 42.4 %collective-permute-start.11 = (bf16[256,1536]{1,0:T(8,128)(2,1)}, bf16[256,1536]{1,0:T(8,128)(2,1)}, u32[]{:S(2)}, u32[]{:S(2)}) collective-permute-start(bf16[256,1536]{1,0:T(8,128)(2,1)} %two1.1), channel_id=1, source_target_pairs={{4,8},{8,4},{5,9},{9,5},{6,10},{10,6},{7,11},{11,7},{20,24},{24,20... | collective-permute-start | bytes 2359304 | tf_op jit(solution)/shard_map/mid_two1/ppermute | solution.py:286
  175.9 33.8 %collective-permute-start.10 = (bf16[64,6656]{1,0:T(8,128)(2,1)S(1)}, bf16[64,6656]{1,0:T(8,128)(2,1)S(1)}, u32[]{:S(2)}, u32[]{:S(2)}) collective-permute-start(bf16[64,6656]{1,0:T(8,128)(2,1)S(1)} %fusion), channel_id=1, source_target_pairs={{0,4},{12,8},{1,5},{13,9},{2,6},{14,10},{3,7},{15,11},{16,20},{28,... | collective-permute-start | bytes 2555912 | tf_op jit(solution)/shard_map/send4/ppermute | solution.py:283
  192.2 44.9 %collective-permute-start.15 = (bf16[256,2048]{1,0:T(8,128)(2,1)}, bf16[256,2048]{1,0:T(8,128)(2,1)}, u32[]{:S(2)}, u32[]{:S(2)}) collective-permute-start(bf16[256,2048]{1,0:T(8,128)(2,1)} %two2.1.refs_4_), channel_id=1, source_target_pairs={{4,8},{8,4},{5,9},{9,5},{6,10},{10,6},{7,11},{11,7},{20,24},{24,20... | collective-permute-start | bytes 3145736 | tf_op jit(solution)/shard_map/mid_two2/ppermute | solution.py:286
  204.3 34.9 %collective-permute-start.17 = (bf16[256,2048]{1,0:T(8,128)(2,1)}, bf16[256,2048]{1,0:T(8,128)(2,1)}, u32[]{:S(2)}, u32[]{:S(2)}) collective-permute-start(bf16[256,2048]{1,0:T(8,128)(2,1)} %two3.1.refs_4_), channel_id=1, source_target_pairs={{4,8},{8,4},{5,9},{9,5},{6,10},{10,6},{7,11},{11,7},{20,24},{24,20... | collective-permute-start | bytes 3145736 | tf_op jit(solution)/shard_map/mid_two3/ppermute | solution.py:286
  205.9 31.2 %collective-permute-start.14 = (bf16[64,6656]{1,0:T(8,128)(2,1)S(1)}, bf16[64,6656]{1,0:T(8,128)(2,1)S(1)}, u32[]{:S(2)}, u32[]{:S(2)}) collective-permute-start(bf16[64,6656]{1,0:T(8,128)(2,1)S(1)} %copy-done), channel_id=1, source_target_pairs={{0,4},{12,8},{1,5},{13,9},{2,6},{14,10},{3,7},{15,11},{16,20},{28,... | collective-permute-start | bytes 2555912 | tf_op jit(solution)/shard_map/send5/ppermute | solution.py:283
  209.8 29.4 %collective-permute-start.16 = (bf16[256,1024]{1,0:T(8,128)(2,1)}, bf16[256,1024]{1,0:T(8,128)(2,1)S(1)}, u32[]{:S(2)}, u32[]{:S(2)}) collective-permute-start(bf16[256,1024]{1,0:T(8,128)(2,1)} %two0.1.refs_4_), channel_id=1, source_target_pairs={{0,4},{12,8},{1,5},{13,9},{2,6},{14,10},{3,7},{15,11},{16,20},{28,... | collective-permute-start | bytes 1572872 | tf_op jit(solution)/shard_map/send6/ppermute | solution.py:283
  239.2 78.7 %all-gather.7.cloned.1.call-start = ((), (), s32[]{:S(2)}) async-start(), calls=%async_computation.1 | async-start | bytes 2621440 | tf_op jit(solution)/shard_map/late_rows/all_gather | solution.py:295
  250.7 26.6 %collective-permute-start.19 = (bf16[2,64,6656]{2,1,0:T(8,128)(2,1)}, bf16[2,64,6656]{2,1,0:T(8,128)(2,1)S(1)}, u32[]{:S(2)}, u32[]{:S(2)}) collective-permute-start(bf16[2,64,6656]{2,1,0:T(8,128)(2,1)} %far_terms.1.refs_4_), channel_id=1, source_target_pairs={{4,8},{8,4},{5,9},{9,5},{6,10},{10,6},{7,11},{11,7},{20,24},{24,20... | collective-permute-start | bytes 5111816 | tf_op jit(solution)/shard_map/far_terms/ppermute | solution.py:286
  274.2 80.9 %collective-permute-start.24 = (bf16[256,1536]{1,0:T(8,128)(2,1)}, bf16[256,1536]{1,0:T(8,128)(2,1)}, u32[]{:S(2)}, u32[]{:S(2)}) collective-permute-start(bf16[256,1536]{1,0:T(8,128)(2,1)} %one1.1), channel_id=1, source_target_pairs={{0,4},{12,8},{4,0},{8,12},{1,5},{13,9},{5,1},{9,13},{2,6},{14,10},... | collective-permute-start | bytes 2359304 | tf_op jit(solution)/shard_map/send9/ppermute | solution.py:292
  287.3 136.3 %collective-permute-start.23 = (bf16[2,64,6656]{2,1,0:T(8,128)(2,1)}, bf16[2,64,6656]{2,1,0:T(8,128)(2,1)}, u32[]{:S(2)}, u32[]{:S(2)}) collective-permute-start(bf16[2,64,6656]{2,1,0:T(8,128)(2,1)} %last_terms.1), channel_id=1, source_target_pairs={{4,0},{8,12},{5,1},{9,13},{6,2},{10,14},{7,3},{11,15},{20,16},{24,... | collective-permute-start | bytes 5111816 | tf_op jit(solution)/shard_map/last_terms/ppermute | solution.py:289
  297.3 126.3 %collective-permute-start.27 = (bf16[2,64,6656]{2,1,0:T(8,128)(2,1)}, bf16[2,64,6656]{2,1,0:T(8,128)(2,1)}, u32[]{:S(2)}, u32[]{:S(2)}) collective-permute-start(bf16[2,64,6656]{2,1,0:T(8,128)(2,1)} %near_terms.1.refs_4_), channel_id=1, source_target_pairs={{4,8},{8,4},{5,9},{9,5},{6,10},{10,6},{7,11},{11,7},{20,24},{24,20... | collective-permute-start | bytes 5111816 | tf_op jit(solution)/shard_map/near_terms/ppermute | solution.py:286
  299.2 53.8 %collective-permute-start.18 = (bf16[256,1024]{1,0:T(8,128)(2,1)S(1)}, bf16[256,1024]{1,0:T(8,128)(2,1)}, u32[]{:S(2)}, u32[]{:S(2)}) collective-permute-start(bf16[256,1024]{1,0:T(8,128)(2,1)S(1)} %copy-done.25), channel_id=1, source_target_pairs={{0,4},{12,8},{4,0},{8,12},{1,5},{13,9},{5,1},{9,13},{2,6},{14,10},... | collective-permute-start | bytes 1572872 | tf_op jit(solution)/shard_map/send8/ppermute | solution.py:292
  324.0 30.3 %collective-permute-start.25 = (bf16[256,1024]{1,0:T(8,128)(2,1)}, bf16[256,1024]{1,0:T(8,128)(2,1)S(1)}, u32[]{:S(2)}, u32[]{:S(2)}) collective-permute-start(bf16[256,1024]{1,0:T(8,128)(2,1)} %late0.1.refs_4_), channel_id=1, source_target_pairs={{4,8},{8,4},{5,9},{9,5},{6,10},{10,6},{7,11},{11,7},{20,24},{24,20... | collective-permute-start | bytes 1572872 | tf_op jit(solution)/shard_map/mid_late0/ppermute | solution.py:286
  353.0 70.6 %collective-permute-start.20 = (bf16[256,2048]{1,0:T(8,128)(2,1)S(1)}, bf16[256,2048]{1,0:T(8,128)(2,1)S(1)}, u32[]{:S(2)}, u32[]{:S(2)}) collective-permute-start(bf16[256,2048]{1,0:T(8,128)(2,1)S(1)} %copy-done.17), channel_id=1, source_target_pairs={{0,4},{12,8},{1,5},{13,9},{2,6},{14,10},{3,7},{15,11},{16,20},{28,... | collective-permute-start | bytes 3145736 | tf_op jit(solution)/shard_map/send10/ppermute | solution.py:283
  355.2 68.4 %collective-permute-start.26 = (bf16[256,2048]{1,0:T(8,128)(2,1)S(1)}, bf16[256,2048]{1,0:T(8,128)(2,1)}, u32[]{:S(2)}, u32[]{:S(2)}) collective-permute-start(bf16[256,2048]{1,0:T(8,128)(2,1)S(1)} %copy-done.18), channel_id=1, source_target_pairs={{0,4},{12,8},{1,5},{13,9},{2,6},{14,10},{3,7},{15,11},{16,20},{28,... | collective-permute-start | bytes 3145736 | tf_op jit(solution)/shard_map/send11/ppermute | solution.py:283
  379.6 44.0 %collective-permute-start.22 = (bf16[256,1536]{1,0:T(8,128)(2,1)}, bf16[256,1536]{1,0:T(8,128)(2,1)}, u32[]{:S(2)}, u32[]{:S(2)}) collective-permute-start(bf16[256,1536]{1,0:T(8,128)(2,1)} %late1.1), channel_id=1, source_target_pairs={{4,8},{8,4},{5,9},{9,5},{6,10},{10,6},{7,11},{11,7},{20,24},{24,20... | collective-permute-start | bytes 2359304 | tf_op jit(solution)/shard_map/mid_late1/ppermute | solution.py:286
  434.8 37.0 %collective-permute-start.28 = (bf16[256,2048]{1,0:T(8,128)(2,1)}, bf16[256,2048]{1,0:T(8,128)(2,1)}, u32[]{:S(2)}, u32[]{:S(2)}) collective-permute-start(bf16[256,2048]{1,0:T(8,128)(2,1)} %late2.1.refs_4_), channel_id=1, source_target_pairs={{4,8},{8,4},{5,9},{9,5},{6,10},{10,6},{7,11},{11,7},{20,24},{24,20... | collective-permute-start | bytes 3145736 | tf_op jit(solution)/shard_map/mid_late2/ppermute | solution.py:286
  446.8 33.8 %collective-permute-start.30 = (bf16[256,2048]{1,0:T(8,128)(2,1)}, bf16[256,2048]{1,0:T(8,128)(2,1)}, u32[]{:S(2)}, u32[]{:S(2)}) collective-permute-start(bf16[256,2048]{1,0:T(8,128)(2,1)} %late3.1), channel_id=1, source_target_pairs={{4,8},{8,4},{5,9},{9,5},{6,10},{10,6},{7,11},{11,7},{20,24},{24,20... | collective-permute-start | bytes 3145736 | tf_op jit(solution)/shard_map/mid_late3/ppermute | solution.py:286
  448.6 28.0 %collective-permute-start.29 = (bf16[256,2048]{1,0:T(8,128)(2,1)}, bf16[256,2048]{1,0:T(8,128)(2,1)}, u32[]{:S(2)}, u32[]{:S(2)}) collective-permute-start(bf16[256,2048]{1,0:T(8,128)(2,1)} %one2.1.refs_4_), channel_id=1, source_target_pairs={{0,4},{12,8},{4,0},{8,12},{1,5},{13,9},{5,1},{9,13},{2,6},{14,10},... | collective-permute-start | bytes 3145736 | tf_op jit(solution)/shard_map/send12/ppermute | solution.py:292
  452.2 40.8 %collective-permute-start.31 = (bf16[256,2048]{1,0:T(8,128)(2,1)}, bf16[256,2048]{1,0:T(8,128)(2,1)}, u32[]{:S(2)}, u32[]{:S(2)}) collective-permute-start(bf16[256,2048]{1,0:T(8,128)(2,1)} %one3.1), channel_id=1, source_target_pairs={{0,4},{12,8},{4,0},{8,12},{1,5},{13,9},{5,1},{9,13},{2,6},{14,10},... | collective-permute-start | bytes 3145736 | tf_op jit(solution)/shard_map/send13/ppermute | solution.py:292
  (46 other events, 650.1 us)
Sparse Core Ops, SparseCore 0:
  9.6 25.2 all-gather.12
  75.4 22.1 all-gather.8
  104.3 24.4 reduce-scatter.1
  130.8 20.8 all-gather.10
  239.3 31.8 all-reduce.2
  272.6 22.5 all-gather.6

commit v3 on v2

--- a/solution.py
+++ b/solution.py
@@ -77,7 +77,7 @@
     return pl.pallas_call(
         kernel,
         compiler_params=pltpu.CompilerParams(vmem_limit_bytes=VMEM),
-        cost_estimate=pl.CostEstimate(flops=flops // 6, bytes_accessed=0, transcendentals=0),
+        cost_estimate=pl.CostEstimate(flops=10 * flops, bytes_accessed=0, transcendentals=0),
         **kwargs,
     )
 
@@ -173,7 +173,7 @@
 def backward(ids, grad_out, adapter_up):
     batch_rows, hidden = grad_out.shape
     tenants, rank_width, _ = adapter_up.shape
-    tile = tile_of(hidden)
+    tile = hidden // 4
     return call(
         backward_kernel,
         2 * batch_rows * hidden * rank_width * 4,
@@ -245,7 +245,7 @@
 
 def combine(weights, terms, dtype, scale=None, extras=()):
     rank_width, hidden = terms[0].shape[1:]
-    tile = tile_of(hidden)
+    tile = hidden // 4
     slots = weights.shape[0]
     if scale is None:
         scale = jnp.ones((slots,), jnp.float32)
@@ -327,7 +327,7 @@
 
     def late_use(value):
         held = Held(value)
-        tie(held, *work[-1:])
+        tie(held, *slot_gate, *work[-1:])
         return held.now
 
     def piece_of(name, rows, j, arrived=None):
@@ -368,8 +368,10 @@
     block_tenant = late_use(block_tenant)
 
     step0[1] = slot(firsts[1])
+    slot_gate[:] = chain[:1]
     firsts[2] = piece_of("first", rows_first, 2)
 
+    slot_gate[:] = chain[1:2]
     tenant_ids = jnp.arange(tenants, dtype=jnp.int32)
     order = jnp.stack([jnp.where(outer, z ^ 3, z), z ^ 2, z ^ 1, jnp.where(outer, z, z ^ 3)])
     blocks_of = block_tenant.reshape(dp_count, local_blocks)
@@ -378,7 +380,7 @@
     ids = ids.reshape(-1)
     own_ids = lax.dynamic_index_in_dim(blocks_of, z, 0, keepdims=False)
     with jax.named_scope("forward"):
-        parts = jnp.stack(forward(row_ids, [first_part, two, one, late_part], down_all, (firsts[2].now,)))
+        parts = jnp.stack(forward(late_use(row_ids), [first_part, two, one, late_part], down_all, ()))
         by_batch = jnp.where((order[None, :] == jnp.arange(dp_count)[:, None])[:, :, None, None], parts, 0.0)
         by_batch = do(jnp.sum(by_batch, axis=1)).now
         projected = lax.psum_scatter(by_batch, "dp", scatter_dimension=0, tiled=True)[0]
@@ -434,14 +436,14 @@
     last_hits = hits(slots_at(jnp.where(z == 2, 3, 0)), z)
     own_hits = jnp.concatenate([hits(own_slots, z), hits(own_slots, z - side)], axis=1) * own_scale[:, None]
 
-    add_one(0)
 
     step1[0] = slot(twos[0])
     pin(mid1[2])
-    add_one(1)
+    add_one(0)
     back_part = do(backward(late_use(own_ids), grad_out, adapter_up))
-    with jax.named_scope("back_mine"):
-        back_mine = (SCALE * lax.psum(back_part.now, "tensor")).astype(jnp.bfloat16)
+    with jax.named_scope("back_proj"):
+        back_full = jnp.where((jnp.arange(dp_count) == z)[:, None, None], back_part.now, 0.0)
+        back_full = lax.psum(back_full, ("dp", "tensor"))
 
     step1[1] = slot(twos[1])
 
@@ -449,50 +451,48 @@
         return [held.now[None] for held in (*up_terms, *moved_terms)]
 
     with jax.named_scope("far_terms"):
-        far_sums = do(combine(far_hits, terms(), jnp.bfloat16))
+        far_sums = do(combine(late_use(far_hits), terms(), jnp.bfloat16))
         far_terms = Held(middle_hop(far_sums.now))
     pin(mid1[3])
-    with jax.named_scope("backs"):
-        backs = lax.all_gather(late_use(back_mine), "dp", axis=0)
 
     step2[0] = slot(ones[0], first_and_last_hop)
     add_late(0)
-    add_one(2)
-
-    step2[1] = slot(ones[1], first_and_last_hop)
+    add_one(1)
+
+    step1[2] = slot(twos[2])
     add_late(1)
     pin(far_terms)
     with jax.named_scope("last_terms"):
-        last_sums = do(
-            combine(last_hits, terms()[:local_blocks], jnp.bfloat16, jnp.ones((OWN_MAX,), jnp.float32), [far_terms.now])
-        )
+        unit = jnp.ones((OWN_MAX,), jnp.float32)
+        last_sums = do(combine(late_use(last_hits), terms()[:local_blocks], jnp.bfloat16, unit, [far_terms.now]))
         last_terms = Held(last_hop(last_sums.now))
 
-    step1[2] = slot(twos[2])
+    step1[3] = slot(twos[3])
     with jax.named_scope("near_terms"):
-        near_sums = do(combine(near_hits, terms(), jnp.bfloat16))
+        near_sums = do(combine(late_use(near_hits), terms(), jnp.bfloat16))
         near_terms = Held(middle_hop(near_sums.now))
     pin(mid2[0])
+    add_one(2)
+
+    step2[1] = slot(ones[1], first_and_last_hop)
+    pin(mid2[1])
+    add_late(2)
     add_one(3)
 
-    step1[3] = slot(twos[3])
-    pin(mid2[1])
-    backs = late_use(backs)
+    step2[2] = slot(ones[2], first_and_last_hop)
+    pin(last_terms)
+    add_late(3)
+    backs = (SCALE * late_use(back_full)).astype(jnp.bfloat16)
     backs = [lax.dynamic_index_in_dim(backs, order[n], 0, keepdims=False) for n in range(dp_count)]
     grad_down = do(
         down_gradient(
             index, ids, inverse, [rows_first, rows_two, rows_one, rows_late], backs, adapter_down.shape
         )
     )
-    pin(last_terms)
-
-    step2[2] = slot(ones[2], first_and_last_hop)
-    add_late(2)
-    pin(near_terms)
 
     step2[3] = slot(ones[3], first_and_last_hop)
-    add_late(3)
-    grad_up = combine(own_hits, terms(), jnp.float32, own_scale, [near_terms.now, last_terms.now])
+    slot_gate[:] = chain[-2:-1]
+    grad_up = do(combine(late_use(own_hits), terms(), jnp.float32, own_scale, [near_terms.now, last_terms.now]))
     own_mask = jnp.broadcast_to(
         (late_use(own_ids)[:, None] == tenant_ids[None, :])[:, None, :, None],
         (local_blocks, ROWS_BLK, tenants, rank_width),
@@ -509,7 +509,7 @@
         total = total + mid2[j].now.astype(jnp.float32)
         total = total + step2[j].now.astype(jnp.float32)
         layer_out = lax.dynamic_update_slice(layer_out, total.astype(jnp.bfloat16), (0, start * tile))
-    return (layer_out, grad_down.now, grad_up)
+    return (layer_out, grad_down.now, grad_up.now)
 
 
 def local_plain(tokens, up_weight, adapter_down, adapter_up, grad_out, block_tenant, owner_of):

time: 506 us -> 396 us (0.78)
  waiting for transfers between devices: 116 us -> 80.4 us
  starting transfers between devices: 103 us -> 75.3 us
  blocking collectives: 31.8 us -> 6.16 us
  Pallas kernels: 196 us -> 175 us
    all_gather x1 -> x0, blocking collectives: 26.6 us -> none  [local(): backs = lax.all_gather(late_use(back_mine), 'dp', axis=0)]
    ppermute x4, starting transfers between devices: 24.8 us -> 7.07 us  [first_and_last_hop(): return lax.ppermute(value, 'dp', [(0, 1), (3, 2), (1, 0), (2, 3)])]
    pallas_call x4, Pallas kernels: 36.1 us -> 19.8 us  [combine(): call(functools.partial(combine_kernel, len(terms), len(extras)), 4 * slot...]
    psum x1, waiting for transfers between devices: 13.4 us -> 0.01 us  [local(): back_full = lax.psum(back_full, ('dp', 'tensor'))]
    ppermute x4, waiting for transfers between devices: 34.9 us -> 22.8 us  [first_and_last_hop(): return lax.ppermute(value, 'dp', [(0, 1), (3, 2), (1, 0), (2, 3)])]
    ppermute x10, waiting for transfers between devices: 18.2 us -> 6.8 us  [first_hop(): return lax.ppermute(value, 'dp', [(0, 1), (3, 2)])]
    ppermute x10, starting transfers between devices: 52.2 us -> 44.7 us  [first_hop(): return lax.ppermute(value, 'dp', [(0, 1), (3, 2)])]
    dynamic_update_slice x3 -> x2, other arithmetic: 9.22 us -> 2.54 us  [local(): lax.dynamic_update_slice(layer_out, total.astype(jnp.bfloat16), (0, start...]
  transfers between devices with their start and end apart: 38 -> 38, of which waited for: 12 -> 10; matrix products, arithmetic and copies ran while one was open for 6% -> 7% of each run, Pallas kernels for 37% -> 44%
where the time goes in v3:
time: 396 us; the launch traced here: 394 us
  Pallas kernels  175 us (44%)
  waiting for transfers between devices  80.4 us (20%)
  starting transfers between devices  75.3 us (19%)
  local copies, waits for them, and re-layouts  16.8 us (4%)
  other arithmetic  15.4 us (4%)
  between operations  14.8 us (4%)
  matrix products  10.2 us (3%)
  blocking collectives  6.16 us (2%)
    pallas_call x16, Pallas kernels, share(): call(functools.partial(share_kernel, masks, has_add, len(deps)), 2 * batc...  142 us
    ppermute x10, starting transfers between devices, first_hop(): return lax.ppermute(value, 'dp', [(0, 1), (3, 2)])  44.7 us
    ppermute x5, waiting for transfers between devices, across(): return lax.ppermute(value, axis, [(i, i ^ bit) for i in range(count)])  37.8 us
    ppermute x4, waiting for transfers between devices, first_and_last_hop(): return lax.ppermute(value, 'dp', [(0, 1), (3, 2), (1, 0), (2, 3)])  22.8 us
    pallas_call x4, Pallas kernels, combine(): call(functools.partial(combine_kernel, len(terms), len(extras)), 4 * slot...  19.8 us
    ppermute x11, starting transfers between devices, middle_hop(): return lax.ppermute(value, 'dp', [(1, 2), (2, 1)])  12.8 us
    ppermute x1, waiting for transfers between devices, local(): far = lax.ppermute(block_for(z ^ 3), 'dp', [(0, 3), (3, 0)])  12.3 us
    unnamed x78, local copies, waits for them, and re-layouts  9.54 us
  transfers between devices with their start and end apart: 38, of which 10 were waited for; matrix products, arithmetic and copies ran while one was open for 7% of the time, Pallas kernels for 44%

profile of v3, /device:TPU:0, one launch (start us, length us, event | category | flops | bytes accessed | tf_op | source)
XLA Modules:
  0.0 394.4 jit_solution(9153240408416570167)
XLA Ops:
  9.7 6.9 %collective-permute-start = (bf16[64,4096]{1,0:T(8,128)(2,1)S(1)}, bf16[64,4096]{1,0:T(8,128)(2,1)}, u32[]{:S(2)}, u32[]{:S(2)}) collective-permute-start(bf16[64,4096]{1,0:T(8,128)(2,1)S(1)} %get-tuple-element.85), channel_id=1, source_target_pairs={{0,12},{12,0},{1,13},{13,1},{2,14},{14,2},{3,15},{15,3},{16,28},{2... | collective-permute-start | bytes 1572872 | tf_op jit(solution)/shard_map/ppermute | solution.py:298
  17.3 12.3 %collective-permute-done = bf16[64,4096]{1,0:T(8,128)(2,1)} collective-permute-done((bf16[64,4096]{1,0:T(8,128)(2,1)S(1)}, bf16[64,4096]{1,0:T(8,128)(2,1)}, u32[]{:S(2)}, u32[]{:S(2)}) %collective-permute-start) | collective-permute-done | bytes 524320 | tf_op jit(solution)/shard_map/ppermute | solution.py:298
  29.6 21.5 %collective-permute-done.1.refs_1_ = bf16[64,4096]{1,0:T(8,128)(2,1)} collective-permute-done((bf16[64,4096]{1,0:T(8,128)(2,1)}, bf16[64,4096]{1,0:T(8,128)(2,1)}, u32[]{:S(2)}, u32[]{:S(2)}) %collective-permute-start.1) | collective-permute-done | bytes 524320 | tf_op jit(solution)/shard_map/ppermute | solution.py:37
  54.1 15.9 %collective-permute-done.4.refs_1_.refs_5_ = bf16[64,4096]{1,0:T(8,128)(2,1)} collective-permute-done((bf16[64,4096]{1,0:T(8,128)(2,1)S(1)}, bf16[64,4096]{1,0:T(8,128)(2,1)}, u32[]{:S(2)}, u32[]{:S(2)}) %collective-permute-start.4) | collective-permute-done | bytes 524320 | tf_op jit(solution)/shard_map/ppermute | solution.py:37
  72.9 6.2 %first0.1.refs_5_ = bf16[256,1024]{1,0:T(8,128)(2,1)} custom-call(s32[1]{0:T(128)} %bitcast.index, bf16[64,4096]{1,0:T(8,128)(2,1)} %copy-done.13, bf16[64,4096]{1,0:T(8,128)(2,1)} %collective-permute-done.4.refs_1_.refs_5_, bf16[64,4096]{1,0:T(8,128)(2,1)} %copy-done.32, bf16[64,4096]{1,0:T(8,128)(2,1)} %copy-done.33, bf16[4096,6656]{1,0:T(8,128)(2,1)} %refs_1_.23), custom_call_target="tpu_custom_call" | custom-call | flops 21474836480 | tf_op jit(solution)/shard_map/first0/pallas_call | solution.py:116
  81.4 8.6 %first1.1.refs_6_ = bf16[256,1536]{1,0:T(8,128)(2,1)} custom-call(s32[1]{0:T(128)} %bitcast.index, bf16[64,4096]{1,0:T(8,128)(2,1)} %copy-done.13, bf16[64,4096]{1,0:T(8,128)(2,1)} %collective-permute-done.4.refs_1_.refs_5_, bf16[64,4096]{1,0:T(8,128)(2,1)} %copy-done.32, bf16[64,4096]{1,0:T(8,128)(2,1)} %copy-done.33, bf16[4096,6656]{1,0:T(8,128)(2,1)} %refs_1_.23, ...), custom_call_target="tpu_custom_call" | custom-call | flops 32212254720 | tf_op jit(solution)/shard_map/first1/pallas_call | solution.py:116
  95.4 10.7 %first2.1 = bf16[256,2048]{1,0:T(8,128)(2,1)} custom-call(s32[1]{0:T(128)} %bitcast.index, bf16[64,4096]{1,0:T(8,128)(2,1)} %copy-done.13, bf16[64,4096]{1,0:T(8,128)(2,1)} %collective-permute-done.4.refs_1_.refs_5_, bf16[64,4096]{1,0:T(8,128)(2,1)} %copy-done.32, bf16[64,4096]{1,0:T(8,128)(2,1)} %copy-done.33, bf16[4096,6656]{1,0:T(8,128)(2,1)} %refs_1_.23, ...), custom_call_target="tpu_custom_call" | custom-call | flops 42949672960 | tf_op jit(solution)/shard_map/first2/pallas_call | solution.py:116
  119.8 5.4 %collective-permute-start.11 = (bf16[256,2048]{1,0:T(8,128)(2,1)S(1)}, bf16[256,2048]{1,0:T(8,128)(2,1)}, u32[]{:S(2)}, u32[]{:S(2)}) collective-permute-start(bf16[256,2048]{1,0:T(8,128)(2,1)S(1)} %copy-done.7), channel_id=1, source_target_pairs={{0,4},{12,8},{1,5},{13,9},{2,6},{14,10},{3,7},{15,11},{16,20},{28,... | collective-permute-start | bytes 3145736 | tf_op jit(solution)/shard_map/send2/ppermute | solution.py:283
  125.2 10.2 %first3.1.refs_4_ = bf16[256,2048]{1,0:T(8,128)(2,1)} custom-call(s32[1]{0:T(128)} %bitcast.index, bf16[64,4096]{1,0:T(8,128)(2,1)} %copy-done.13, bf16[64,4096]{1,0:T(8,128)(2,1)} %collective-permute-done.4.refs_1_.refs_5_, bf16[64,4096]{1,0:T(8,128)(2,1)} %copy-done.32, bf16[64,4096]{1,0:T(8,128)(2,1)} %copy-done.33, bf16[4096,6656]{1,0:T(8,128)(2,1)} %refs_1_.23, ...), custom_call_target="tpu_custom_call" | custom-call | flops 42949672960 | tf_op jit(solution)/shard_map/first3/pallas_call | solution.py:116
  137.7 6.2 %two0.1.refs_4_ = bf16[256,1024]{1,0:T(8,128)(2,1)} custom-call(s32[1]{0:T(128)} %bitcast.index, bf16[256,4096]{1,0:T(8,128)(2,1)} %all-gather.6.cloned.1.call-done.refs_0_.refs_8_, bf16[4096,6656]{1,0:T(8,128)(2,1)} %refs_1_.23, bf16[256,1024]{1,0:T(8,128)(2,1)} %collective-permute-done.8.refs_5_.refs_2_.refs_3_, ...), custom_call_target="tpu_custom_call" | custom-call | flops 21474836480 | tf_op jit(solution)/shard_map/two0/pallas_call | solution.py:116
  144.6 8.9 %two1.1 = bf16[256,1536]{1,0:T(8,128)(2,1)} custom-call(s32[1]{0:T(128)} %bitcast.index, bf16[256,4096]{1,0:T(8,128)(2,1)} %all-gather.6.cloned.1.call-done.refs_0_.refs_8_, bf16[4096,6656]{1,0:T(8,128)(2,1)} %refs_1_.23, bf16[256,1536]{1,0:T(8,128)(2,1)} %collective-permute-done.7.refs_2_.refs_3_, bf16[256,1536]{1,0:T(8,128)(2,1)} %collective-permute-done.7.refs_2_.refs_3_, ...), custom_call_target="tpu_custom_call" | custom-call | flops 32212254720 | tf_op jit(solution)/shard_map/two1/pallas_call | solution.py:116
  155.0 6.2 %all_gather.21 = bf16[256,64]{1,0:T(8,128)(2,1)S(1)} all-gather(bf16[64,64]{1,0:T(8,128)(2,1)S(1)} %convert_element_type.76), channel_id=1, replica_groups=mesh['groups'=2,'dp'=4,'tensor'=4] {'tensor'}, dimensions={0}, use_global_device_ids=true | all-gather | bytes 40960 | tf_op jit(solution)/shard_map/projected/all_gather | solution.py:395
  169.5 10.4 %two2.1.refs_4_ = bf16[256,2048]{1,0:T(8,128)(2,1)} custom-call(s32[1]{0:T(128)} %bitcast.index, bf16[256,4096]{1,0:T(8,128)(2,1)} %all-gather.6.cloned.1.call-done.refs_0_.refs_8_, bf16[4096,6656]{1,0:T(8,128)(2,1)} %refs_1_.23, bf16[256,2048]{1,0:T(8,128)(2,1)} %collective-permute-done.11.refs_2_.refs_3_, ...), custom_call_target="tpu_custom_call" | custom-call | flops 42949672960 | tf_op jit(solution)/shard_map/two2/pallas_call | solution.py:116
  182.4 10.5 %two3.1.refs_4_ = bf16[256,2048]{1,0:T(8,128)(2,1)} custom-call(s32[1]{0:T(128)} %bitcast.index, bf16[256,4096]{1,0:T(8,128)(2,1)} %all-gather.6.cloned.1.call-done.refs_0_.refs_8_, bf16[4096,6656]{1,0:T(8,128)(2,1)} %refs_1_.23, bf16[256,2048]{1,0:T(8,128)(2,1)} %collective-permute-done.9.refs_2_.refs_3_, ...), custom_call_target="tpu_custom_call" | custom-call | flops 42949672960 | tf_op jit(solution)/shard_map/two3/pallas_call | solution.py:116
  195.0 4.5 %collective-permute-start.12 = (bf16[64,6656]{1,0:T(8,128)(2,1)S(1)}, bf16[64,6656]{1,0:T(8,128)(2,1)S(1)}, u32[]{:S(2)}, u32[]{:S(2)}) collective-permute-start(bf16[64,6656]{1,0:T(8,128)(2,1)S(1)} %copy-done.1), channel_id=1, source_target_pairs={{0,4},{12,8},{1,5},{13,9},{2,6},{14,10},{3,7},{15,11},{16,20},{28,... | collective-permute-start | bytes 2555912 | tf_op jit(solution)/shard_map/send5/ppermute | solution.py:283
  203.2 6.2 %one0.1 = bf16[256,1024]{1,0:T(8,128)(2,1)} custom-call(s32[1]{0:T(128)} %bitcast.index, bf16[256,4096]{1,0:T(8,128)(2,1)} %all-gather.8.cloned.1.call-done.refs_0_.refs_9_, bf16[4096,6656]{1,0:T(8,128)(2,1)} %refs_1_.23, bf16[256,1024]{1,0:T(8,128)(2,1)} %copy-done.36, bf16[64,6656]{1,0:T(8,128)(2,1)} %copy-done.2, bf16[256,2048]{1,0:T(8,128)(2,1)} %two3.1.refs_4_), custom_call_target="tpu_custom_call" | custom-call | flops 21474836480 | tf_op jit(solution)/shard_map/one0/pallas_call | solution.py:116
  211.6 5.6 %shard_map.94 = f32[256,64]{1,0:T(8,128)} custom-call(s32[2]{0:T(128)} %fusion.31.ids, bf16[256,6656]{1,0:T(8,128)(2,1)} %grad.1, bf16[4,64,6656]{2,1,0:T(8,128)(2,1)} %up.1), custom_call_target="tpu_custom_call" | custom-call | flops 8724152320 | tf_op jit(solution)/shard_map/pallas_call | solution.py:177
  223.5 4.6 %far_terms.1.refs_4_ = bf16[2,64,6656]{2,1,0:T(8,128)(2,1)} custom-call(f32[2,4]{1,0:T(2,128)} %add_convert_fusion.5.weights, f32[2]{0:T(128)} %broadcast_16_scale.2.scale, bf16[1,64,6656]{2,1,0:T(8,128)(2,1)} %bitcast.50, bf16[1,64,6656]{2,1,0:T(8,128)(2,1)} %bitcast.54, bf16[1,64,6656]{2,1,0:T(8,128)(2,1)} %bitcast.58, bf16[1,64,6656]{2,1,0:T(8,128)(2,1)} %bitcast.61), custom_call_target="tpu_custom_call" | custom-call | flops 136314880 | tf_op jit(solution)/shard_map/far_terms/pallas_call | solution.py:252
  233.2 6.2 %late0.1.refs_4_ = bf16[256,1024]{1,0:T(8,128)(2,1)} custom-call(s32[1]{0:T(128)} %bitcast.index, bf16[256,4096]{1,0:T(8,128)(2,1)} %all-gather.10.cloned.1.call-done.refs_0_.refs_10_, bf16[4096,6656]{1,0:T(8,128)(2,1)} %refs_1_.23, bf16[256,1024]{1,0:T(8,128)(2,1)} %collective-permute-done.16.refs_2_.refs_3_, ...), custom_call_target="tpu_custom_call" | custom-call | flops 21474836480 | tf_op jit(solution)/shard_map/late0/pallas_call | solution.py:116
  240.1 8.7 %one1.1.refs_4_ = bf16[256,1536]{1,0:T(8,128)(2,1)} custom-call(s32[1]{0:T(128)} %bitcast.index, bf16[256,4096]{1,0:T(8,128)(2,1)} %all-gather.8.cloned.1.call-done.refs_0_.refs_9_, bf16[4096,6656]{1,0:T(8,128)(2,1)} %refs_1_.23, bf16[256,1536]{1,0:T(8,128)(2,1)} %collective-permute-done.15.refs_2_, ...), custom_call_target="tpu_custom_call" | custom-call | flops 32212254720 | tf_op jit(solution)/shard_map/one1/pallas_call | solution.py:116
  251.0 8.7 %late1.1 = bf16[256,1536]{1,0:T(8,128)(2,1)} custom-call(s32[1]{0:T(128)} %bitcast.index, bf16[256,4096]{1,0:T(8,128)(2,1)} %all-gather.10.cloned.1.call-done.refs_0_.refs_10_, bf16[4096,6656]{1,0:T(8,128)(2,1)} %refs_1_.23, bf16[256,1536]{1,0:T(8,128)(2,1)} %copy-done.30, bf16[256,1536]{1,0:T(8,128)(2,1)} %copy-done.30, bf16[256,1536]{1,0:T(8,128)(2,1)} %one1.1.refs_4_), custom_call_target="tpu_custom_call" | custom-call | flops 32212254720 | tf_op jit(solution)/shard_map/late1/pallas_call | solution.py:116
  260.4 8.4 %collective-permute-start.24 = (bf16[256,2048]{1,0:T(8,128)(2,1)}, bf16[256,2048]{1,0:T(8,128)(2,1)}, u32[]{:S(2)}, u32[]{:S(2)}) collective-permute-start(bf16[256,2048]{1,0:T(8,128)(2,1)} %two2.1.refs_4_), channel_id=1, source_target_pairs={{0,4},{12,8},{1,5},{13,9},{2,6},{14,10},{3,7},{15,11},{16,20},{28,... | collective-permute-start | bytes 3145736 | tf_op jit(solution)/shard_map/send9/ppermute | solution.py:283
  270.0 4.5 %last_terms.1 = bf16[2,64,6656]{2,1,0:T(8,128)(2,1)} custom-call(f32[2,2]{1,0:T(2,128)} %get-tuple-element.138.weights, f32[2]{0:T(128)} %broadcast_16_scale.2.scale, bf16[1,64,6656]{2,1,0:T(8,128)(2,1)} %bitcast.51, bf16[1,64,6656]{2,1,0:T(8,128)(2,1)} %bitcast.55, bf16[2,64,6656]{2,1,0:T(8,128)(2,1)} %copy-done.6), custom_call_target="tpu_custom_call" | custom-call | flops 68157440 | tf_op jit(solution)/shard_map/last_terms/pallas_call | solution.py:252
  275.7 4.7 %near_terms.1.refs_4_ = bf16[2,64,6656]{2,1,0:T(8,128)(2,1)} custom-call(f32[2,4]{1,0:T(2,128)} %add_convert_fusion.4.weights, f32[2]{0:T(128)} %broadcast_16_scale.2.scale, bf16[1,64,6656]{2,1,0:T(8,128)(2,1)} %bitcast.52, bf16[1,64,6656]{2,1,0:T(8,128)(2,1)} %bitcast.56, bf16[1,64,6656]{2,1,0:T(8,128)(2,1)} %bitcast.59, bf16[1,64,6656]{2,1,0:T(8,128)(2,1)} %bitcast.62), custom_call_target="tpu_custom_call" | custom-call | flops 136314880 | tf_op jit(solution)/shard_map/near_terms/pallas_call | solution.py:252
  282.4 10.3 %one2.1.refs_4_ = bf16[256,2048]{1,0:T(8,128)(2,1)} custom-call(s32[1]{0:T(128)} %bitcast.index, bf16[256,4096]{1,0:T(8,128)(2,1)} %all-gather.8.cloned.1.call-done.refs_0_.refs_9_, bf16[4096,6656]{1,0:T(8,128)(2,1)} %refs_1_.23, bf16[256,2048]{1,0:T(8,128)(2,1)} %collective-permute-done.13.refs_2_, bf16[256,1024]{1,0:T(8,128)(2,1)} %collective-permute-done.18.refs_3_, ...), custom_call_target="tpu_custom_call" | custom-call | flops 42949672960 | tf_op jit(solution)/shard_map/one2/pallas_call | solution.py:116
  292.7 10.3 %collective-permute-start.21 = (bf16[256,2048]{1,0:T(8,128)(2,1)S(1)}, bf16[256,2048]{1,0:T(8,128)(2,1)}, u32[]{:S(2)}, u32[]{:S(2)}) collective-permute-start(bf16[256,2048]{1,0:T(8,128)(2,1)S(1)} %copy-done.27), channel_id=1, source_target_pairs={{0,4},{12,8},{1,5},{13,9},{2,6},{14,10},{3,7},{15,11},{16,20},{28,... | collective-permute-start | bytes 3145736 | tf_op jit(solution)/shard_map/send10/ppermute | solution.py:283
  302.9 10.2 %late2.1.refs_4_ = bf16[256,2048]{1,0:T(8,128)(2,1)} custom-call(s32[1]{0:T(128)} %bitcast.index, bf16[256,4096]{1,0:T(8,128)(2,1)} %all-gather.10.cloned.1.call-done.refs_0_.refs_10_, bf16[4096,6656]{1,0:T(8,128)(2,1)} %refs_1_.23, bf16[256,2048]{1,0:T(8,128)(2,1)} %collective-permute-done.24.refs_2_.refs_3_, ...), custom_call_target="tpu_custom_call" | custom-call | flops 42949672960 | tf_op jit(solution)/shard_map/late2/pallas_call | solution.py:116
  313.9 10.2 %one3.1.refs_4_ = bf16[256,2048]{1,0:T(8,128)(2,1)} custom-call(s32[1]{0:T(128)} %bitcast.index, bf16[256,4096]{1,0:T(8,128)(2,1)} %all-gather.8.cloned.1.call-done.refs_0_.refs_9_, bf16[4096,6656]{1,0:T(8,128)(2,1)} %refs_1_.23, bf16[256,2048]{1,0:T(8,128)(2,1)} %collective-permute-done.17.refs_2_, ...), custom_call_target="tpu_custom_call" | custom-call | flops 42949672960 | tf_op jit(solution)/shard_map/one3/pallas_call | solution.py:116
  326.5 10.2 %late3.1 = bf16[256,2048]{1,0:T(8,128)(2,1)} custom-call(s32[1]{0:T(128)} %bitcast.index, bf16[256,4096]{1,0:T(8,128)(2,1)} %all-gather.10.cloned.1.call-done.refs_0_.refs_10_, bf16[4096,6656]{1,0:T(8,128)(2,1)} %refs_1_.23, bf16[256,2048]{1,0:T(8,128)(2,1)} %collective-permute-done.21.refs_2_.refs_3_, ...), custom_call_target="tpu_custom_call" | custom-call | flops 42949672960 | tf_op jit(solution)/shard_map/late3/pallas_call | solution.py:116
  338.5 3.9 shard_map.95
  348.8 18.5 %collective-permute-done.23 = bf16[256,2048]{1,0:T(8,128)(2,1)S(1)} collective-permute-done((bf16[256,2048]{1,0:T(8,128)(2,1)}, bf16[256,2048]{1,0:T(8,128)(2,1)S(1)}, u32[]{:S(2)}, u32[]{:S(2)}) %collective-permute-start.23) | collective-permute-done | bytes 1048608 | tf_op jit(solution)/shard_map/send12/ppermute | solution.py:292
  367.3 6.0 %shard_map.96 = f32[2,64,6656]{2,1,0:T(8,128)} custom-call(f32[2,4]{1,0:T(2,128)} %add_select_fusion.weights, f32[2]{0:T(128)} %copy-done.17, bf16[1,64,6656]{2,1,0:T(8,128)(2,1)} %bitcast.53, bf16[1,64,6656]{2,1,0:T(8,128)(2,1)} %bitcast.57, bf16[1,64,6656]{2,1,0:T(8,128)(2,1)} %bitcast.60, bf16[1,64,6656]{2,1,0:T(8,128)(2,1)} %bitcast.63, ...), custom_call_target="tpu_custom_call" | custom-call | flops 136314880 | tf_op jit(solution)/shard_map/pallas_call | solution.py:252
  (200 shorter events, 98.0 us)
Async XLA Ops:
  7.2 102.7 %all-gather.12.cloned.1.call-start = ((), (), s32[]{:S(2)}) async-start(), calls=%async_computation.6 | async-start | bytes 2621440 | tf_op jit(solution)/shard_map/all_gather | solution.py:297
  9.7 19.9 %collective-permute-start = (bf16[64,4096]{1,0:T(8,128)(2,1)S(1)}, bf16[64,4096]{1,0:T(8,128)(2,1)}, u32[]{:S(2)}, u32[]{:S(2)}) collective-permute-start(bf16[64,4096]{1,0:T(8,128)(2,1)S(1)} %get-tuple-element.85), channel_id=1, source_target_pairs={{0,12},{12,0},{1,13},{13,1},{2,14},{14,2},{3,15},{15,3},{16,28},{2... | collective-permute-start | bytes 1572872 | tf_op jit(solution)/shard_map/ppermute | solution.py:298
  16.6 34.5 %collective-permute-start.1 = (bf16[64,4096]{1,0:T(8,128)(2,1)}, bf16[64,4096]{1,0:T(8,128)(2,1)}, u32[]{:S(2)}, u32[]{:S(2)}) collective-permute-start(bf16[64,4096]{1,0:T(8,128)(2,1)} %get-tuple-element.168), channel_id=1, source_target_pairs={{0,8},{4,12},{8,0},{12,4},{1,9},{5,13},{9,1},{13,5},{2,10},{6,14},... | collective-permute-start | bytes 1572872 | tf_op jit(solution)/shard_map/ppermute | solution.py:37
  16.7 34.4 %collective-permute-start.2 = (bf16[64,4096]{1,0:T(8,128)(2,1)S(1)}, bf16[64,4096]{1,0:T(8,128)(2,1)}, u32[]{:S(2)}, u32[]{:S(2)}) collective-permute-start(bf16[64,4096]{1,0:T(8,128)(2,1)S(1)} %get-tuple-element.167), channel_id=1, source_target_pairs={{0,4},{4,0},{8,12},{12,8},{1,5},{5,1},{9,13},{13,9},{2,6},{6,2},{1... | collective-permute-start | bytes 1572872 | tf_op jit(solution)/shard_map/ppermute | solution.py:37
  53.9 83.8 %all-gather.6.cloned.1.call-start = ((), (), s32[]{:S(2)}) async-start(), calls=%async_computation.2 | async-start | bytes 2621440 | tf_op jit(solution)/shard_map/two_rows/all_gather | solution.py:295
  94.4 50.1 %reduce-scatter.2.cloned.1.call-start = ((), (), s32[]{:S(2)}) async-start(), calls=%async_computation.1 | async-start | bytes 163840 | tf_op jit(solution)/shard_map/forward/reduce_scatter | solution.py:386
  115.1 87.2 %all-gather.8.cloned.1.call-start = ((), (), s32[]{:S(2)}) async-start(), calls=%async_computation.3 | async-start | bytes 2621440 | tf_op jit(solution)/shard_map/one_rows/all_gather | solution.py:295
  115.7 117.5 %all-gather.10.cloned.1.call-start = ((), (), s32[]{:S(2)}) async-start(), calls=%async_computation.4 | async-start | bytes 2621440 | tf_op jit(solution)/shard_map/late_rows/all_gather | solution.py:295
  119.2 217.5 %all-reduce.3.cloned.1.call-start = ((), (), s32[]{:S(2)}) async-start(), calls=%async_computation.5 | async-start | bytes 1048576 | tf_op jit(solution)/shard_map/back_proj/psum | solution.py:446
  119.8 46.4 %collective-permute-start.11 = (bf16[256,2048]{1,0:T(8,128)(2,1)S(1)}, bf16[256,2048]{1,0:T(8,128)(2,1)}, u32[]{:S(2)}, u32[]{:S(2)}) collective-permute-start(bf16[256,2048]{1,0:T(8,128)(2,1)S(1)} %copy-done.7), channel_id=1, source_target_pairs={{0,4},{12,8},{1,5},{13,9},{2,6},{14,10},{3,7},{15,11},{16,20},{28,... | collective-permute-start | bytes 3145736 | tf_op jit(solution)/shard_map/send2/ppermute | solution.py:283
  135.4 47.0 %collective-permute-start.9 = (bf16[256,2048]{1,0:T(8,128)(2,1)}, bf16[256,2048]{1,0:T(8,128)(2,1)}, u32[]{:S(2)}, u32[]{:S(2)}) collective-permute-start(bf16[256,2048]{1,0:T(8,128)(2,1)} %first3.1.refs_4_), channel_id=1, source_target_pairs={{0,4},{12,8},{1,5},{13,9},{2,6},{14,10},{3,7},{15,11},{16,20},{28,... | collective-permute-start | bytes 3145736 | tf_op jit(solution)/shard_map/send3/ppermute | solution.py:283
  143.9 38.5 %collective-permute-start.10 = (bf16[256,1024]{1,0:T(8,128)(2,1)}, bf16[256,1024]{1,0:T(8,128)(2,1)S(1)}, u32[]{:S(2)}, u32[]{:S(2)}) collective-permute-start(bf16[256,1024]{1,0:T(8,128)(2,1)} %two0.1.refs_4_), channel_id=1, source_target_pairs={{4,8},{8,4},{5,9},{9,5},{6,10},{10,6},{7,11},{11,7},{20,24},{24,20... | collective-permute-start | bytes 1572872 | tf_op jit(solution)/shard_map/mid_two0/ppermute | solution.py:286
  153.5 48.8 %collective-permute-start.15 = (bf16[256,1536]{1,0:T(8,128)(2,1)}, bf16[256,1536]{1,0:T(8,128)(2,1)}, u32[]{:S(2)}, u32[]{:S(2)}) collective-permute-start(bf16[256,1536]{1,0:T(8,128)(2,1)} %two1.1), channel_id=1, source_target_pairs={{4,8},{8,4},{5,9},{9,5},{6,10},{10,6},{7,11},{11,7},{20,24},{24,20... | collective-permute-start | bytes 2359304 | tf_op jit(solution)/shard_map/mid_two1/ppermute | solution.py:286
  166.2 36.1 %collective-permute-start.14 = (bf16[64,6656]{1,0:T(8,128)(2,1)S(1)}, bf16[64,6656]{1,0:T(8,128)(2,1)S(1)}, u32[]{:S(2)}, u32[]{:S(2)}) collective-permute-start(bf16[64,6656]{1,0:T(8,128)(2,1)S(1)} %fusion.1), channel_id=1, source_target_pairs={{0,4},{12,8},{1,5},{13,9},{2,6},{14,10},{3,7},{15,11},{16,20},{28,... | collective-permute-start | bytes 2555912 | tf_op jit(solution)/shard_map/send4/ppermute | solution.py:283
  179.9 39.1 %collective-permute-start.13 = (bf16[256,2048]{1,0:T(8,128)(2,1)}, bf16[256,2048]{1,0:T(8,128)(2,1)}, u32[]{:S(2)}, u32[]{:S(2)}) collective-permute-start(bf16[256,2048]{1,0:T(8,128)(2,1)} %two2.1.refs_4_), channel_id=1, source_target_pairs={{4,8},{8,4},{5,9},{9,5},{6,10},{10,6},{7,11},{11,7},{20,24},{24,20... | collective-permute-start | bytes 3145736 | tf_op jit(solution)/shard_map/mid_two2/ppermute | solution.py:286
  192.9 37.8 %collective-permute-start.17 = (bf16[256,2048]{1,0:T(8,128)(2,1)}, bf16[256,2048]{1,0:T(8,128)(2,1)}, u32[]{:S(2)}, u32[]{:S(2)}) collective-permute-start(bf16[256,2048]{1,0:T(8,128)(2,1)} %two3.1.refs_4_), channel_id=1, source_target_pairs={{4,8},{8,4},{5,9},{9,5},{6,10},{10,6},{7,11},{11,7},{20,24},{24,20... | collective-permute-start | bytes 3145736 | tf_op jit(solution)/shard_map/mid_two3/ppermute | solution.py:286
  195.0 24.1 %collective-permute-start.12 = (bf16[64,6656]{1,0:T(8,128)(2,1)S(1)}, bf16[64,6656]{1,0:T(8,128)(2,1)S(1)}, u32[]{:S(2)}, u32[]{:S(2)}) collective-permute-start(bf16[64,6656]{1,0:T(8,128)(2,1)S(1)} %copy-done.1), channel_id=1, source_target_pairs={{0,4},{12,8},{1,5},{13,9},{2,6},{14,10},{3,7},{15,11},{16,20},{28,... | collective-permute-start | bytes 2555912 | tf_op jit(solution)/shard_map/send5/ppermute | solution.py:283
  209.4 21.3 %collective-permute-start.16 = (bf16[256,1024]{1,0:T(8,128)(2,1)}, bf16[256,1024]{1,0:T(8,128)(2,1)}, u32[]{:S(2)}, u32[]{:S(2)}) collective-permute-start(bf16[256,1024]{1,0:T(8,128)(2,1)} %two0.1.refs_4_), channel_id=1, source_target_pairs={{0,4},{12,8},{1,5},{13,9},{2,6},{14,10},{3,7},{15,11},{16,20},{28,... | collective-permute-start | bytes 1572872 | tf_op jit(solution)/shard_map/send6/ppermute | solution.py:283
  219.1 31.0 %collective-permute-start.20 = (bf16[256,1536]{1,0:T(8,128)(2,1)S(1)}, bf16[256,1536]{1,0:T(8,128)(2,1)S(1)}, u32[]{:S(2)}, u32[]{:S(2)}) collective-permute-start(bf16[256,1536]{1,0:T(8,128)(2,1)S(1)} %copy-done.29), channel_id=1, source_target_pairs={{0,4},{12,8},{1,5},{13,9},{2,6},{14,10},{3,7},{15,11},{16,20},{28,... | collective-permute-start | bytes 2359304 | tf_op jit(solution)/shard_map/send7/ppermute | solution.py:283
  228.2 40.6 %collective-permute-start.19 = (bf16[2,64,6656]{2,1,0:T(8,128)(2,1)}, bf16[2,64,6656]{2,1,0:T(8,128)(2,1)S(1)}, u32[]{:S(2)}, u32[]{:S(2)}) collective-permute-start(bf16[2,64,6656]{2,1,0:T(8,128)(2,1)} %far_terms.1.refs_4_), channel_id=1, source_target_pairs={{4,8},{8,4},{5,9},{9,5},{6,10},{10,6},{7,11},{11,7},{20,24},{24,20... | collective-permute-start | bytes 5111816 | tf_op jit(solution)/shard_map/far_terms/ppermute | solution.py:286
  230.7 38.1 %collective-permute-start.18 = (bf16[256,1024]{1,0:T(8,128)(2,1)}, bf16[256,1024]{1,0:T(8,128)(2,1)}, u32[]{:S(2)}, u32[]{:S(2)}) collective-permute-start(bf16[256,1024]{1,0:T(8,128)(2,1)} %one0.1), channel_id=1, source_target_pairs={{0,4},{12,8},{4,0},{8,12},{1,5},{13,9},{5,1},{9,13},{2,6},{14,10},... | collective-permute-start | bytes 1572872 | tf_op jit(solution)/shard_map/send8/ppermute | solution.py:292
  239.4 53.3 %collective-permute-start.25 = (bf16[256,1024]{1,0:T(8,128)(2,1)}, bf16[256,1024]{1,0:T(8,128)(2,1)S(1)}, u32[]{:S(2)}, u32[]{:S(2)}) collective-permute-start(bf16[256,1024]{1,0:T(8,128)(2,1)} %late0.1.refs_4_), channel_id=1, source_target_pairs={{4,8},{8,4},{5,9},{9,5},{6,10},{10,6},{7,11},{11,7},{20,24},{24,20... | collective-permute-start | bytes 1572872 | tf_op jit(solution)/shard_map/mid_late0/ppermute | solution.py:286
  259.7 64.4 %collective-permute-start.22 = (bf16[256,1536]{1,0:T(8,128)(2,1)}, bf16[256,1536]{1,0:T(8,128)(2,1)S(1)}, u32[]{:S(2)}, u32[]{:S(2)}) collective-permute-start(bf16[256,1536]{1,0:T(8,128)(2,1)} %late1.1), channel_id=1, source_target_pairs={{4,8},{8,4},{5,9},{9,5},{6,10},{10,6},{7,11},{11,7},{20,24},{24,20... | collective-permute-start | bytes 2359304 | tf_op jit(solution)/shard_map/mid_late1/ppermute | solution.py:286
  260.4 42.5 %collective-permute-start.24 = (bf16[256,2048]{1,0:T(8,128)(2,1)}, bf16[256,2048]{1,0:T(8,128)(2,1)}, u32[]{:S(2)}, u32[]{:S(2)}) collective-permute-start(bf16[256,2048]{1,0:T(8,128)(2,1)} %two2.1.refs_4_), channel_id=1, source_target_pairs={{0,4},{12,8},{1,5},{13,9},{2,6},{14,10},{3,7},{15,11},{16,20},{28,... | collective-permute-start | bytes 3145736 | tf_op jit(solution)/shard_map/send9/ppermute | solution.py:283
  274.4 72.1 %collective-permute-start.28 = (bf16[2,64,6656]{2,1,0:T(8,128)(2,1)}, bf16[2,64,6656]{2,1,0:T(8,128)(2,1)}, u32[]{:S(2)}, u32[]{:S(2)}) collective-permute-start(bf16[2,64,6656]{2,1,0:T(8,128)(2,1)} %last_terms.1), channel_id=1, source_target_pairs={{4,0},{8,12},{5,1},{9,13},{6,2},{10,14},{7,3},{11,15},{20,16},{24,... | collective-permute-start | bytes 5111816 | tf_op jit(solution)/shard_map/last_terms/ppermute | solution.py:289
  280.4 86.9 %collective-permute-start.26 = (bf16[2,64,6656]{2,1,0:T(8,128)(2,1)}, bf16[2,64,6656]{2,1,0:T(8,128)(2,1)}, u32[]{:S(2)}, u32[]{:S(2)}) collective-permute-start(bf16[2,64,6656]{2,1,0:T(8,128)(2,1)} %near_terms.1.refs_4_), channel_id=1, source_target_pairs={{4,8},{8,4},{5,9},{9,5},{6,10},{10,6},{7,11},{11,7},{20,24},{24,20... | collective-permute-start | bytes 5111816 | tf_op jit(solution)/shard_map/near_terms/ppermute | solution.py:286
  292.7 31.8 %collective-permute-start.21 = (bf16[256,2048]{1,0:T(8,128)(2,1)S(1)}, bf16[256,2048]{1,0:T(8,128)(2,1)}, u32[]{:S(2)}, u32[]{:S(2)}) collective-permute-start(bf16[256,2048]{1,0:T(8,128)(2,1)S(1)} %copy-done.27), channel_id=1, source_target_pairs={{0,4},{12,8},{1,5},{13,9},{2,6},{14,10},{3,7},{15,11},{16,20},{28,... | collective-permute-start | bytes 3145736 | tf_op jit(solution)/shard_map/send10/ppermute | solution.py:283
  313.2 66.6 %collective-permute-start.29 = (bf16[256,2048]{1,0:T(8,128)(2,1)}, bf16[256,2048]{1,0:T(8,128)(2,1)S(1)}, u32[]{:S(2)}, u32[]{:S(2)}) collective-permute-start(bf16[256,2048]{1,0:T(8,128)(2,1)} %late2.1.refs_4_), channel_id=1, source_target_pairs={{4,8},{8,4},{5,9},{9,5},{6,10},{10,6},{7,11},{11,7},{20,24},{24,20... | collective-permute-start | bytes 3145736 | tf_op jit(solution)/shard_map/mid_late2/ppermute | solution.py:286
  324.1 20.8 %collective-permute-start.27 = (bf16[256,1536]{1,0:T(8,128)(2,1)}, bf16[256,1536]{1,0:T(8,128)(2,1)}, u32[]{:S(2)}, u32[]{:S(2)}) collective-permute-start(bf16[256,1536]{1,0:T(8,128)(2,1)} %one1.1.refs_4_), channel_id=1, source_target_pairs={{0,4},{12,8},{4,0},{8,12},{1,5},{13,9},{5,1},{9,13},{2,6},{14,10},... | collective-permute-start | bytes 2359304 | tf_op jit(solution)/shard_map/send11/ppermute | solution.py:292
  324.5 42.8 %collective-permute-start.23 = (bf16[256,2048]{1,0:T(8,128)(2,1)}, bf16[256,2048]{1,0:T(8,128)(2,1)S(1)}, u32[]{:S(2)}, u32[]{:S(2)}) collective-permute-start(bf16[256,2048]{1,0:T(8,128)(2,1)} %one2.1.refs_4_), channel_id=1, source_target_pairs={{0,4},{12,8},{4,0},{8,12},{1,5},{13,9},{5,1},{9,13},{2,6},{14,10},... | collective-permute-start | bytes 3145736 | tf_op jit(solution)/shard_map/send12/ppermute | solution.py:292
  344.9 36.7 %collective-permute-start.30 = (bf16[256,2048]{1,0:T(8,128)(2,1)}, bf16[256,2048]{1,0:T(8,128)(2,1)}, u32[]{:S(2)}, u32[]{:S(2)}) collective-permute-start(bf16[256,2048]{1,0:T(8,128)(2,1)} %late3.1), channel_id=1, source_target_pairs={{4,8},{8,4},{5,9},{9,5},{6,10},{10,6},{7,11},{11,7},{20,24},{24,20... | collective-permute-start | bytes 3145736 | tf_op jit(solution)/shard_map/mid_late3/ppermute | solution.py:286
  346.6 36.9 %collective-permute-start.31 = (bf16[256,2048]{1,0:T(8,128)(2,1)}, bf16[256,2048]{1,0:T(8,128)(2,1)}, u32[]{:S(2)}, u32[]{:S(2)}) collective-permute-start(bf16[256,2048]{1,0:T(8,128)(2,1)} %one3.1.refs_4_), channel_id=1, source_target_pairs={{0,4},{12,8},{4,0},{8,12},{1,5},{13,9},{5,1},{9,13},{2,6},{14,10},... | collective-permute-start | bytes 3145736 | tf_op jit(solution)/shard_map/send13/ppermute | solution.py:292
  (45 other events, 542.6 us)
Sparse Core Ops, SparseCore 0:
  54.0 24.9 all-gather.11
  94.6 24.4 all-gather.5
  121.8 19.8 reduce-scatter.1
  143.3 21.1 all-gather.7
  166.5 22.5 all-gather.9
  219.1 93.8 all-reduce.2

commit v4 on v3

--- a/solution.py
+++ b/solution.py
@@ -12,6 +12,7 @@
 SCALE = 0.5
 SPLIT = ((0, 2), (2, 5), (5, 9), (9, 13))
 WINDOW = 2
+FULL = 5
 VMEM = 60 * 1024 * 1024
 ANY = pl.BlockSpec(memory_space=pl.ANY)
 SMEM = pl.BlockSpec(memory_space=pltpu.SMEM)
@@ -130,6 +131,34 @@
     )(index, *blocks, weight, *([arrived] if has_add else []), *deps)
 
 
+def pair_kernel(deps, batch, weight, *refs):
+    outs = refs[deps:]
+    value = jnp.dot(batch[...], weight[...], preferred_element_type=jnp.float32)
+    rows = outs[0].shape[0]
+    for n, out in enumerate(outs):
+        out[...] = value[n * rows : (n + 1) * rows].astype(jnp.bfloat16)
+
+
+def pair(batches, weight, piece, deps):
+    count_batches, rows, depth = batches.shape
+    batch = batches.reshape(count_batches * rows, depth)
+    tile = tile_of(weight.shape[1])
+    first, count = piece
+    column = pl.BlockSpec((rows, tile), lambda i: (0, i))
+    return call(
+        functools.partial(pair_kernel, len(deps)),
+        2 * batch.size * count * tile,
+        out_shape=[jax.ShapeDtypeStruct((rows, count * tile), jnp.bfloat16)] * count_batches,
+        grid=(count,),
+        in_specs=[
+            pl.BlockSpec(batch.shape, lambda i: (0, 0)),
+            pl.BlockSpec((depth, tile), lambda i: (0, first + i)),
+        ]
+        + [ANY] * len(deps),
+        out_specs=[column] * count_batches,
+    )(batch, weight, *deps)
+
+
 def forward_kernel(count, deps, ids, *refs):
     blocks, down, outs = refs[:count], refs[count], refs[count + 1 + deps :]
     slices, _, _, width = down.shape
@@ -298,11 +327,19 @@
     far = lax.ppermute(block_for(z ^ 3), "dp", [(0, 3), (3, 0)])
     two = across(block_for(z ^ 2), "dp", 2)
     one = across(block_for(z ^ 1), "dp", 1)
-    far, two, one = lax.optimization_barrier((far, two, one))
+    far, one = lax.optimization_barrier((far, one))
     middle = middle_hop(after(block_for(z ^ 3), far))
     mine = block_for(z)
     first_part = jnp.where(outer, far, mine)
-    rows_first = gather_rows(first_part)
+    with jax.named_scope("first_rows"):
+        other_chip = across(first_part, "tensor", 2)
+        other_chip, two = lax.optimization_barrier((other_chip, two))
+        rows_first = [
+            (0, first_part),
+            (2, other_chip),
+            (1, across(first_part, "tensor", 1)),
+            (3, across(other_chip, "tensor", 1)),
+        ]
 
     chain = []
     work, earlier_work, pinned = [], [], []
@@ -310,9 +347,10 @@
 
     def slot(value, hop=first_hop):
         k = len(chain)
-        slot_gate[:] = chain[max(k - WINDOW, 0) : max(k - WINDOW + 1, 0)]
+        at = max(k - WINDOW, 0)
+        slot_gate[:] = chain[at : at + 1]
         with jax.named_scope(f"send{k}"):
-            tie(value, *slot_gate, *pinned, *earlier_work)
+            tie(value, *slot_gate, *pinned, *(work[-1:] if k >= FULL else earlier_work))
             chain.append(Held(hop(value.now)))
         earlier_work[:] = work[-1:]
         pinned.clear()
@@ -339,39 +377,43 @@
     firsts, twos, ones, lates = {}, {}, {}, {}
     step0, step1, step2, mid1, mid2 = {}, {}, {}, {}, {}
 
-    def add_two(j):
+    def two_of(j):
         twos[j] = piece_of("two", rows_two, j, step0[j])
         with jax.named_scope(f"mid_two{j}"):
             mid1[j] = Held(middle_hop(twos[j].now))
 
+    def pair_of(j):
+        with jax.named_scope(f"pair{j}"):
+            deps = [held.now for held in (*slot_gate, *work[-1:])]
+            ones[j], lates[j] = map(Held, pair(rows_pair, up_weight, pieces[j], deps))
+            work.append(lates[j])
+
+    def add(own, arrived):
+        tie(own, arrived, *slot_gate, *work[-1:])
+        return do((own.now.astype(jnp.float32) + arrived.now.astype(jnp.float32)).astype(jnp.bfloat16))
+
     def add_late(j):
-        lates[j] = piece_of("late", rows_late, j, step1[j])
-        with jax.named_scope(f"mid_late{j}"):
-            mid2[j] = Held(middle_hop(lates[j].now))
+        with jax.named_scope(f"late{j}"):
+            mid2[j] = Held(middle_hop(add(lates[j], step1[j]).now))
 
     def add_one(j):
-        ones[j] = piece_of("one", rows_one, j, mid1[j])
-
+        with jax.named_scope(f"one{j}"):
+            ones[j] = add(ones[j], mid1[j])
+
+    with jax.named_scope("two_rows"):
+        rows_two = gather(two)
     firsts[0] = piece_of("first", rows_first, 0)
-    with jax.named_scope("two_rows"):
-        two = late_use(two)
-        rows_two = gather(two)
 
     step0[0] = slot(firsts[0])
     firsts[1] = piece_of("first", rows_first, 1)
-    with jax.named_scope("one_rows"):
-        one = late_use(one)
-        rows_one = gather(one)
-    with jax.named_scope("late_rows"):
+    with jax.named_scope("rest_rows"):
         late_part = jnp.where(outer, mine, late_use(middle))
-        rows_late = gather(late_part)
+        rows_pair = lax.all_gather(jnp.stack([one, late_part]), "tensor", axis=1, tiled=True)
     block_tenant = late_use(block_tenant)
 
     step0[1] = slot(firsts[1])
     slot_gate[:] = chain[:1]
-    firsts[2] = piece_of("first", rows_first, 2)
-
-    slot_gate[:] = chain[1:2]
+
     tenant_ids = jnp.arange(tenants, dtype=jnp.int32)
     order = jnp.stack([jnp.where(outer, z ^ 3, z), z ^ 2, z ^ 1, jnp.where(outer, z, z ^ 3)])
     blocks_of = block_tenant.reshape(dp_count, local_blocks)
@@ -384,16 +426,18 @@
         by_batch = jnp.where((order[None, :] == jnp.arange(dp_count)[:, None])[:, :, None, None], parts, 0.0)
         by_batch = do(jnp.sum(by_batch, axis=1)).now
         projected = lax.psum_scatter(by_batch, "dp", scatter_dimension=0, tiled=True)[0]
+    firsts[2] = piece_of("first", rows_first, 2)
 
     step0[2] = slot(firsts[2])
+    slot_gate[:] = chain[1:2]
     firsts[3] = piece_of("first", rows_first, 3)
-    add_two(0)
+    two_of(0)
 
     step0[3] = slot(firsts[3])
     with jax.named_scope("projected"):
         projected = late_use(projected).astype(jnp.bfloat16)
         projected = lax.all_gather(projected, "tensor", axis=0, tiled=True)
-    add_two(1)
+    two_of(1)
     projected = late_use(projected)
     up_terms = []
     for b in range(local_blocks):
@@ -404,11 +448,14 @@
         up_terms.append(do(term.astype(jnp.bfloat16)))
 
     moved_terms = [slot(up_terms[0])]
-    add_two(2)
+    two_of(2)
+    pair_of(0)
+    pair_of(1)
     pin(mid1[0])
 
     moved_terms.append(slot(up_terms[1]))
-    add_two(3)
+    two_of(3)
+    pair_of(2)
     pin(mid1[1])
     owner_of = late_use(owner_of)
     onehot = (block_tenant[None, :] == tenant_ids[:, None]).astype(jnp.float32)
@@ -439,6 +486,7 @@
 
     step1[0] = slot(twos[0])
     pin(mid1[2])
+    pair_of(3)
     add_one(0)
     back_part = do(backward(late_use(own_ids), grad_out, adapter_up))
     with jax.named_scope("back_proj"):
@@ -486,7 +534,7 @@
     backs = [lax.dynamic_index_in_dim(backs, order[n], 0, keepdims=False) for n in range(dp_count)]
     grad_down = do(
         down_gradient(
-            index, ids, inverse, [rows_first, rows_two, rows_one, rows_late], backs, adapter_down.shape
+            index, ids, inverse, [rows_first, rows_two, *([(0, rows)] for rows in rows_pair)], backs, adapter_down.shape
         )
     )
 

time: 396 us -> 423 us (1.068)
  waiting for transfers between devices: 80.4 us -> 105 us
  Pallas kernels: 175 us -> 152 us
  other arithmetic: 15.4 us -> 38 us
    pallas_call x16 -> x8, Pallas kernels: 142 us -> 71.6 us  [share(): call(functools.partial(share_kernel, masks, has_add, len(deps)), 2 * batc...]
    pallas_call x0 -> x4, Pallas kernels: none -> 47.7 us  [pair(): call(functools.partial(pair_kernel, len(deps)), 2 * batch.size * count *...]
    ppermute x10, waiting for transfers between devices: 6.8 us -> 38.3 us  [first_hop(): return lax.ppermute(value, 'dp', [(0, 1), (3, 2)])]
    convert_element_type x0 -> x9, other arithmetic: none -> 16.6 us  [the longest x8 14.9 us: add(): (own.now.astype(jnp.float32) + arrived.now.astype(jnp.float32)).astype(jn...]
    ppermute x1, waiting for transfers between devices: 12.3 us -> 0.01 us  [local(): far = lax.ppermute(block_for(z ^ 3), 'dp', [(0, 3), (3, 0)])]
    ppermute x4, waiting for transfers between devices: 22.8 us -> 29.7 us  [first_and_last_hop(): return lax.ppermute(value, 'dp', [(0, 1), (3, 2), (1, 0), (2, 3)])]
    another operation x1 -> x2, local copies, waits for them, and re-layouts: 0.57 us -> 5.27 us  [the longest x1 4.74 us: local(): grad_down = do(down_gradient(index, ids, inverse, [rows_first, rows_two,...]
    unnamed x78 -> x74, local copies, waits for them, and re-layouts: 9.54 us -> 5.68 us
  transfers between devices with their start and end apart: 38 -> 37, of which waited for: 10 -> 10; matrix products, arithmetic and copies ran while one was open for 7% -> 13% of each run, Pallas kernels for 44% -> 36%
where the time goes in v4:
time: 423 us; the launch traced here: 419 us
  Pallas kernels  152 us (36%)
  waiting for transfers between devices  105 us (25%)
  starting transfers between devices  79.5 us (19%)
  other arithmetic  38 us (9%)
  local copies, waits for them, and re-layouts  17.6 us (4%)
  between operations  14.5 us (3%)
  matrix products  6.63 us (2%)
  blocking collectives  5.23 us (1%)
    pallas_call x8, Pallas kernels, share(): call(functools.partial(share_kernel, masks, has_add, len(deps)), 2 * batc...  71.6 us
    pallas_call x4, Pallas kernels, pair(): call(functools.partial(pair_kernel, len(deps)), 2 * batch.size * count *...  47.7 us
    ppermute x10, starting transfers between devices, first_hop(): return lax.ppermute(value, 'dp', [(0, 1), (3, 2)])  45.2 us
    ppermute x10, waiting for transfers between devices, first_hop(): return lax.ppermute(value, 'dp', [(0, 1), (3, 2)])  38.3 us
    ppermute x5, waiting for transfers between devices, across(): return lax.ppermute(value, axis, [(i, i ^ bit) for i in range(count)])  36.4 us
    ppermute x4, waiting for transfers between devices, first_and_last_hop(): return lax.ppermute(value, 'dp', [(0, 1), (3, 2), (1, 0), (2, 3)])  29.7 us
    pallas_call x4, Pallas kernels, combine(): call(functools.partial(combine_kernel, len(terms), len(extras)), 4 * slot...  20 us
    ppermute x11, starting transfers between devices, middle_hop(): return lax.ppermute(value, 'dp', [(1, 2), (2, 1)])  16.6 us
  transfers between devices with their start and end apart: 37, of which 10 were waited for; matrix products, arithmetic and copies ran while one was open for 13% of the time, Pallas kernels for 36%

profile of v4, /device:TPU:0, one launch (start us, length us, event | category | flops | bytes accessed | tf_op | source)
XLA Modules:
  0.0 419.0 jit_solution(13898035984688918096)
XLA Ops:
  13.3 4.4 %collective-permute-start = (bf16[64,4096]{1,0:T(8,128)(2,1)S(1)}, bf16[64,4096]{1,0:T(8,128)(2,1)}, u32[]{:S(2)}, u32[]{:S(2)}) collective-permute-start(bf16[64,4096]{1,0:T(8,128)(2,1)S(1)} %get-tuple-element.115), channel_id=1, source_target_pairs={{0,12},{12,0},{1,13},{13,1},{2,14},{14,2},{3,15},{15,3},{16,28},{2... | collective-permute-start | bytes 1572872 | tf_op jit(solution)/shard_map/ppermute | solution.py:327
  17.8 26.1 %collective-permute-done.1.refs_2_ = bf16[64,4096]{1,0:T(8,128)(2,1)} collective-permute-done((bf16[64,4096]{1,0:T(8,128)(2,1)}, bf16[64,4096]{1,0:T(8,128)(2,1)}, u32[]{:S(2)}, u32[]{:S(2)}) %collective-permute-start.1) | collective-permute-done | bytes 524320 | tf_op jit(solution)/shard_map/ppermute | solution.py:38
  50.3 4.1 collective-permute-done.4.refs_1_
  54.4 5.0 %collective-permute-done.3.refs_1_.refs_5_ = bf16[64,4096]{1,0:T(8,128)(2,1)} collective-permute-done((bf16[64,4096]{1,0:T(8,128)(2,1)}, bf16[64,4096]{1,0:T(8,128)(2,1)}, u32[]{:S(2)}, u32[]{:S(2)}) %collective-permute-start.3) | collective-permute-done | bytes 524320 | tf_op jit(solution)/shard_map/first_rows/ppermute | solution.py:38
  61.6 6.2 %first0.1.refs_5_ = bf16[256,1024]{1,0:T(8,128)(2,1)} custom-call(s32[1]{0:T(128)} %bitcast.index, bf16[64,4096]{1,0:T(8,128)(2,1)} %broadcast_select_fusion.1.refs_0_.refs_4_, bf16[64,4096]{1,0:T(8,128)(2,1)} %collective-permute-done.3.refs_1_.refs_5_, bf16[64,4096]{1,0:T(8,128)(2,1)} %collective-permute-done.5.refs_2_.refs_6_, ...), custom_call_target="tpu_custom_call" | custom-call | flops 21474836480 | tf_op jit(solution)/shard_map/first0/pallas_call | solution.py:117
  71.7 8.7 %first1.1 = bf16[256,1536]{1,0:T(8,128)(2,1)} custom-call(s32[1]{0:T(128)} %bitcast.index, bf16[64,4096]{1,0:T(8,128)(2,1)} %broadcast_select_fusion.1.refs_0_.refs_4_, bf16[64,4096]{1,0:T(8,128)(2,1)} %collective-permute-done.3.refs_1_.refs_5_, bf16[64,4096]{1,0:T(8,128)(2,1)} %collective-permute-done.5.refs_2_.refs_6_, ...), custom_call_target="tpu_custom_call" | custom-call | flops 32212254720 | tf_op jit(solution)/shard_map/first1/pallas_call | solution.py:117
  94.3 10.2 %first2.1.refs_6_ = bf16[256,2048]{1,0:T(8,128)(2,1)} custom-call(s32[1]{0:T(128)} %bitcast.index, bf16[64,4096]{1,0:T(8,128)(2,1)} %broadcast_select_fusion.1.refs_0_.refs_4_, bf16[64,4096]{1,0:T(8,128)(2,1)} %collective-permute-done.3.refs_1_.refs_5_, bf16[64,4096]{1,0:T(8,128)(2,1)} %collective-permute-done.5.refs_2_.refs_6_, ...), custom_call_target="tpu_custom_call" | custom-call | flops 42949672960 | tf_op jit(solution)/shard_map/first2/pallas_call | solution.py:117
  106.8 6.9 %collective-permute-done.8.refs_5_.refs_3_.refs_2_ = bf16[256,1536]{1,0:T(8,128)(2,1)S(1)} collective-permute-done((bf16[256,1536]{1,0:T(8,128)(2,1)S(1)}, bf16[256,1536]{1,0:T(8,128)(2,1)S(1)}, u32[]{:S(2)}, u32[]{:S(2)}) %collective-permute-start.8) | collective-permute-done | bytes 786464 | tf_op jit(solution)/shard_map/send1/ppermute | solution.py:312
  114.6 11.0 %first3.1.refs_4_ = bf16[256,2048]{1,0:T(8,128)(2,1)} custom-call(s32[1]{0:T(128)} %bitcast.index, bf16[64,4096]{1,0:T(8,128)(2,1)} %broadcast_select_fusion.1.refs_0_.refs_4_, bf16[64,4096]{1,0:T(8,128)(2,1)} %collective-permute-done.3.refs_1_.refs_5_, bf16[64,4096]{1,0:T(8,128)(2,1)} %collective-permute-done.5.refs_2_.refs_6_, ...), custom_call_target="tpu_custom_call" | custom-call | flops 42949672960 | tf_op jit(solution)/shard_map/first3/pallas_call | solution.py:117
  125.7 5.3 %collective-permute-start.9 = (bf16[256,2048]{1,0:T(8,128)(2,1)}, bf16[256,2048]{1,0:T(8,128)(2,1)}, u32[]{:S(2)}, u32[]{:S(2)}) collective-permute-start(bf16[256,2048]{1,0:T(8,128)(2,1)} %first3.1.refs_4_), channel_id=1, source_target_pairs={{0,4},{12,8},{1,5},{13,9},{2,6},{14,10},{3,7},{15,11},{16,20},{28,... | collective-permute-start | bytes 3145736 | tf_op jit(solution)/shard_map/send3/ppermute | solution.py:312
  131.0 6.2 %two0.1.refs_4_ = bf16[256,1024]{1,0:T(8,128)(2,1)} custom-call(s32[1]{0:T(128)} %bitcast.index, bf16[256,4096]{1,0:T(8,128)(2,1)} %all-gather.5.cloned.1.call-done.refs_0_.refs_8_, bf16[4096,6656]{1,0:T(8,128)(2,1)} %weight.7, bf16[256,1024]{1,0:T(8,128)(2,1)} %collective-permute-done.7.refs_5_.refs_2_, bf16[256,1536]{1,0:T(8,128)(2,1)} %copy-done.34, ...), custom_call_target="tpu_custom_call" | custom-call | flops 21474836480 | tf_op jit(solution)/shard_map/two0/pallas_call | solution.py:117
  138.7 8.9 %two1.1 = bf16[256,1536]{1,0:T(8,128)(2,1)} custom-call(s32[1]{0:T(128)} %bitcast.index, bf16[256,4096]{1,0:T(8,128)(2,1)} %all-gather.5.cloned.1.call-done.refs_0_.refs_8_, bf16[4096,6656]{1,0:T(8,128)(2,1)} %weight.7, bf16[256,1536]{1,0:T(8,128)(2,1)} %copy-done.34, bf16[256,1536]{1,0:T(8,128)(2,1)} %copy-done.34, bf16[256,1024]{1,0:T(8,128)(2,1)} %two0.1.refs_4_), custom_call_target="tpu_custom_call" | custom-call | flops 32212254720 | tf_op jit(solution)/shard_map/two1/pallas_call | solution.py:117
  149.2 5.2 %all_gather.18 = bf16[256,64]{1,0:T(8,128)(2,1)S(1)} all-gather(bf16[64,64]{1,0:T(8,128)(2,1)S(1)} %convert_element_type.148), channel_id=1, replica_groups=mesh['groups'=2,'dp'=4,'tensor'=4] {'tensor'}, dimensions={0}, use_global_device_ids=true | all-gather | bytes 40960 | tf_op jit(solution)/shard_map/projected/all_gather | solution.py:439
  156.5 4.1 collective-permute-start.12
  162.0 10.2 %two2.1.refs_1_ = bf16[256,2048]{1,0:T(8,128)(2,1)} custom-call(s32[1]{0:T(128)} %bitcast.index, bf16[256,4096]{1,0:T(8,128)(2,1)} %all-gather.5.cloned.1.call-done.refs_0_.refs_8_, bf16[4096,6656]{1,0:T(8,128)(2,1)} %weight.7, bf16[256,2048]{1,0:T(8,128)(2,1)} %collective-permute-done.11.refs_2_.refs_3_.refs_0_, ...), custom_call_target="tpu_custom_call" | custom-call | flops 42949672960 | tf_op jit(solution)/shard_map/two2/pallas_call | solution.py:117
  173.8 9.0 %pair0.1 = (bf16[256,1024]{1,0:T(8,128)(2,1)}, bf16[256,1024]{1,0:T(8,128)(2,1)}) custom-call(bf16[512,4096]{1,0:T(8,128)(2,1)} %bitcast.64, bf16[4096,6656]{1,0:T(8,128)(2,1)} %weight.7, bf16[256,2048]{1,0:T(8,128)(2,1)} %collective-permute-done.11.refs_2_.refs_3_.refs_0_, bf16[256,2048]{1,0:T(8,128)(2,1)} %two2.1.refs_1_), custom_call_target="tpu_custom_call" | custom-call | flops 42949672960 | tf_op jit(solution)/shard_map/pair0/pallas_call | solution.py:148
  182.8 11.3 %pair1.1 = (bf16[256,1536]{1,0:T(8,128)(2,1)}, bf16[256,1536]{1,0:T(8,128)(2,1)}) custom-call(bf16[512,4096]{1,0:T(8,128)(2,1)} %bitcast.65, bf16[4096,6656]{1,0:T(8,128)(2,1)} %weight.7, bf16[256,2048]{1,0:T(8,128)(2,1)} %collective-permute-done.11.refs_2_.refs_3_.refs_0_, bf16[256,1024]{1,0:T(8,128)(2,1)} %get-tuple-element.172.refs_1_), custom_call_target="tpu_custom_call" | custom-call | flops 64424509440 | tf_op jit(solution)/shard_map/pair1/pallas_call | solution.py:148
  194.0 10.2 %two3.1.refs_1_ = bf16[256,2048]{1,0:T(8,128)(2,1)} custom-call(s32[1]{0:T(128)} %bitcast.index, bf16[256,4096]{1,0:T(8,128)(2,1)} %all-gather.5.cloned.1.call-done.refs_0_.refs_8_, bf16[4096,6656]{1,0:T(8,128)(2,1)} %weight.7, bf16[256,2048]{1,0:T(8,128)(2,1)} %collective-permute-done.9.refs_2_.refs_3_.refs_0_, ...), custom_call_target="tpu_custom_call" | custom-call | flops 42949672960 | tf_op jit(solution)/shard_map/two3/pallas_call | solution.py:117
  206.1 13.7 %pair2.1 = (bf16[256,2048]{1,0:T(8,128)(2,1)}, bf16[256,2048]{1,0:T(8,128)(2,1)}) custom-call(bf16[512,4096]{1,0:T(8,128)(2,1)} %bitcast.66, bf16[4096,6656]{1,0:T(8,128)(2,1)} %weight.7, bf16[256,2048]{1,0:T(8,128)(2,1)} %collective-permute-done.9.refs_2_.refs_3_.refs_0_, bf16[256,2048]{1,0:T(8,128)(2,1)} %two3.1.refs_1_), custom_call_target="tpu_custom_call" | custom-call | flops 85899345920 | tf_op jit(solution)/shard_map/pair2/pallas_call | solution.py:148
  225.7 13.7 %pair3.1 = (bf16[256,2048]{1,0:T(8,128)(2,1)}, bf16[256,2048]{1,0:T(8,128)(2,1)}) custom-call(bf16[512,4096]{1,0:T(8,128)(2,1)} %bitcast.67, bf16[4096,6656]{1,0:T(8,128)(2,1)} %weight.7, bf16[64,6656]{1,0:T(8,128)(2,1)} %collective-permute-done.12.refs_0_, bf16[256,2048]{1,0:T(8,128)(2,1)} %get-tuple-element.197.refs_1_), custom_call_target="tpu_custom_call" | custom-call | flops 85899345920 | tf_op jit(solution)/shard_map/pair3/pallas_call | solution.py:148
  240.6 5.6 %shard_map.94 = f32[256,64]{1,0:T(8,128)} custom-call(s32[2]{0:T(128)} %fusion.26.ids, bf16[256,6656]{1,0:T(8,128)(2,1)} %grad.1, bf16[4,64,6656]{2,1,0:T(8,128)(2,1)} %up.1), custom_call_target="tpu_custom_call" | custom-call | flops 8724152320 | tf_op jit(solution)/shard_map/pallas_call | solution.py:206
  250.3 4.7 %far_terms.1 = bf16[2,64,6656]{2,1,0:T(8,128)(2,1)} custom-call(f32[2,4]{1,0:T(2,128)} %get-tuple-element.167.weights, f32[2]{0:T(128)} %broadcast_16_scale.2.scale, bf16[1,64,6656]{2,1,0:T(8,128)(2,1)} %bitcast.22.refs_0_, bf16[1,64,6656]{2,1,0:T(8,128)(2,1)} %bitcast.57, bf16[1,64,6656]{2,1,0:T(8,128)(2,1)} %bitcast.24.refs_2_, bf16[1,64,6656]{2,1,0:T(8,128)(2,1)} %bitcast.61), custom_call_target="tpu_custom_call" | custom-call | flops 136314880 | tf_op jit(solution)/shard_map/far_terms/pallas_call | solution.py:281
  256.0 4.7 %slice_bitcast_fusion = (bf16[256,4096]{1,0:T(8,128)(2,1)}, bf16[256,4096]{1,0:T(8,128)(2,1)}) fusion(bf16[2,256,4096]{2,1,0:T(8,128)(2,1)} %all-gather.7.cloned.1.call-done), kind=kLoop, calls=%fused_computation.9 | loop fusion | bytes 8388608 | tf_op jit(solution)/shard_map/unstack | solution.py:537
  270.0 14.3 %collective-permute-done.16 = bf16[256,1536]{1,0:T(8,128)(2,1)S(1)} collective-permute-done((bf16[256,1536]{1,0:T(8,128)(2,1)S(1)}, bf16[256,1536]{1,0:T(8,128)(2,1)S(1)}, u32[]{:S(2)}, u32[]{:S(2)}) %collective-permute-start.16) | collective-permute-done | bytes 786464 | tf_op jit(solution)/shard_map/send7/ppermute | solution.py:312
  284.3 5.4 %collective-permute-start.19 = (bf16[256,2048]{1,0:T(8,128)(2,1)}, bf16[256,2048]{1,0:T(8,128)(2,1)}, u32[]{:S(2)}, u32[]{:S(2)}) collective-permute-start(bf16[256,2048]{1,0:T(8,128)(2,1)} %two2.1.refs_1_), channel_id=1, source_target_pairs={{0,4},{12,8},{1,5},{13,9},{2,6},{14,10},{3,7},{15,11},{16,20},{28,... | collective-permute-start | bytes 3145736 | tf_op jit(solution)/shard_map/send9/ppermute | solution.py:312
  293.6 4.5 %last_terms.1 = bf16[2,64,6656]{2,1,0:T(8,128)(2,1)} custom-call(f32[2,2]{1,0:T(2,128)} %get-tuple-element.184.weights, f32[2]{0:T(128)} %broadcast_16_scale.2.scale, bf16[1,64,6656]{2,1,0:T(8,128)(2,1)} %bitcast.22.refs_0_, bf16[1,64,6656]{2,1,0:T(8,128)(2,1)} %bitcast.58, bf16[2,64,6656]{2,1,0:T(8,128)(2,1)} %copy-done.11), custom_call_target="tpu_custom_call" | custom-call | flops 68157440 | tf_op jit(solution)/shard_map/last_terms/pallas_call | solution.py:281
  299.4 4.8 %near_terms.1 = bf16[2,64,6656]{2,1,0:T(8,128)(2,1)} custom-call(f32[2,4]{1,0:T(2,128)} %get-tuple-element.187.weights, f32[2]{0:T(128)} %broadcast_16_scale.2.scale, bf16[1,64,6656]{2,1,0:T(8,128)(2,1)} %bitcast.22.refs_0_, bf16[1,64,6656]{2,1,0:T(8,128)(2,1)} %bitcast.59, bf16[1,64,6656]{2,1,0:T(8,128)(2,1)} %bitcast.24.refs_2_, bf16[1,64,6656]{2,1,0:T(8,128)(2,1)} %bitcast.62), custom_call_target="tpu_custom_call" | custom-call | flops 136314880 | tf_op jit(solution)/shard_map/near_terms/pallas_call | solution.py:281
  308.8 12.5 %collective-permute-start.23 = (bf16[256,2048]{1,0:T(8,128)(2,1)S(1)}, bf16[256,2048]{1,0:T(8,128)(2,1)S(1)}, u32[]{:S(2)}, u32[]{:S(2)}) collective-permute-start(bf16[256,2048]{1,0:T(8,128)(2,1)S(1)} %copy-done.32), channel_id=1, source_target_pairs={{0,4},{12,8},{1,5},{13,9},{2,6},{14,10},{3,7},{15,11},{16,20},{28,... | collective-permute-start | bytes 3145736 | tf_op jit(solution)/shard_map/send10/ppermute | solution.py:312
  330.6 17.0 %collective-permute-done.23 = bf16[256,2048]{1,0:T(8,128)(2,1)S(1)} collective-permute-done((bf16[256,2048]{1,0:T(8,128)(2,1)S(1)}, bf16[256,2048]{1,0:T(8,128)(2,1)S(1)}, u32[]{:S(2)}, u32[]{:S(2)}) %collective-permute-start.23) | collective-permute-done | bytes 1048608 | tf_op jit(solution)/shard_map/send10/ppermute | solution.py:312
  357.3 8.8 %collective-permute-done.26 = bf16[256,1536]{1,0:T(8,128)(2,1)} collective-permute-done((bf16[256,1536]{1,0:T(8,128)(2,1)}, bf16[256,1536]{1,0:T(8,128)(2,1)}, u32[]{:S(2)}, u32[]{:S(2)}) %collective-permute-start.26) | collective-permute-done | bytes 786464 | tf_op jit(solution)/shard_map/send11/ppermute | solution.py:321
  369.9 18.6 %collective-permute-done.25 = bf16[256,2048]{1,0:T(8,128)(2,1)} collective-permute-done((bf16[256,2048]{1,0:T(8,128)(2,1)}, bf16[256,2048]{1,0:T(8,128)(2,1)}, u32[]{:S(2)}, u32[]{:S(2)}) %collective-permute-start.25) | collective-permute-done | bytes 1048608 | tf_op jit(solution)/shard_map/send12/ppermute | solution.py:321
  388.6 6.0 %shard_map.96 = f32[2,64,6656]{2,1,0:T(8,128)} custom-call(f32[2,4]{1,0:T(2,128)} %add_select_fusion.weights, f32[2]{0:T(128)} %copy-done.23, bf16[1,64,6656]{2,1,0:T(8,128)(2,1)} %bitcast.22.refs_0_, bf16[1,64,6656]{2,1,0:T(8,128)(2,1)} %bitcast.60, bf16[1,64,6656]{2,1,0:T(8,128)(2,1)} %bitcast.24.refs_2_, bf16[1,64,6656]{2,1,0:T(8,128)(2,1)} %bitcast.63, ...), custom_call_target="tpu_custom_call" | custom-call | flops 136314880 | tf_op jit(solution)/shard_map/pallas_call | solution.py:281
  (201 shorter events, 117.2 us)
Async XLA Ops:
  7.2 77.0 %all-gather.9.cloned.1.call-start = ((), (), s32[]{:S(2)}) async-start(), calls=%async_computation.5 | async-start | bytes 2621440 | tf_op jit(solution)/shard_map/all_gather | solution.py:326
  7.9 123.1 %all-gather.5.cloned.1.call-start = ((), (), s32[]{:S(2)}) async-start(), calls=%async_computation.2 | async-start | bytes 2621440 | tf_op jit(solution)/shard_map/two_rows/all_gather | solution.py:324
  10.3 33.7 %collective-permute-start.1 = (bf16[64,4096]{1,0:T(8,128)(2,1)}, bf16[64,4096]{1,0:T(8,128)(2,1)}, u32[]{:S(2)}, u32[]{:S(2)}) collective-permute-start(bf16[64,4096]{1,0:T(8,128)(2,1)} %get-tuple-element.230), channel_id=1, source_target_pairs={{0,4},{4,0},{8,12},{12,8},{1,5},{5,1},{9,13},{13,9},{2,6},{6,2},{1... | collective-permute-start | bytes 1572872 | tf_op jit(solution)/shard_map/ppermute | solution.py:38
  13.3 30.6 %collective-permute-start = (bf16[64,4096]{1,0:T(8,128)(2,1)S(1)}, bf16[64,4096]{1,0:T(8,128)(2,1)}, u32[]{:S(2)}, u32[]{:S(2)}) collective-permute-start(bf16[64,4096]{1,0:T(8,128)(2,1)S(1)} %get-tuple-element.115), channel_id=1, source_target_pairs={{0,12},{12,0},{1,13},{13,1},{2,14},{14,2},{3,15},{15,3},{16,28},{2... | collective-permute-start | bytes 1572872 | tf_op jit(solution)/shard_map/ppermute | solution.py:327
  17.7 36.7 %collective-permute-start.4 = (bf16[64,4096]{1,0:T(8,128)(2,1)S(1)}, bf16[64,4096]{1,0:T(8,128)(2,1)}, u32[]{:S(2)}, u32[]{:S(2)}) collective-permute-start(bf16[64,4096]{1,0:T(8,128)(2,1)S(1)} %get-tuple-element.229), channel_id=1, source_target_pairs={{0,8},{4,12},{8,0},{12,4},{1,9},{5,13},{9,1},{13,5},{2,10},{6,14},... | collective-permute-start | bytes 1572872 | tf_op jit(solution)/shard_map/ppermute | solution.py:38
  60.2 78.5 %reduce-scatter.2.cloned.1.call-start = ((), (), s32[]{:S(2)}) async-start(), calls=%async_computation.1 | async-start | bytes 163840 | tf_op jit(solution)/shard_map/forward/reduce_scatter | solution.py:428
  89.4 84.3 %all-gather.7.cloned.1.call-start = ((), (), s32[]{:S(2)}) async-start(), calls=%async_computation.3 | async-start | bytes 5242880 | tf_op jit(solution)/shard_map/rest_rows/all_gather | solution.py:411
  91.3 260.2 %all-reduce.3.cloned.1.call-start = ((), (), s32[]{:S(2)}) async-start(), calls=%async_computation.4 | async-start | bytes 1048576 | tf_op jit(solution)/shard_map/back_proj/psum | solution.py:494
  91.4 22.4 %collective-permute-start.8 = (bf16[256,1536]{1,0:T(8,128)(2,1)S(1)}, bf16[256,1536]{1,0:T(8,128)(2,1)S(1)}, u32[]{:S(2)}, u32[]{:S(2)}) collective-permute-start(bf16[256,1536]{1,0:T(8,128)(2,1)S(1)} %copy-done.16), channel_id=1, source_target_pairs={{0,4},{12,8},{1,5},{13,9},{2,6},{14,10},{3,7},{15,11},{16,20},{28,... | collective-permute-start | bytes 2359304 | tf_op jit(solution)/shard_map/send1/ppermute | solution.py:312
  104.5 52.0 %collective-permute-start.11 = (bf16[256,2048]{1,0:T(8,128)(2,1)}, bf16[256,2048]{1,0:T(8,128)(2,1)}, u32[]{:S(2)}, u32[]{:S(2)}) collective-permute-start(bf16[256,2048]{1,0:T(8,128)(2,1)} %first2.1.refs_6_), channel_id=1, source_target_pairs={{0,4},{12,8},{1,5},{13,9},{2,6},{14,10},{3,7},{15,11},{16,20},{28,... | collective-permute-start | bytes 3145736 | tf_op jit(solution)/shard_map/send2/ppermute | solution.py:312
  125.7 68.4 %collective-permute-start.9 = (bf16[256,2048]{1,0:T(8,128)(2,1)}, bf16[256,2048]{1,0:T(8,128)(2,1)}, u32[]{:S(2)}, u32[]{:S(2)}) collective-permute-start(bf16[256,2048]{1,0:T(8,128)(2,1)} %first3.1.refs_4_), channel_id=1, source_target_pairs={{0,4},{12,8},{1,5},{13,9},{2,6},{14,10},{3,7},{15,11},{16,20},{28,... | collective-permute-start | bytes 3145736 | tf_op jit(solution)/shard_map/send3/ppermute | solution.py:312
  137.3 56.8 %collective-permute-start.10 = (bf16[256,1024]{1,0:T(8,128)(2,1)}, bf16[256,1024]{1,0:T(8,128)(2,1)}, u32[]{:S(2)}, u32[]{:S(2)}) collective-permute-start(bf16[256,1024]{1,0:T(8,128)(2,1)} %two0.1.refs_4_), channel_id=1, source_target_pairs={{4,8},{8,4},{5,9},{9,5},{6,10},{10,6},{7,11},{11,7},{20,24},{24,20... | collective-permute-start | bytes 1572872 | tf_op jit(solution)/shard_map/mid_two0/ppermute | solution.py:315
  147.6 75.5 %collective-permute-start.13 = (bf16[256,1536]{1,0:T(8,128)(2,1)}, bf16[256,1536]{1,0:T(8,128)(2,1)}, u32[]{:S(2)}, u32[]{:S(2)}) collective-permute-start(bf16[256,1536]{1,0:T(8,128)(2,1)} %two1.1), channel_id=1, source_target_pairs={{4,8},{8,4},{5,9},{9,5},{6,10},{10,6},{7,11},{11,7},{20,24},{24,20... | collective-permute-start | bytes 2359304 | tf_op jit(solution)/shard_map/mid_two1/ppermute | solution.py:315
  156.5 66.6 %collective-permute-start.12 = (bf16[64,6656]{1,0:T(8,128)(2,1)}, bf16[64,6656]{1,0:T(8,128)(2,1)}, u32[]{:S(2)}, u32[]{:S(2)}) collective-permute-start(bf16[64,6656]{1,0:T(8,128)(2,1)} %fusion.1), channel_id=1, source_target_pairs={{0,4},{12,8},{1,5},{13,9},{2,6},{14,10},{3,7},{15,11},{16,20},{28,... | collective-permute-start | bytes 2555912 | tf_op jit(solution)/shard_map/send4/ppermute | solution.py:312
  172.2 77.3 %collective-permute-start.15 = (bf16[256,2048]{1,0:T(8,128)(2,1)}, bf16[256,2048]{1,0:T(8,128)(2,1)}, u32[]{:S(2)}, u32[]{:S(2)}) collective-permute-start(bf16[256,2048]{1,0:T(8,128)(2,1)} %two2.1.refs_1_), channel_id=1, source_target_pairs={{4,8},{8,4},{5,9},{9,5},{6,10},{10,6},{7,11},{11,7},{20,24},{24,20... | collective-permute-start | bytes 3145736 | tf_op jit(solution)/shard_map/mid_two2/ppermute | solution.py:315
  204.3 60.5 %collective-permute-start.18 = (bf16[256,2048]{1,0:T(8,128)(2,1)}, bf16[256,2048]{1,0:T(8,128)(2,1)}, u32[]{:S(2)}, u32[]{:S(2)}) collective-permute-start(bf16[256,2048]{1,0:T(8,128)(2,1)} %two3.1.refs_1_), channel_id=1, source_target_pairs={{4,8},{8,4},{5,9},{9,5},{6,10},{10,6},{7,11},{11,7},{20,24},{24,20... | collective-permute-start | bytes 3145736 | tf_op jit(solution)/shard_map/mid_two3/ppermute | solution.py:315
  219.9 29.5 %collective-permute-start.14 = (bf16[64,6656]{1,0:T(8,128)(2,1)S(1)}, bf16[64,6656]{1,0:T(8,128)(2,1)S(1)}, u32[]{:S(2)}, u32[]{:S(2)}) collective-permute-start(bf16[64,6656]{1,0:T(8,128)(2,1)S(1)} %copy-done), channel_id=1, source_target_pairs={{0,4},{12,8},{1,5},{13,9},{2,6},{14,10},{3,7},{15,11},{16,20},{28,... | collective-permute-start | bytes 2555912 | tf_op jit(solution)/shard_map/send5/ppermute | solution.py:312
  223.5 41.4 %collective-permute-start.17 = (bf16[256,1024]{1,0:T(8,128)(2,1)}, bf16[256,1024]{1,0:T(8,128)(2,1)}, u32[]{:S(2)}, u32[]{:S(2)}) collective-permute-start(bf16[256,1024]{1,0:T(8,128)(2,1)} %two0.1.refs_4_), channel_id=1, source_target_pairs={{0,4},{12,8},{1,5},{13,9},{2,6},{14,10},{3,7},{15,11},{16,20},{28,... | collective-permute-start | bytes 1572872 | tf_op jit(solution)/shard_map/send6/ppermute | solution.py:312
  255.1 37.3 %collective-permute-start.22 = (bf16[2,64,6656]{2,1,0:T(8,128)(2,1)}, bf16[2,64,6656]{2,1,0:T(8,128)(2,1)S(1)}, u32[]{:S(2)}, u32[]{:S(2)}) collective-permute-start(bf16[2,64,6656]{2,1,0:T(8,128)(2,1)} %far_terms.1), channel_id=1, source_target_pairs={{4,8},{8,4},{5,9},{9,5},{6,10},{10,6},{7,11},{11,7},{20,24},{24,20... | collective-permute-start | bytes 5111816 | tf_op jit(solution)/shard_map/far_terms/ppermute | solution.py:315
  261.5 22.8 %collective-permute-start.16 = (bf16[256,1536]{1,0:T(8,128)(2,1)S(1)}, bf16[256,1536]{1,0:T(8,128)(2,1)S(1)}, u32[]{:S(2)}, u32[]{:S(2)}) collective-permute-start(bf16[256,1536]{1,0:T(8,128)(2,1)S(1)} %copy-done.33), channel_id=1, source_target_pairs={{0,4},{12,8},{1,5},{13,9},{2,6},{14,10},{3,7},{15,11},{16,20},{28,... | collective-permute-start | bytes 2359304 | tf_op jit(solution)/shard_map/send7/ppermute | solution.py:312
  266.1 42.7 %collective-permute-start.20 = (bf16[256,1024]{1,0:T(8,128)(2,1)S(1)}, bf16[256,1024]{1,0:T(8,128)(2,1)}, u32[]{:S(2)}, u32[]{:S(2)}) collective-permute-start(bf16[256,1024]{1,0:T(8,128)(2,1)S(1)} %add_convert_fusion.10), channel_id=1, source_target_pairs={{4,8},{8,4},{5,9},{9,5},{6,10},{10,6},{7,11},{11,7},{20,24},{24,20... | collective-permute-start | bytes 1572872 | tf_op jit(solution)/shard_map/late0/ppermute | solution.py:315
  267.5 31.9 %collective-permute-start.21 = (bf16[256,1024]{1,0:T(8,128)(2,1)S(1)}, bf16[256,1024]{1,0:T(8,128)(2,1)}, u32[]{:S(2)}, u32[]{:S(2)}) collective-permute-start(bf16[256,1024]{1,0:T(8,128)(2,1)S(1)} %add_convert_fusion.11), channel_id=1, source_target_pairs={{0,4},{12,8},{4,0},{8,12},{1,5},{13,9},{5,1},{9,13},{2,6},{14,10},... | collective-permute-start | bytes 1572872 | tf_op jit(solution)/shard_map/send8/ppermute | solution.py:321
  284.3 37.0 %collective-permute-start.19 = (bf16[256,2048]{1,0:T(8,128)(2,1)}, bf16[256,2048]{1,0:T(8,128)(2,1)}, u32[]{:S(2)}, u32[]{:S(2)}) collective-permute-start(bf16[256,2048]{1,0:T(8,128)(2,1)} %two2.1.refs_1_), channel_id=1, source_target_pairs={{0,4},{12,8},{1,5},{13,9},{2,6},{14,10},{3,7},{15,11},{16,20},{28,... | collective-permute-start | bytes 3145736 | tf_op jit(solution)/shard_map/send9/ppermute | solution.py:312
  290.7 37.6 %collective-permute-start.24 = (bf16[256,1536]{1,0:T(8,128)(2,1)}, bf16[256,1536]{1,0:T(8,128)(2,1)}, u32[]{:S(2)}, u32[]{:S(2)}) collective-permute-start(bf16[256,1536]{1,0:T(8,128)(2,1)} %add_convert_fusion.7), channel_id=1, source_target_pairs={{4,8},{8,4},{5,9},{9,5},{6,10},{10,6},{7,11},{11,7},{20,24},{24,20... | collective-permute-start | bytes 2359304 | tf_op jit(solution)/shard_map/late1/ppermute | solution.py:315
  298.1 69.6 %collective-permute-start.27 = (bf16[2,64,6656]{2,1,0:T(8,128)(2,1)}, bf16[2,64,6656]{2,1,0:T(8,128)(2,1)}, u32[]{:S(2)}, u32[]{:S(2)}) collective-permute-start(bf16[2,64,6656]{2,1,0:T(8,128)(2,1)} %last_terms.1), channel_id=1, source_target_pairs={{4,0},{8,12},{5,1},{9,13},{6,2},{10,14},{7,3},{11,15},{20,16},{24,... | collective-permute-start | bytes 5111816 | tf_op jit(solution)/shard_map/last_terms/ppermute | solution.py:318
  304.2 84.4 %collective-permute-start.28 = (bf16[2,64,6656]{2,1,0:T(8,128)(2,1)}, bf16[2,64,6656]{2,1,0:T(8,128)(2,1)}, u32[]{:S(2)}, u32[]{:S(2)}) collective-permute-start(bf16[2,64,6656]{2,1,0:T(8,128)(2,1)} %near_terms.1), channel_id=1, source_target_pairs={{4,8},{8,4},{5,9},{9,5},{6,10},{10,6},{7,11},{11,7},{20,24},{24,20... | collective-permute-start | bytes 5111816 | tf_op jit(solution)/shard_map/near_terms/ppermute | solution.py:315
  308.8 38.8 %collective-permute-start.23 = (bf16[256,2048]{1,0:T(8,128)(2,1)S(1)}, bf16[256,2048]{1,0:T(8,128)(2,1)S(1)}, u32[]{:S(2)}, u32[]{:S(2)}) collective-permute-start(bf16[256,2048]{1,0:T(8,128)(2,1)S(1)} %copy-done.32), channel_id=1, source_target_pairs={{0,4},{12,8},{1,5},{13,9},{2,6},{14,10},{3,7},{15,11},{16,20},{28,... | collective-permute-start | bytes 3145736 | tf_op jit(solution)/shard_map/send10/ppermute | solution.py:312
  324.0 79.2 %collective-permute-start.29 = (bf16[256,2048]{1,0:T(8,128)(2,1)}, bf16[256,2048]{1,0:T(8,128)(2,1)}, u32[]{:S(2)}, u32[]{:S(2)}) collective-permute-start(bf16[256,2048]{1,0:T(8,128)(2,1)} %add_convert_fusion.4), channel_id=1, source_target_pairs={{4,8},{8,4},{5,9},{9,5},{6,10},{10,6},{7,11},{11,7},{20,24},{24,20... | collective-permute-start | bytes 3145736 | tf_op jit(solution)/shard_map/late2/ppermute | solution.py:315
  328.4 37.7 %collective-permute-start.26 = (bf16[256,1536]{1,0:T(8,128)(2,1)}, bf16[256,1536]{1,0:T(8,128)(2,1)}, u32[]{:S(2)}, u32[]{:S(2)}) collective-permute-start(bf16[256,1536]{1,0:T(8,128)(2,1)} %add_convert_fusion.8), channel_id=1, source_target_pairs={{0,4},{12,8},{4,0},{8,12},{1,5},{13,9},{5,1},{9,13},{2,6},{14,10},... | collective-permute-start | bytes 2359304 | tf_op jit(solution)/shard_map/send11/ppermute | solution.py:321
  347.6 40.9 %collective-permute-start.25 = (bf16[256,2048]{1,0:T(8,128)(2,1)}, bf16[256,2048]{1,0:T(8,128)(2,1)}, u32[]{:S(2)}, u32[]{:S(2)}) collective-permute-start(bf16[256,2048]{1,0:T(8,128)(2,1)} %add_convert_fusion.5), channel_id=1, source_target_pairs={{0,4},{12,8},{4,0},{8,12},{1,5},{13,9},{5,1},{9,13},{2,6},{14,10},... | collective-permute-start | bytes 3145736 | tf_op jit(solution)/shard_map/send12/ppermute | solution.py:321
  366.1 40.1 %collective-permute-start.30 = (bf16[256,2048]{1,0:T(8,128)(2,1)}, bf16[256,2048]{1,0:T(8,128)(2,1)}, u32[]{:S(2)}, u32[]{:S(2)}) collective-permute-start(bf16[256,2048]{1,0:T(8,128)(2,1)} %add_convert_fusion.2), channel_id=1, source_target_pairs={{4,8},{8,4},{5,9},{9,5},{6,10},{10,6},{7,11},{11,7},{20,24},{24,20... | collective-permute-start | bytes 3145736 | tf_op jit(solution)/shard_map/late3/ppermute | solution.py:315
  367.8 40.7 %collective-permute-start.31 = (bf16[256,2048]{1,0:T(8,128)(2,1)}, bf16[256,2048]{1,0:T(8,128)(2,1)}, u32[]{:S(2)}, u32[]{:S(2)}) collective-permute-start(bf16[256,2048]{1,0:T(8,128)(2,1)} %add_convert_fusion.3), channel_id=1, source_target_pairs={{0,4},{12,8},{4,0},{8,12},{1,5},{13,9},{5,1},{9,13},{2,6},{14,10},... | collective-permute-start | bytes 3145736 | tf_op jit(solution)/shard_map/send13/ppermute | solution.py:321
  (42 other events, 503.5 us)
Sparse Core Ops, SparseCore 0:
  9.6 25.2 all-gather.8
  60.4 23.8 all-gather.4
  89.6 19.2 reduce-scatter.1
  110.9 32.6 all-gather.6
  248.2 94.0 all-reduce.2

commit v5 on v4

--- a/solution.py
+++ b/solution.py
@@ -350,7 +350,7 @@
         at = max(k - WINDOW, 0)
         slot_gate[:] = chain[at : at + 1]
         with jax.named_scope(f"send{k}"):
-            tie(value, *slot_gate, *pinned, *(work[-1:] if k >= FULL else earlier_work))
+            tie(value, *slot_gate, *pinned, *earlier_work)
             chain.append(Held(hop(value.now)))
         earlier_work[:] = work[-1:]
         pinned.clear()
@@ -377,38 +377,30 @@
     firsts, twos, ones, lates = {}, {}, {}, {}
     step0, step1, step2, mid1, mid2 = {}, {}, {}, {}, {}
 
-    def two_of(j):
+    def add_two(j):
         twos[j] = piece_of("two", rows_two, j, step0[j])
         with jax.named_scope(f"mid_two{j}"):
             mid1[j] = Held(middle_hop(twos[j].now))
 
-    def pair_of(j):
-        with jax.named_scope(f"pair{j}"):
-            deps = [held.now for held in (*slot_gate, *work[-1:])]
-            ones[j], lates[j] = map(Held, pair(rows_pair, up_weight, pieces[j], deps))
-            work.append(lates[j])
-
-    def add(own, arrived):
-        tie(own, arrived, *slot_gate, *work[-1:])
-        return do((own.now.astype(jnp.float32) + arrived.now.astype(jnp.float32)).astype(jnp.bfloat16))
-
     def add_late(j):
-        with jax.named_scope(f"late{j}"):
-            mid2[j] = Held(middle_hop(add(lates[j], step1[j]).now))
+        lates[j] = piece_of("late", rows_late, j, step1[j])
+        with jax.named_scope(f"mid_late{j}"):
+            mid2[j] = Held(middle_hop(lates[j].now))
 
     def add_one(j):
-        with jax.named_scope(f"one{j}"):
-            ones[j] = add(ones[j], mid1[j])
+        ones[j] = piece_of("one", rows_one, j, mid1[j])
 
     with jax.named_scope("two_rows"):
         rows_two = gather(two)
     firsts[0] = piece_of("first", rows_first, 0)
-
     step0[0] = slot(firsts[0])
     firsts[1] = piece_of("first", rows_first, 1)
-    with jax.named_scope("rest_rows"):
+    with jax.named_scope("one_rows"):
+        one = late_use(one)
+        rows_one = gather(one)
+    with jax.named_scope("late_rows"):
         late_part = jnp.where(outer, mine, late_use(middle))
-        rows_pair = lax.all_gather(jnp.stack([one, late_part]), "tensor", axis=1, tiled=True)
+        rows_late = gather(late_part)
     block_tenant = late_use(block_tenant)
 
     step0[1] = slot(firsts[1])
@@ -429,15 +421,14 @@
     firsts[2] = piece_of("first", rows_first, 2)
 
     step0[2] = slot(firsts[2])
-    slot_gate[:] = chain[1:2]
     firsts[3] = piece_of("first", rows_first, 3)
-    two_of(0)
+    add_two(0)
 
     step0[3] = slot(firsts[3])
+    add_two(1)
     with jax.named_scope("projected"):
         projected = late_use(projected).astype(jnp.bfloat16)
         projected = lax.all_gather(projected, "tensor", axis=0, tiled=True)
-    two_of(1)
     projected = late_use(projected)
     up_terms = []
     for b in range(local_blocks):
@@ -448,14 +439,11 @@
         up_terms.append(do(term.astype(jnp.bfloat16)))
 
     moved_terms = [slot(up_terms[0])]
-    two_of(2)
-    pair_of(0)
-    pair_of(1)
+    add_two(2)
     pin(mid1[0])
 
     moved_terms.append(slot(up_terms[1]))
-    two_of(3)
-    pair_of(2)
+    add_one(0)
     pin(mid1[1])
     owner_of = late_use(owner_of)
     onehot = (block_tenant[None, :] == tenant_ids[:, None]).astype(jnp.float32)
@@ -486,8 +474,7 @@
 
     step1[0] = slot(twos[0])
     pin(mid1[2])
-    pair_of(3)
-    add_one(0)
+    add_two(3)
     back_part = do(backward(late_use(own_ids), grad_out, adapter_up))
     with jax.named_scope("back_proj"):
         back_full = jnp.where((jnp.arange(dp_count) == z)[:, None, None], back_part.now, 0.0)
@@ -534,7 +521,7 @@
     backs = [lax.dynamic_index_in_dim(backs, order[n], 0, keepdims=False) for n in range(dp_count)]
     grad_down = do(
         down_gradient(
-            index, ids, inverse, [rows_first, rows_two, *([(0, rows)] for rows in rows_pair)], backs, adapter_down.shape
+            index, ids, inverse, [rows_first, rows_two, rows_one, rows_late], backs, adapter_down.shape
         )
     )
 

time: 423 us -> 399 us (0.943)
  waiting for transfers between devices: 105 us -> 78.4 us
  Pallas kernels: 152 us -> 175 us
  other arithmetic: 38 us -> 20.8 us
    pallas_call x8 -> x16, Pallas kernels: 71.6 us -> 142 us  [share(): call(functools.partial(share_kernel, masks, has_add, len(deps)), 2 * batc...]
    pallas_call x4 -> x0, Pallas kernels: 47.7 us -> none  [pair(): call(functools.partial(pair_kernel, len(deps)), 2 * batch.size * count *...]
    ppermute x10, waiting for transfers between devices: 38.3 us -> 7.87 us  [first_hop(): return lax.ppermute(value, 'dp', [(0, 1), (3, 2)])]
    convert_element_type x8 -> x0, other arithmetic: 14.9 us -> none  [add(): (own.now.astype(jnp.float32) + arrived.now.astype(jnp.float32)).astype(jn...]
    ppermute x1, waiting for transfers between devices: 0.01 us -> 12.3 us  [local(): far = lax.ppermute(block_for(z ^ 3), 'dp', [(0, 3), (3, 0)])]
    ppermute x4, waiting for transfers between devices: 29.7 us -> 21.4 us  [first_and_last_hop(): return lax.ppermute(value, 'dp', [(0, 1), (3, 2), (1, 0), (2, 3)])]
    ppermute x4, starting transfers between devices: 7.13 us -> 12.3 us  [first_and_last_hop(): return lax.ppermute(value, 'dp', [(0, 1), (3, 2), (1, 0), (2, 3)])]
    another operation x2 -> x1, local copies, waits for them, and re-layouts: 5.27 us -> 0.54 us  [the longest x1 4.74 us: local(): grad_down = do(down_gradient(index, ids, inverse, [rows_first, rows_two,...]
  transfers between devices with their start and end apart: 37 -> 38, of which waited for: 10 -> 8; matrix products, arithmetic and copies ran while one was open for 13% -> 8% of each run, Pallas kernels for 36% -> 44%
where the time goes in v5:
time: 399 us; the launch traced here: 398 us
  Pallas kernels  175 us (44%)
  starting transfers between devices  80.9 us (20%)
  waiting for transfers between devices  78.4 us (20%)
  other arithmetic  20.8 us (5%)
  local copies, waits for them, and re-layouts  15.8 us (4%)
  between operations  14.8 us (4%)
  matrix products  6.65 us (2%)
  blocking collectives  5.54 us (1%)
    pallas_call x16, Pallas kernels, share(): call(functools.partial(share_kernel, masks, has_add, len(deps)), 2 * batc...  142 us
    ppermute x10, starting transfers between devices, first_hop(): return lax.ppermute(value, 'dp', [(0, 1), (3, 2)])  44.3 us
    ppermute x5, waiting for transfers between devices, across(): return lax.ppermute(value, axis, [(i, i ^ bit) for i in range(count)])  35.4 us
    ppermute x4, waiting for transfers between devices, first_and_last_hop(): return lax.ppermute(value, 'dp', [(0, 1), (3, 2), (1, 0), (2, 3)])  21.4 us
    pallas_call x4, Pallas kernels, combine(): call(functools.partial(combine_kernel, len(terms), len(extras)), 4 * slot...  19.8 us
    ppermute x11, starting transfers between devices, middle_hop(): return lax.ppermute(value, 'dp', [(1, 2), (2, 1)])  13.7 us
    ppermute x4, starting transfers between devices, first_and_last_hop(): return lax.ppermute(value, 'dp', [(0, 1), (3, 2), (1, 0), (2, 3)])  12.3 us
    ppermute x1, waiting for transfers between devices, local(): far = lax.ppermute(block_for(z ^ 3), 'dp', [(0, 3), (3, 0)])  12.3 us
  transfers between devices with their start and end apart: 38, of which 8 were waited for; matrix products, arithmetic and copies ran while one was open for 8% of the time, Pallas kernels for 44%

profile of v5, /device:TPU:0, one launch (start us, length us, event | category | flops | bytes accessed | tf_op | source)
XLA Modules:
  0.0 397.6 jit_solution(6355400386418770676)
XLA Ops:
  10.3 6.9 %collective-permute-start = (bf16[64,4096]{1,0:T(8,128)(2,1)S(1)}, bf16[64,4096]{1,0:T(8,128)(2,1)}, u32[]{:S(2)}, u32[]{:S(2)}) collective-permute-start(bf16[64,4096]{1,0:T(8,128)(2,1)S(1)} %get-tuple-element.86), channel_id=1, source_target_pairs={{0,12},{12,0},{1,13},{13,1},{2,14},{14,2},{3,15},{15,3},{16,28},{2... | collective-permute-start | bytes 1572872 | tf_op jit(solution)/shard_map/ppermute | solution.py:327
  17.9 12.3 %collective-permute-done = bf16[64,4096]{1,0:T(8,128)(2,1)} collective-permute-done((bf16[64,4096]{1,0:T(8,128)(2,1)S(1)}, bf16[64,4096]{1,0:T(8,128)(2,1)}, u32[]{:S(2)}, u32[]{:S(2)}) %collective-permute-start) | collective-permute-done | bytes 524320 | tf_op jit(solution)/shard_map/ppermute | solution.py:327
  30.2 21.5 %collective-permute-done.1.refs_2_ = bf16[64,4096]{1,0:T(8,128)(2,1)} collective-permute-done((bf16[64,4096]{1,0:T(8,128)(2,1)}, bf16[64,4096]{1,0:T(8,128)(2,1)}, u32[]{:S(2)}, u32[]{:S(2)}) %collective-permute-start.1) | collective-permute-done | bytes 524320 | tf_op jit(solution)/shard_map/ppermute | solution.py:38
  55.2 12.7 %collective-permute-done.3.refs_1_.refs_5_ = bf16[64,4096]{1,0:T(8,128)(2,1)} collective-permute-done((bf16[64,4096]{1,0:T(8,128)(2,1)}, bf16[64,4096]{1,0:T(8,128)(2,1)}, u32[]{:S(2)}, u32[]{:S(2)}) %collective-permute-start.3) | collective-permute-done | bytes 524320 | tf_op jit(solution)/shard_map/first_rows/ppermute | solution.py:38
  70.1 6.2 %first0.1.refs_5_ = bf16[256,1024]{1,0:T(8,128)(2,1)} custom-call(s32[1]{0:T(128)} %bitcast.index, bf16[64,4096]{1,0:T(8,128)(2,1)} %broadcast_select_fusion.1.refs_0_.refs_4_, bf16[64,4096]{1,0:T(8,128)(2,1)} %collective-permute-done.3.refs_1_.refs_5_, bf16[64,4096]{1,0:T(8,128)(2,1)} %collective-permute-done.5.refs_2_.refs_6_, ...), custom_call_target="tpu_custom_call" | custom-call | flops 21474836480 | tf_op jit(solution)/shard_map/first0/pallas_call | solution.py:117
  78.5 8.6 %first1.1 = bf16[256,1536]{1,0:T(8,128)(2,1)} custom-call(s32[1]{0:T(128)} %bitcast.index, bf16[64,4096]{1,0:T(8,128)(2,1)} %broadcast_select_fusion.1.refs_0_.refs_4_, bf16[64,4096]{1,0:T(8,128)(2,1)} %collective-permute-done.3.refs_1_.refs_5_, bf16[64,4096]{1,0:T(8,128)(2,1)} %collective-permute-done.5.refs_2_.refs_6_, ...), custom_call_target="tpu_custom_call" | custom-call | flops 32212254720 | tf_op jit(solution)/shard_map/first1/pallas_call | solution.py:117
  104.2 10.2 %first2.1.refs_6_ = bf16[256,2048]{1,0:T(8,128)(2,1)} custom-call(s32[1]{0:T(128)} %bitcast.index, bf16[64,4096]{1,0:T(8,128)(2,1)} %broadcast_select_fusion.1.refs_0_.refs_4_, bf16[64,4096]{1,0:T(8,128)(2,1)} %collective-permute-done.3.refs_1_.refs_5_, bf16[64,4096]{1,0:T(8,128)(2,1)} %collective-permute-done.5.refs_2_.refs_6_, ...), custom_call_target="tpu_custom_call" | custom-call | flops 42949672960 | tf_op jit(solution)/shard_map/first2/pallas_call | solution.py:117
  116.8 10.7 %first3.1.refs_4_ = bf16[256,2048]{1,0:T(8,128)(2,1)} custom-call(s32[1]{0:T(128)} %bitcast.index, bf16[64,4096]{1,0:T(8,128)(2,1)} %broadcast_select_fusion.1.refs_0_.refs_4_, bf16[64,4096]{1,0:T(8,128)(2,1)} %collective-permute-done.3.refs_1_.refs_5_, bf16[64,4096]{1,0:T(8,128)(2,1)} %collective-permute-done.5.refs_2_.refs_6_, ...), custom_call_target="tpu_custom_call" | custom-call | flops 42949672960 | tf_op jit(solution)/shard_map/first3/pallas_call | solution.py:117
  129.8 6.2 %two0.1.refs_4_ = bf16[256,1024]{1,0:T(8,128)(2,1)} custom-call(s32[1]{0:T(128)} %bitcast.index, bf16[256,4096]{1,0:T(8,128)(2,1)} %all-gather.6.cloned.1.call-done.refs_0_.refs_8_, bf16[4096,6656]{1,0:T(8,128)(2,1)} %refs_1_.23, bf16[256,1024]{1,0:T(8,128)(2,1)} %collective-permute-done.7.refs_5_.refs_2_.refs_3_, ...), custom_call_target="tpu_custom_call" | custom-call | flops 21474836480 | tf_op jit(solution)/shard_map/two0/pallas_call | solution.py:117
  137.5 8.6 %two1.1 = bf16[256,1536]{1,0:T(8,128)(2,1)} custom-call(s32[1]{0:T(128)} %bitcast.index, bf16[256,4096]{1,0:T(8,128)(2,1)} %all-gather.6.cloned.1.call-done.refs_0_.refs_8_, bf16[4096,6656]{1,0:T(8,128)(2,1)} %refs_1_.23, bf16[256,1536]{1,0:T(8,128)(2,1)} %copy-done.36, bf16[256,1536]{1,0:T(8,128)(2,1)} %copy-done.36, bf16[256,1024]{1,0:T(8,128)(2,1)} %two0.1.refs_4_), custom_call_target="tpu_custom_call" | custom-call | flops 32212254720 | tf_op jit(solution)/shard_map/two1/pallas_call | solution.py:117
  148.4 5.5 %all_gather.21 = bf16[256,64]{1,0:T(8,128)(2,1)S(1)} all-gather(bf16[64,64]{1,0:T(8,128)(2,1)S(1)} %convert_element_type.76), channel_id=1, replica_groups=mesh['groups'=2,'dp'=4,'tensor'=4] {'tensor'}, dimensions={0}, use_global_device_ids=true | all-gather | bytes 40960 | tf_op jit(solution)/shard_map/projected/all_gather | solution.py:431
  158.9 10.1 %two2.1.refs_4_ = bf16[256,2048]{1,0:T(8,128)(2,1)} custom-call(s32[1]{0:T(128)} %bitcast.index, bf16[256,4096]{1,0:T(8,128)(2,1)} %all-gather.6.cloned.1.call-done.refs_0_.refs_8_, bf16[4096,6656]{1,0:T(8,128)(2,1)} %refs_1_.23, bf16[256,2048]{1,0:T(8,128)(2,1)} %collective-permute-done.11.refs_2_.refs_3_, ...), custom_call_target="tpu_custom_call" | custom-call | flops 42949672960 | tf_op jit(solution)/shard_map/two2/pallas_call | solution.py:117
  174.7 6.3 %one0.1.refs_4_ = bf16[256,1024]{1,0:T(8,128)(2,1)} custom-call(s32[1]{0:T(128)} %bitcast.index, bf16[256,4096]{1,0:T(8,128)(2,1)} %all-gather.8.cloned.1.call-done.refs_0_.refs_9_, bf16[4096,6656]{1,0:T(8,128)(2,1)} %refs_1_.23, bf16[256,1024]{1,0:T(8,128)(2,1)} %collective-permute-done.10.refs_2_, ...), custom_call_target="tpu_custom_call" | custom-call | flops 21474836480 | tf_op jit(solution)/shard_map/one0/pallas_call | solution.py:117
  185.6 7.5 %collective-permute-done.14.refs_3_ = bf16[64,6656]{1,0:T(8,128)(2,1)S(1)} collective-permute-done((bf16[64,6656]{1,0:T(8,128)(2,1)S(1)}, bf16[64,6656]{1,0:T(8,128)(2,1)S(1)}, u32[]{:S(2)}, u32[]{:S(2)}) %collective-permute-start.14) | collective-permute-done | bytes 852000 | tf_op jit(solution)/shard_map/send4/ppermute | solution.py:312
  194.1 10.2 %two3.1 = bf16[256,2048]{1,0:T(8,128)(2,1)} custom-call(s32[1]{0:T(128)} %bitcast.index, bf16[256,4096]{1,0:T(8,128)(2,1)} %all-gather.6.cloned.1.call-done.refs_0_.refs_8_, bf16[4096,6656]{1,0:T(8,128)(2,1)} %refs_1_.23, bf16[256,2048]{1,0:T(8,128)(2,1)} %collective-permute-done.9.refs_3_.refs_2_, bf16[64,6656]{1,0:T(8,128)(2,1)} %copy-done.2, ...), custom_call_target="tpu_custom_call" | custom-call | flops 42949672960 | tf_op jit(solution)/shard_map/two3/pallas_call | solution.py:117
  205.2 7.1 %collective-permute-start.16 = (bf16[256,1024]{1,0:T(8,128)(2,1)}, bf16[256,1024]{1,0:T(8,128)(2,1)S(1)}, u32[]{:S(2)}, u32[]{:S(2)}) collective-permute-start(bf16[256,1024]{1,0:T(8,128)(2,1)} %two0.1.refs_4_), channel_id=1, source_target_pairs={{0,4},{12,8},{1,5},{13,9},{2,6},{14,10},{3,7},{15,11},{16,20},{28,... | collective-permute-start | bytes 1572872 | tf_op jit(solution)/shard_map/send6/ppermute | solution.py:312
  212.3 5.6 %shard_map.94 = f32[256,64]{1,0:T(8,128)} custom-call(s32[2]{0:T(128)} %fusion.26.ids, bf16[256,6656]{1,0:T(8,128)(2,1)} %grad.1, bf16[4,64,6656]{2,1,0:T(8,128)(2,1)} %up.1), custom_call_target="tpu_custom_call" | custom-call | flops 8724152320 | tf_op jit(solution)/shard_map/pallas_call | solution.py:206
  222.4 4.7 %far_terms.1.refs_4_ = bf16[2,64,6656]{2,1,0:T(8,128)(2,1)} custom-call(f32[2,4]{1,0:T(2,128)} %add_convert_fusion.5.weights, f32[2]{0:T(128)} %broadcast_16_scale.2.scale, bf16[1,64,6656]{2,1,0:T(8,128)(2,1)} %bitcast.50, bf16[1,64,6656]{2,1,0:T(8,128)(2,1)} %bitcast.54, bf16[1,64,6656]{2,1,0:T(8,128)(2,1)} %bitcast.58, bf16[1,64,6656]{2,1,0:T(8,128)(2,1)} %bitcast.61), custom_call_target="tpu_custom_call" | custom-call | flops 136314880 | tf_op jit(solution)/shard_map/far_terms/pallas_call | solution.py:281
  228.7 8.1 %collective-permute-start.18 = (bf16[256,1024]{1,0:T(8,128)(2,1)}, bf16[256,1024]{1,0:T(8,128)(2,1)S(1)}, u32[]{:S(2)}, u32[]{:S(2)}) collective-permute-start(bf16[256,1024]{1,0:T(8,128)(2,1)} %one0.1.refs_4_), channel_id=1, source_target_pairs={{0,4},{12,8},{4,0},{8,12},{1,5},{13,9},{5,1},{9,13},{2,6},{14,10},... | collective-permute-start | bytes 1572872 | tf_op jit(solution)/shard_map/send8/ppermute | solution.py:321
  236.8 6.2 %late0.1.refs_4_ = bf16[256,1024]{1,0:T(8,128)(2,1)} custom-call(s32[1]{0:T(128)} %bitcast.index, bf16[256,4096]{1,0:T(8,128)(2,1)} %all-gather.10.cloned.1.call-done.refs_0_.refs_10_, bf16[4096,6656]{1,0:T(8,128)(2,1)} %refs_1_.23, bf16[256,1024]{1,0:T(8,128)(2,1)} %copy-done.37, bf16[256,1024]{1,0:T(8,128)(2,1)} %copy-done.37, ...), custom_call_target="tpu_custom_call" | custom-call | flops 21474836480 | tf_op jit(solution)/shard_map/late0/pallas_call | solution.py:117
  243.7 8.7 %one1.1.refs_4_ = bf16[256,1536]{1,0:T(8,128)(2,1)} custom-call(s32[1]{0:T(128)} %bitcast.index, bf16[256,4096]{1,0:T(8,128)(2,1)} %all-gather.8.cloned.1.call-done.refs_0_.refs_9_, bf16[4096,6656]{1,0:T(8,128)(2,1)} %refs_1_.23, bf16[256,1536]{1,0:T(8,128)(2,1)} %collective-permute-done.15.refs_2_, bf16[256,1024]{1,0:T(8,128)(2,1)} %copy-done.37, ...), custom_call_target="tpu_custom_call" | custom-call | flops 32212254720 | tf_op jit(solution)/shard_map/one1/pallas_call | solution.py:117
  252.4 8.7 %late1.1 = bf16[256,1536]{1,0:T(8,128)(2,1)} custom-call(s32[1]{0:T(128)} %bitcast.index, bf16[256,4096]{1,0:T(8,128)(2,1)} %all-gather.10.cloned.1.call-done.refs_0_.refs_10_, bf16[4096,6656]{1,0:T(8,128)(2,1)} %refs_1_.23, bf16[256,1536]{1,0:T(8,128)(2,1)} %collective-permute-done.20.refs_2_.refs_3_, ...), custom_call_target="tpu_custom_call" | custom-call | flops 32212254720 | tf_op jit(solution)/shard_map/late1/pallas_call | solution.py:117
  261.8 7.7 %collective-permute-start.24 = (bf16[256,2048]{1,0:T(8,128)(2,1)}, bf16[256,2048]{1,0:T(8,128)(2,1)}, u32[]{:S(2)}, u32[]{:S(2)}) collective-permute-start(bf16[256,2048]{1,0:T(8,128)(2,1)} %two2.1.refs_4_), channel_id=1, source_target_pairs={{0,4},{12,8},{1,5},{13,9},{2,6},{14,10},{3,7},{15,11},{16,20},{28,... | collective-permute-start | bytes 3145736 | tf_op jit(solution)/shard_map/send9/ppermute | solution.py:312
  270.8 4.5 %last_terms.1 = bf16[2,64,6656]{2,1,0:T(8,128)(2,1)} custom-call(f32[2,2]{1,0:T(2,128)} %get-tuple-element.139.weights, f32[2]{0:T(128)} %broadcast_16_scale.2.scale, bf16[1,64,6656]{2,1,0:T(8,128)(2,1)} %bitcast.51, bf16[1,64,6656]{2,1,0:T(8,128)(2,1)} %bitcast.55, bf16[2,64,6656]{2,1,0:T(8,128)(2,1)} %copy-done.7), custom_call_target="tpu_custom_call" | custom-call | flops 68157440 | tf_op jit(solution)/shard_map/last_terms/pallas_call | solution.py:281
  276.5 4.7 %near_terms.1.refs_4_ = bf16[2,64,6656]{2,1,0:T(8,128)(2,1)} custom-call(f32[2,4]{1,0:T(2,128)} %add_convert_fusion.4.weights, f32[2]{0:T(128)} %broadcast_16_scale.2.scale, bf16[1,64,6656]{2,1,0:T(8,128)(2,1)} %bitcast.52, bf16[1,64,6656]{2,1,0:T(8,128)(2,1)} %bitcast.56, bf16[1,64,6656]{2,1,0:T(8,128)(2,1)} %bitcast.59, bf16[1,64,6656]{2,1,0:T(8,128)(2,1)} %bitcast.62), custom_call_target="tpu_custom_call" | custom-call | flops 136314880 | tf_op jit(solution)/shard_map/near_terms/pallas_call | solution.py:281
  283.2 10.4 %one2.1.refs_4_ = bf16[256,2048]{1,0:T(8,128)(2,1)} custom-call(s32[1]{0:T(128)} %bitcast.index, bf16[256,4096]{1,0:T(8,128)(2,1)} %all-gather.8.cloned.1.call-done.refs_0_.refs_9_, bf16[4096,6656]{1,0:T(8,128)(2,1)} %refs_1_.23, bf16[256,2048]{1,0:T(8,128)(2,1)} %collective-permute-done.13.refs_2_, bf16[256,1024]{1,0:T(8,128)(2,1)} %copy-done.18, ...), custom_call_target="tpu_custom_call" | custom-call | flops 42949672960 | tf_op jit(solution)/shard_map/one2/pallas_call | solution.py:117
  293.6 11.4 %collective-permute-start.21 = (bf16[256,2048]{1,0:T(8,128)(2,1)S(1)}, bf16[256,2048]{1,0:T(8,128)(2,1)S(1)}, u32[]{:S(2)}, u32[]{:S(2)}) collective-permute-start(bf16[256,2048]{1,0:T(8,128)(2,1)S(1)} %copy-done.33), channel_id=1, source_target_pairs={{0,4},{12,8},{1,5},{13,9},{2,6},{14,10},{3,7},{15,11},{16,20},{28,... | collective-permute-start | bytes 3145736 | tf_op jit(solution)/shard_map/send10/ppermute | solution.py:312
  305.0 10.3 %late2.1.refs_4_ = bf16[256,2048]{1,0:T(8,128)(2,1)} custom-call(s32[1]{0:T(128)} %bitcast.index, bf16[256,4096]{1,0:T(8,128)(2,1)} %all-gather.10.cloned.1.call-done.refs_0_.refs_10_, bf16[4096,6656]{1,0:T(8,128)(2,1)} %refs_1_.23, bf16[256,2048]{1,0:T(8,128)(2,1)} %collective-permute-done.24.refs_2_.refs_3_, ...), custom_call_target="tpu_custom_call" | custom-call | flops 42949672960 | tf_op jit(solution)/shard_map/late2/pallas_call | solution.py:117
  316.9 10.2 %one3.1.refs_4_ = bf16[256,2048]{1,0:T(8,128)(2,1)} custom-call(s32[1]{0:T(128)} %bitcast.index, bf16[256,4096]{1,0:T(8,128)(2,1)} %all-gather.8.cloned.1.call-done.refs_0_.refs_9_, bf16[4096,6656]{1,0:T(8,128)(2,1)} %refs_1_.23, bf16[256,2048]{1,0:T(8,128)(2,1)} %copy-done.34, bf16[256,2048]{1,0:T(8,128)(2,1)} %collective-permute-done.24.refs_2_.refs_3_, ...), custom_call_target="tpu_custom_call" | custom-call | flops 42949672960 | tf_op jit(solution)/shard_map/one3/pallas_call | solution.py:117
  329.2 10.3 %late3.1 = bf16[256,2048]{1,0:T(8,128)(2,1)} custom-call(s32[1]{0:T(128)} %bitcast.index, bf16[256,4096]{1,0:T(8,128)(2,1)} %all-gather.10.cloned.1.call-done.refs_0_.refs_10_, bf16[4096,6656]{1,0:T(8,128)(2,1)} %refs_1_.23, bf16[256,2048]{1,0:T(8,128)(2,1)} %copy-done.35, bf16[256,2048]{1,0:T(8,128)(2,1)} %copy-done.35, bf16[256,2048]{1,0:T(8,128)(2,1)} %one3.1.refs_4_), custom_call_target="tpu_custom_call" | custom-call | flops 42949672960 | tf_op jit(solution)/shard_map/late3/pallas_call | solution.py:117
  351.8 18.7 %collective-permute-done.23 = bf16[256,2048]{1,0:T(8,128)(2,1)} collective-permute-done((bf16[256,2048]{1,0:T(8,128)(2,1)}, bf16[256,2048]{1,0:T(8,128)(2,1)}, u32[]{:S(2)}, u32[]{:S(2)}) %collective-permute-start.23) | collective-permute-done | bytes 1048608 | tf_op jit(solution)/shard_map/send12/ppermute | solution.py:321
  370.4 6.0 %shard_map.96 = f32[2,64,6656]{2,1,0:T(8,128)} custom-call(f32[2,4]{1,0:T(2,128)} %add_select_fusion.weights, f32[2]{0:T(128)} %copy-done.24, bf16[1,64,6656]{2,1,0:T(8,128)(2,1)} %bitcast.53, bf16[1,64,6656]{2,1,0:T(8,128)(2,1)} %bitcast.57, bf16[1,64,6656]{2,1,0:T(8,128)(2,1)} %bitcast.60, bf16[1,64,6656]{2,1,0:T(8,128)(2,1)} %bitcast.63, ...), custom_call_target="tpu_custom_call" | custom-call | flops 136314880 | tf_op jit(solution)/shard_map/pallas_call | solution.py:281
  (204 shorter events, 96.3 us)
Async XLA Ops:
  7.2 82.6 %all-gather.12.cloned.1.call-start = ((), (), s32[]{:S(2)}) async-start(), calls=%async_computation.6 | async-start | bytes 2621440 | tf_op jit(solution)/shard_map/all_gather | solution.py:326
  7.9 121.9 %all-gather.6.cloned.1.call-start = ((), (), s32[]{:S(2)}) async-start(), calls=%async_computation.2 | async-start | bytes 2621440 | tf_op jit(solution)/shard_map/two_rows/all_gather | solution.py:324
  17.2 34.5 %collective-permute-start.1 = (bf16[64,4096]{1,0:T(8,128)(2,1)}, bf16[64,4096]{1,0:T(8,128)(2,1)}, u32[]{:S(2)}, u32[]{:S(2)}) collective-permute-start(bf16[64,4096]{1,0:T(8,128)(2,1)} %get-tuple-element.170), channel_id=1, source_target_pairs={{0,4},{4,0},{8,12},{12,8},{1,5},{5,1},{9,13},{13,9},{2,6},{6,2},{1... | collective-permute-start | bytes 1572872 | tf_op jit(solution)/shard_map/ppermute | solution.py:38
  17.3 37.9 %collective-permute-start.4 = (bf16[64,4096]{1,0:T(8,128)(2,1)S(1)}, bf16[64,4096]{1,0:T(8,128)(2,1)}, u32[]{:S(2)}, u32[]{:S(2)}) collective-permute-start(bf16[64,4096]{1,0:T(8,128)(2,1)S(1)} %get-tuple-element.169), channel_id=1, source_target_pairs={{0,8},{4,12},{8,0},{12,4},{1,9},{5,13},{9,1},{13,5},{2,10},{6,14},... | collective-permute-start | bytes 1572872 | tf_op jit(solution)/shard_map/ppermute | solution.py:38
  68.8 78.9 %reduce-scatter.2.cloned.1.call-start = ((), (), s32[]{:S(2)}) async-start(), calls=%async_computation.1 | async-start | bytes 163840 | tf_op jit(solution)/shard_map/forward/reduce_scatter | solution.py:420
  95.0 79.7 %all-gather.8.cloned.1.call-start = ((), (), s32[]{:S(2)}) async-start(), calls=%async_computation.3 | async-start | bytes 2621440 | tf_op jit(solution)/shard_map/one_rows/all_gather | solution.py:324
  95.6 141.3 %all-gather.10.cloned.1.call-start = ((), (), s32[]{:S(2)}) async-start(), calls=%async_computation.4 | async-start | bytes 2621440 | tf_op jit(solution)/shard_map/late_rows/all_gather | solution.py:324
  99.1 240.3 %all-reduce.3.cloned.1.call-start = ((), (), s32[]{:S(2)}) async-start(), calls=%async_computation.5 | async-start | bytes 1048576 | tf_op jit(solution)/shard_map/back_proj/psum | solution.py:481
  99.8 27.7 %collective-permute-start.8 = (bf16[256,1536]{1,0:T(8,128)(2,1)S(1)}, bf16[256,1536]{1,0:T(8,128)(2,1)S(1)}, u32[]{:S(2)}, u32[]{:S(2)}) collective-permute-start(bf16[256,1536]{1,0:T(8,128)(2,1)S(1)} %copy-done.12), channel_id=1, source_target_pairs={{0,4},{12,8},{1,5},{13,9},{2,6},{14,10},{3,7},{15,11},{16,20},{28,... | collective-permute-start | bytes 2359304 | tf_op jit(solution)/shard_map/send1/ppermute | solution.py:312
  114.4 44.5 %collective-permute-start.11 = (bf16[256,2048]{1,0:T(8,128)(2,1)}, bf16[256,2048]{1,0:T(8,128)(2,1)}, u32[]{:S(2)}, u32[]{:S(2)}) collective-permute-start(bf16[256,2048]{1,0:T(8,128)(2,1)} %first2.1.refs_6_), channel_id=1, source_target_pairs={{0,4},{12,8},{1,5},{13,9},{2,6},{14,10},{3,7},{15,11},{16,20},{28,... | collective-permute-start | bytes 3145736 | tf_op jit(solution)/shard_map/send2/ppermute | solution.py:312
  127.5 47.2 %collective-permute-start.9 = (bf16[256,2048]{1,0:T(8,128)(2,1)}, bf16[256,2048]{1,0:T(8,128)(2,1)}, u32[]{:S(2)}, u32[]{:S(2)}) collective-permute-start(bf16[256,2048]{1,0:T(8,128)(2,1)} %first3.1.refs_4_), channel_id=1, source_target_pairs={{0,4},{12,8},{1,5},{13,9},{2,6},{14,10},{3,7},{15,11},{16,20},{28,... | collective-permute-start | bytes 3145736 | tf_op jit(solution)/shard_map/send3/ppermute | solution.py:312
  136.0 38.7 %collective-permute-start.10 = (bf16[256,1024]{1,0:T(8,128)(2,1)}, bf16[256,1024]{1,0:T(8,128)(2,1)}, u32[]{:S(2)}, u32[]{:S(2)}) collective-permute-start(bf16[256,1024]{1,0:T(8,128)(2,1)} %two0.1.refs_4_), channel_id=1, source_target_pairs={{4,8},{8,4},{5,9},{9,5},{6,10},{10,6},{7,11},{11,7},{20,24},{24,20... | collective-permute-start | bytes 1572872 | tf_op jit(solution)/shard_map/mid_two0/ppermute | solution.py:315
  146.1 39.6 %collective-permute-start.15 = (bf16[256,1536]{1,0:T(8,128)(2,1)}, bf16[256,1536]{1,0:T(8,128)(2,1)}, u32[]{:S(2)}, u32[]{:S(2)}) collective-permute-start(bf16[256,1536]{1,0:T(8,128)(2,1)} %two1.1), channel_id=1, source_target_pairs={{4,8},{8,4},{5,9},{9,5},{6,10},{10,6},{7,11},{11,7},{20,24},{24,20... | collective-permute-start | bytes 2359304 | tf_op jit(solution)/shard_map/mid_two1/ppermute | solution.py:315
  169.0 50.6 %collective-permute-start.13 = (bf16[256,2048]{1,0:T(8,128)(2,1)}, bf16[256,2048]{1,0:T(8,128)(2,1)}, u32[]{:S(2)}, u32[]{:S(2)}) collective-permute-start(bf16[256,2048]{1,0:T(8,128)(2,1)} %two2.1.refs_4_), channel_id=1, source_target_pairs={{4,8},{8,4},{5,9},{9,5},{6,10},{10,6},{7,11},{11,7},{20,24},{24,20... | collective-permute-start | bytes 3145736 | tf_op jit(solution)/shard_map/mid_two2/ppermute | solution.py:315
  170.7 22.4 %collective-permute-start.14 = (bf16[64,6656]{1,0:T(8,128)(2,1)S(1)}, bf16[64,6656]{1,0:T(8,128)(2,1)S(1)}, u32[]{:S(2)}, u32[]{:S(2)}) collective-permute-start(bf16[64,6656]{1,0:T(8,128)(2,1)S(1)} %fusion.1), channel_id=1, source_target_pairs={{0,4},{12,8},{1,5},{13,9},{2,6},{14,10},{3,7},{15,11},{16,20},{28,... | collective-permute-start | bytes 2555912 | tf_op jit(solution)/shard_map/send4/ppermute | solution.py:312
  181.4 38.3 %collective-permute-start.12 = (bf16[64,6656]{1,0:T(8,128)(2,1)S(1)}, bf16[64,6656]{1,0:T(8,128)(2,1)S(1)}, u32[]{:S(2)}, u32[]{:S(2)}) collective-permute-start(bf16[64,6656]{1,0:T(8,128)(2,1)S(1)} %copy-done.1), channel_id=1, source_target_pairs={{0,4},{12,8},{1,5},{13,9},{2,6},{14,10},{3,7},{15,11},{16,20},{28,... | collective-permute-start | bytes 2555912 | tf_op jit(solution)/shard_map/send5/ppermute | solution.py:312
  204.3 24.4 %collective-permute-start.17 = (bf16[256,2048]{1,0:T(8,128)(2,1)}, bf16[256,2048]{1,0:T(8,128)(2,1)S(1)}, u32[]{:S(2)}, u32[]{:S(2)}) collective-permute-start(bf16[256,2048]{1,0:T(8,128)(2,1)} %two3.1), channel_id=1, source_target_pairs={{4,8},{8,4},{5,9},{9,5},{6,10},{10,6},{7,11},{11,7},{20,24},{24,20... | collective-permute-start | bytes 3145736 | tf_op jit(solution)/shard_map/mid_two3/ppermute | solution.py:315
  205.2 22.7 %collective-permute-start.16 = (bf16[256,1024]{1,0:T(8,128)(2,1)}, bf16[256,1024]{1,0:T(8,128)(2,1)S(1)}, u32[]{:S(2)}, u32[]{:S(2)}) collective-permute-start(bf16[256,1024]{1,0:T(8,128)(2,1)} %two0.1.refs_4_), channel_id=1, source_target_pairs={{0,4},{12,8},{1,5},{13,9},{2,6},{14,10},{3,7},{15,11},{16,20},{28,... | collective-permute-start | bytes 1572872 | tf_op jit(solution)/shard_map/send6/ppermute | solution.py:312
  219.7 32.7 %collective-permute-start.20 = (bf16[256,1536]{1,0:T(8,128)(2,1)}, bf16[256,1536]{1,0:T(8,128)(2,1)}, u32[]{:S(2)}, u32[]{:S(2)}) collective-permute-start(bf16[256,1536]{1,0:T(8,128)(2,1)} %two1.1), channel_id=1, source_target_pairs={{0,4},{12,8},{1,5},{13,9},{2,6},{14,10},{3,7},{15,11},{16,20},{28,... | collective-permute-start | bytes 2359304 | tf_op jit(solution)/shard_map/send7/ppermute | solution.py:312
  227.1 42.5 %collective-permute-start.19 = (bf16[2,64,6656]{2,1,0:T(8,128)(2,1)}, bf16[2,64,6656]{2,1,0:T(8,128)(2,1)S(1)}, u32[]{:S(2)}, u32[]{:S(2)}) collective-permute-start(bf16[2,64,6656]{2,1,0:T(8,128)(2,1)} %far_terms.1.refs_4_), channel_id=1, source_target_pairs={{4,8},{8,4},{5,9},{9,5},{6,10},{10,6},{7,11},{11,7},{20,24},{24,20... | collective-permute-start | bytes 5111816 | tf_op jit(solution)/shard_map/far_terms/ppermute | solution.py:315
  228.7 40.8 %collective-permute-start.18 = (bf16[256,1024]{1,0:T(8,128)(2,1)}, bf16[256,1024]{1,0:T(8,128)(2,1)S(1)}, u32[]{:S(2)}, u32[]{:S(2)}) collective-permute-start(bf16[256,1024]{1,0:T(8,128)(2,1)} %one0.1.refs_4_), channel_id=1, source_target_pairs={{0,4},{12,8},{4,0},{8,12},{1,5},{13,9},{5,1},{9,13},{2,6},{14,10},... | collective-permute-start | bytes 1572872 | tf_op jit(solution)/shard_map/send8/ppermute | solution.py:321
  243.0 50.5 %collective-permute-start.25 = (bf16[256,1024]{1,0:T(8,128)(2,1)}, bf16[256,1024]{1,0:T(8,128)(2,1)S(1)}, u32[]{:S(2)}, u32[]{:S(2)}) collective-permute-start(bf16[256,1024]{1,0:T(8,128)(2,1)} %late0.1.refs_4_), channel_id=1, source_target_pairs={{4,8},{8,4},{5,9},{9,5},{6,10},{10,6},{7,11},{11,7},{20,24},{24,20... | collective-permute-start | bytes 1572872 | tf_op jit(solution)/shard_map/mid_late0/ppermute | solution.py:315
  261.1 65.9 %collective-permute-start.22 = (bf16[256,1536]{1,0:T(8,128)(2,1)}, bf16[256,1536]{1,0:T(8,128)(2,1)S(1)}, u32[]{:S(2)}, u32[]{:S(2)}) collective-permute-start(bf16[256,1536]{1,0:T(8,128)(2,1)} %late1.1), channel_id=1, source_target_pairs={{4,8},{8,4},{5,9},{9,5},{6,10},{10,6},{7,11},{11,7},{20,24},{24,20... | collective-permute-start | bytes 2359304 | tf_op jit(solution)/shard_map/mid_late1/ppermute | solution.py:315
  261.8 43.1 %collective-permute-start.24 = (bf16[256,2048]{1,0:T(8,128)(2,1)}, bf16[256,2048]{1,0:T(8,128)(2,1)}, u32[]{:S(2)}, u32[]{:S(2)}) collective-permute-start(bf16[256,2048]{1,0:T(8,128)(2,1)} %two2.1.refs_4_), channel_id=1, source_target_pairs={{0,4},{12,8},{1,5},{13,9},{2,6},{14,10},{3,7},{15,11},{16,20},{28,... | collective-permute-start | bytes 3145736 | tf_op jit(solution)/shard_map/send9/ppermute | solution.py:312
  275.2 74.4 %collective-permute-start.28 = (bf16[2,64,6656]{2,1,0:T(8,128)(2,1)}, bf16[2,64,6656]{2,1,0:T(8,128)(2,1)}, u32[]{:S(2)}, u32[]{:S(2)}) collective-permute-start(bf16[2,64,6656]{2,1,0:T(8,128)(2,1)} %last_terms.1), channel_id=1, source_target_pairs={{4,0},{8,12},{5,1},{9,13},{6,2},{10,14},{7,3},{11,15},{20,16},{24,... | collective-permute-start | bytes 5111816 | tf_op jit(solution)/shard_map/last_terms/ppermute | solution.py:318
  281.2 89.3 %collective-permute-start.26 = (bf16[2,64,6656]{2,1,0:T(8,128)(2,1)}, bf16[2,64,6656]{2,1,0:T(8,128)(2,1)}, u32[]{:S(2)}, u32[]{:S(2)}) collective-permute-start(bf16[2,64,6656]{2,1,0:T(8,128)(2,1)} %near_terms.1.refs_4_), channel_id=1, source_target_pairs={{4,8},{8,4},{5,9},{9,5},{6,10},{10,6},{7,11},{11,7},{20,24},{24,20... | collective-permute-start | bytes 5111816 | tf_op jit(solution)/shard_map/near_terms/ppermute | solution.py:315
  293.6 34.1 %collective-permute-start.21 = (bf16[256,2048]{1,0:T(8,128)(2,1)S(1)}, bf16[256,2048]{1,0:T(8,128)(2,1)S(1)}, u32[]{:S(2)}, u32[]{:S(2)}) collective-permute-start(bf16[256,2048]{1,0:T(8,128)(2,1)S(1)} %copy-done.33), channel_id=1, source_target_pairs={{0,4},{12,8},{1,5},{13,9},{2,6},{14,10},{3,7},{15,11},{16,20},{28,... | collective-permute-start | bytes 3145736 | tf_op jit(solution)/shard_map/send10/ppermute | solution.py:312
  315.2 68.1 %collective-permute-start.29 = (bf16[256,2048]{1,0:T(8,128)(2,1)}, bf16[256,2048]{1,0:T(8,128)(2,1)}, u32[]{:S(2)}, u32[]{:S(2)}) collective-permute-start(bf16[256,2048]{1,0:T(8,128)(2,1)} %late2.1.refs_4_), channel_id=1, source_target_pairs={{4,8},{8,4},{5,9},{9,5},{6,10},{10,6},{7,11},{11,7},{20,24},{24,20... | collective-permute-start | bytes 3145736 | tf_op jit(solution)/shard_map/mid_late2/ppermute | solution.py:315
  327.1 20.9 %collective-permute-start.27 = (bf16[256,1536]{1,0:T(8,128)(2,1)}, bf16[256,1536]{1,0:T(8,128)(2,1)}, u32[]{:S(2)}, u32[]{:S(2)}) collective-permute-start(bf16[256,1536]{1,0:T(8,128)(2,1)} %one1.1.refs_4_), channel_id=1, source_target_pairs={{0,4},{12,8},{4,0},{8,12},{1,5},{13,9},{5,1},{9,13},{2,6},{14,10},... | collective-permute-start | bytes 2359304 | tf_op jit(solution)/shard_map/send11/ppermute | solution.py:321
  327.6 42.8 %collective-permute-start.23 = (bf16[256,2048]{1,0:T(8,128)(2,1)}, bf16[256,2048]{1,0:T(8,128)(2,1)}, u32[]{:S(2)}, u32[]{:S(2)}) collective-permute-start(bf16[256,2048]{1,0:T(8,128)(2,1)} %one2.1.refs_4_), channel_id=1, source_target_pairs={{0,4},{12,8},{4,0},{8,12},{1,5},{13,9},{5,1},{9,13},{2,6},{14,10},... | collective-permute-start | bytes 3145736 | tf_op jit(solution)/shard_map/send12/ppermute | solution.py:321
  347.9 38.7 %collective-permute-start.30 = (bf16[256,2048]{1,0:T(8,128)(2,1)}, bf16[256,2048]{1,0:T(8,128)(2,1)}, u32[]{:S(2)}, u32[]{:S(2)}) collective-permute-start(bf16[256,2048]{1,0:T(8,128)(2,1)} %late3.1), channel_id=1, source_target_pairs={{4,8},{8,4},{5,9},{9,5},{6,10},{10,6},{7,11},{11,7},{20,24},{24,20... | collective-permute-start | bytes 3145736 | tf_op jit(solution)/shard_map/mid_late3/ppermute | solution.py:315
  349.6 37.1 %collective-permute-start.31 = (bf16[256,2048]{1,0:T(8,128)(2,1)}, bf16[256,2048]{1,0:T(8,128)(2,1)}, u32[]{:S(2)}, u32[]{:S(2)}) collective-permute-start(bf16[256,2048]{1,0:T(8,128)(2,1)} %one3.1.refs_4_), channel_id=1, source_target_pairs={{0,4},{12,8},{4,0},{8,12},{1,5},{13,9},{5,1},{9,13},{2,6},{14,10},... | collective-permute-start | bytes 3145736 | tf_op jit(solution)/shard_map/send13/ppermute | solution.py:321
  (46 other events, 444.1 us)
Sparse Core Ops, SparseCore 0:
  9.6 25.2 all-gather.11
  68.9 21.4 all-gather.5
  95.1 20.4 reduce-scatter.1
  117.1 20.8 all-gather.7
  139.4 22.9 all-gather.9
  219.8 92.5 all-reduce.2

commit v6 on v3

--- a/solution.py
+++ b/solution.py
@@ -12,6 +12,7 @@
 SCALE = 0.5
 SPLIT = ((0, 2), (2, 5), (5, 9), (9, 13))
 WINDOW = 2
+FULL = 5
 VMEM = 60 * 1024 * 1024
 ANY = pl.BlockSpec(memory_space=pl.ANY)
 SMEM = pl.BlockSpec(memory_space=pltpu.SMEM)
@@ -130,6 +131,37 @@
     )(index, *blocks, weight, *([arrived] if has_add else []), *deps)
 
 
+def pair_kernel(deps, one, other, weight, arrived_one, arrived_other, *refs):
+    out_one, out_other, batch = refs[deps:]
+    rows = one.shape[0]
+
+    @pl.when(pl.program_id(0) == 0)
+    def _():
+        batch[:rows, :] = one[...]
+        batch[rows:, :] = other[...]
+
+    value = jnp.dot(batch[...], weight[...], preferred_element_type=jnp.float32)
+    out_one[...] = (value[:rows] + arrived_one[...].astype(jnp.float32)).astype(jnp.bfloat16)
+    out_other[...] = (value[rows:] + arrived_other[...].astype(jnp.float32)).astype(jnp.bfloat16)
+
+
+def pair(one, other, weight, piece, arrived_one, arrived_other, deps):
+    rows, depth = one.shape
+    tile = tile_of(weight.shape[1])
+    first, count = piece
+    column = pl.BlockSpec((rows, tile), lambda i: (0, i))
+    whole = pl.BlockSpec((rows, depth), lambda i: (0, 0))
+    return call(
+        functools.partial(pair_kernel, len(deps)),
+        4 * rows * depth * count * tile,
+        out_shape=[jax.ShapeDtypeStruct((rows, count * tile), jnp.bfloat16)] * 2,
+        grid=(count,),
+        in_specs=[whole, whole, pl.BlockSpec((depth, tile), lambda i: (0, first + i)), column, column] + [ANY] * len(deps),
+        out_specs=[column] * 2,
+        scratch_shapes=[pltpu.VMEM((2 * rows, depth), jnp.bfloat16)],
+    )(one, other, weight, arrived_one, arrived_other, *deps)
+
+
 def forward_kernel(count, deps, ids, *refs):
     blocks, down, outs = refs[:count], refs[count], refs[count + 1 + deps :]
     slices, _, _, width = down.shape
@@ -352,6 +384,15 @@
     def add_one(j):
         ones[j] = piece_of("one", rows_one, j, mid1[j])
 
+    def add_pair(j):
+        with jax.named_scope(f"pair{j}"):
+            deps = [held.now for held in (*slot_gate, *work[-1:])]
+            lates[j], ones[j] = map(
+                Held, pair(rows_late[0][1], rows_one[0][1], up_weight, pieces[j], step1[j].now, mid1[j].now, deps)
+            )
+            work.append(lates[j])
+            mid2[j] = Held(middle_hop(lates[j].now))
+
     firsts[0] = piece_of("first", rows_first, 0)
     with jax.named_scope("two_rows"):
         two = late_use(two)
@@ -457,10 +498,9 @@
 
     step2[0] = slot(ones[0], first_and_last_hop)
     add_late(0)
-    add_one(1)
 
     step1[2] = slot(twos[2])
-    add_late(1)
+    add_pair(1)
     pin(far_terms)
     with jax.named_scope("last_terms"):
         unit = jnp.ones((OWN_MAX,), jnp.float32)
@@ -472,16 +512,14 @@
         near_sums = do(combine(late_use(near_hits), terms(), jnp.bfloat16))
         near_terms = Held(middle_hop(near_sums.now))
     pin(mid2[0])
-    add_one(2)
 
     step2[1] = slot(ones[1], first_and_last_hop)
     pin(mid2[1])
-    add_late(2)
-    add_one(3)
+    add_pair(2)
 
     step2[2] = slot(ones[2], first_and_last_hop)
     pin(last_terms)
-    add_late(3)
+    add_pair(3)
     backs = (SCALE * late_use(back_full)).astype(jnp.bfloat16)
     backs = [lax.dynamic_index_in_dim(backs, order[n], 0, keepdims=False) for n in range(dp_count)]
     grad_down = do(

time: 396 us -> 393 us (level)
  Pallas kernels: 175 us -> 157 us
  waiting for transfers between devices: 80.4 us -> 94.3 us
  starting transfers between devices: 75.3 us -> 82.6 us
  local copies, waits for them, and re-layouts: 16.8 us -> 12.1 us
    pallas_call x16 -> x10, Pallas kernels: 142 us -> 83.7 us  [share(): call(functools.partial(share_kernel, masks, has_add, len(deps)), 2 * batc...]
    pallas_call x0 -> x3, Pallas kernels: none -> 40.8 us  [pair(): call(functools.partial(pair_kernel, len(deps)), 4 * rows * depth * count...]
    ppermute x4, waiting for transfers between devices: 22.8 us -> 37.9 us  [first_and_last_hop(): return lax.ppermute(value, 'dp', [(0, 1), (3, 2), (1, 0), (2, 3)])]
    ppermute x4, starting transfers between devices: 7.07 us -> 13.1 us  [first_and_last_hop(): return lax.ppermute(value, 'dp', [(0, 1), (3, 2), (1, 0), (2, 3)])]
    ppermute x1, starting transfers between devices: 6.95 us -> 1.91 us  [local(): far = lax.ppermute(block_for(z ^ 3), 'dp', [(0, 3), (3, 0)])]
    ppermute x5, starting transfers between devices: 2.26 us -> 7.24 us  [across(): return lax.ppermute(value, axis, [(i, i ^ bit) for i in range(count)])]
    unnamed x78 -> x74, local copies, waits for them, and re-layouts: 9.54 us -> 4.94 us
  transfers between devices with their start and end apart: 38 -> 38, of which waited for: 10 -> 10; matrix products, arithmetic and copies ran while one was open for 7% -> 6% of each run, Pallas kernels for 44% -> 40%
where the time goes in v6:
time: 393 us; the launch traced here: 392 us
  Pallas kernels  157 us (40%)
  waiting for transfers between devices  94.3 us (24%)
  starting transfers between devices  82.6 us (21%)
  other arithmetic  17.4 us (4%)
  between operations  14.8 us (4%)
  local copies, waits for them, and re-layouts  12.1 us (3%)
  matrix products  7.04 us (2%)
  blocking collectives  5.81 us (1%)
    pallas_call x10, Pallas kernels, share(): call(functools.partial(share_kernel, masks, has_add, len(deps)), 2 * batc...  83.7 us
    ppermute x10, starting transfers between devices, first_hop(): return lax.ppermute(value, 'dp', [(0, 1), (3, 2)])  43.8 us
    pallas_call x3, Pallas kernels, pair(): call(functools.partial(pair_kernel, len(deps)), 4 * rows * depth * count...  40.8 us
    ppermute x4, waiting for transfers between devices, first_and_last_hop(): return lax.ppermute(value, 'dp', [(0, 1), (3, 2), (1, 0), (2, 3)])  37.9 us
    ppermute x5, waiting for transfers between devices, across(): return lax.ppermute(value, axis, [(i, i ^ bit) for i in range(count)])  35.3 us
    pallas_call x4, Pallas kernels, combine(): call(functools.partial(combine_kernel, len(terms), len(extras)), 4 * slot...  19.8 us
    ppermute x11, starting transfers between devices, middle_hop(): return lax.ppermute(value, 'dp', [(1, 2), (2, 1)])  15.1 us
    ppermute x1, waiting for transfers between devices, local(): far = lax.ppermute(block_for(z ^ 3), 'dp', [(0, 3), (3, 0)])  13.1 us
  transfers between devices with their start and end apart: 38, of which 10 were waited for; matrix products, arithmetic and copies ran while one was open for 6% of the time, Pallas kernels for 40%

profile of v6, /device:TPU:0, one launch (start us, length us, event | category | flops | bytes accessed | tf_op | source)
XLA Modules:
  0.0 391.6 jit_solution(8101137984545206)
XLA Ops:
  17.2 19.0 %collective-permute-done.2.refs_2_ = bf16[64,4096]{1,0:T(8,128)(2,1)} collective-permute-done((bf16[64,4096]{1,0:T(8,128)(2,1)}, bf16[64,4096]{1,0:T(8,128)(2,1)}, u32[]{:S(2)}, u32[]{:S(2)}) %collective-permute-start.2) | collective-permute-done | bytes 524320 | tf_op jit(solution)/shard_map/ppermute | solution.py:38
  36.5 13.1 %collective-permute-done = bf16[64,4096]{1,0:T(8,128)(2,1)} collective-permute-done((bf16[64,4096]{1,0:T(8,128)(2,1)S(1)}, bf16[64,4096]{1,0:T(8,128)(2,1)}, u32[]{:S(2)}, u32[]{:S(2)}) %collective-permute-start) | collective-permute-done | bytes 524320 | tf_op jit(solution)/shard_map/ppermute | solution.py:330
  52.5 15.3 %collective-permute-done.4.refs_1_.refs_5_ = bf16[64,4096]{1,0:T(8,128)(2,1)} collective-permute-done((bf16[64,4096]{1,0:T(8,128)(2,1)S(1)}, bf16[64,4096]{1,0:T(8,128)(2,1)}, u32[]{:S(2)}, u32[]{:S(2)}) %collective-permute-start.4) | collective-permute-done | bytes 524320 | tf_op jit(solution)/shard_map/ppermute | solution.py:38
  70.3 6.3 %first0.1.refs_5_ = bf16[256,1024]{1,0:T(8,128)(2,1)} custom-call(s32[1]{0:T(128)} %bitcast.index, bf16[64,4096]{1,0:T(8,128)(2,1)} %copy-done.14, bf16[64,4096]{1,0:T(8,128)(2,1)} %collective-permute-done.4.refs_1_.refs_5_, bf16[64,4096]{1,0:T(8,128)(2,1)} %copy-done.33, bf16[64,4096]{1,0:T(8,128)(2,1)} %collective-permute-done.6.refs_3_.refs_7_, ...), custom_call_target="tpu_custom_call" | custom-call | flops 21474836480 | tf_op jit(solution)/shard_map/first0/pallas_call | solution.py:117
  78.8 8.6 %first1.1.refs_6_ = bf16[256,1536]{1,0:T(8,128)(2,1)} custom-call(s32[1]{0:T(128)} %bitcast.index, bf16[64,4096]{1,0:T(8,128)(2,1)} %copy-done.14, bf16[64,4096]{1,0:T(8,128)(2,1)} %collective-permute-done.4.refs_1_.refs_5_, bf16[64,4096]{1,0:T(8,128)(2,1)} %copy-done.33, bf16[64,4096]{1,0:T(8,128)(2,1)} %collective-permute-done.6.refs_3_.refs_7_, ...), custom_call_target="tpu_custom_call" | custom-call | flops 32212254720 | tf_op jit(solution)/shard_map/first1/pallas_call | solution.py:117
  92.1 10.3 %first2.1 = bf16[256,2048]{1,0:T(8,128)(2,1)} custom-call(s32[1]{0:T(128)} %bitcast.index, bf16[64,4096]{1,0:T(8,128)(2,1)} %copy-done.14, bf16[64,4096]{1,0:T(8,128)(2,1)} %collective-permute-done.4.refs_1_.refs_5_, bf16[64,4096]{1,0:T(8,128)(2,1)} %copy-done.33, bf16[64,4096]{1,0:T(8,128)(2,1)} %collective-permute-done.6.refs_3_.refs_7_, ...), custom_call_target="tpu_custom_call" | custom-call | flops 42949672960 | tf_op jit(solution)/shard_map/first2/pallas_call | solution.py:117
  102.4 4.9 %collective-permute-done.7.refs_2_.refs_3_ = bf16[256,1536]{1,0:T(8,128)(2,1)} collective-permute-done((bf16[256,1536]{1,0:T(8,128)(2,1)}, bf16[256,1536]{1,0:T(8,128)(2,1)}, u32[]{:S(2)}, u32[]{:S(2)}) %collective-permute-start.7) | collective-permute-done | bytes 786464 | tf_op jit(solution)/shard_map/send1/ppermute | solution.py:315
  117.3 5.4 %collective-permute-start.11 = (bf16[256,2048]{1,0:T(8,128)(2,1)}, bf16[256,2048]{1,0:T(8,128)(2,1)}, u32[]{:S(2)}, u32[]{:S(2)}) collective-permute-start(bf16[256,2048]{1,0:T(8,128)(2,1)} %first2.1), channel_id=1, source_target_pairs={{0,4},{12,8},{1,5},{13,9},{2,6},{14,10},{3,7},{15,11},{16,20},{28,... | collective-permute-start | bytes 3145736 | tf_op jit(solution)/shard_map/send2/ppermute | solution.py:315
  122.7 10.3 %first3.1.refs_4_ = bf16[256,2048]{1,0:T(8,128)(2,1)} custom-call(s32[1]{0:T(128)} %bitcast.index, bf16[64,4096]{1,0:T(8,128)(2,1)} %copy-done.14, bf16[64,4096]{1,0:T(8,128)(2,1)} %collective-permute-done.4.refs_1_.refs_5_, bf16[64,4096]{1,0:T(8,128)(2,1)} %copy-done.33, bf16[64,4096]{1,0:T(8,128)(2,1)} %collective-permute-done.6.refs_3_.refs_7_, ...), custom_call_target="tpu_custom_call" | custom-call | flops 42949672960 | tf_op jit(solution)/shard_map/first3/pallas_call | solution.py:117
  135.3 6.2 %two0.1.refs_4_ = bf16[256,1024]{1,0:T(8,128)(2,1)} custom-call(s32[1]{0:T(128)} %bitcast.index, bf16[256,4096]{1,0:T(8,128)(2,1)} %all-gather.6.cloned.1.call-done.refs_0_.refs_8_, bf16[4096,6656]{1,0:T(8,128)(2,1)} %weight.5, bf16[256,1024]{1,0:T(8,128)(2,1)} %collective-permute-done.8.refs_5_.refs_2_.refs_3_, ...), custom_call_target="tpu_custom_call" | custom-call | flops 21474836480 | tf_op jit(solution)/shard_map/two0/pallas_call | solution.py:117
  143.0 8.8 %two1.1 = bf16[256,1536]{1,0:T(8,128)(2,1)} custom-call(s32[1]{0:T(128)} %bitcast.index, bf16[256,4096]{1,0:T(8,128)(2,1)} %all-gather.6.cloned.1.call-done.refs_0_.refs_8_, bf16[4096,6656]{1,0:T(8,128)(2,1)} %weight.5, bf16[256,1536]{1,0:T(8,128)(2,1)} %collective-permute-done.7.refs_2_.refs_3_, bf16[256,1536]{1,0:T(8,128)(2,1)} %collective-permute-done.7.refs_2_.refs_3_, ...), custom_call_target="tpu_custom_call" | custom-call | flops 32212254720 | tf_op jit(solution)/shard_map/two1/pallas_call | solution.py:117
  153.3 5.8 %all_gather.21 = bf16[256,64]{1,0:T(8,128)(2,1)S(1)} all-gather(bf16[64,64]{1,0:T(8,128)(2,1)S(1)} %convert_element_type.76), channel_id=1, replica_groups=mesh['groups'=2,'dp'=4,'tensor'=4] {'tensor'}, dimensions={0}, use_global_device_ids=true | all-gather | bytes 40960 | tf_op jit(solution)/shard_map/projected/all_gather | solution.py:436
  165.9 10.6 %two2.1.refs_4_ = bf16[256,2048]{1,0:T(8,128)(2,1)} custom-call(s32[1]{0:T(128)} %bitcast.index, bf16[256,4096]{1,0:T(8,128)(2,1)} %all-gather.6.cloned.1.call-done.refs_0_.refs_8_, bf16[4096,6656]{1,0:T(8,128)(2,1)} %weight.5, bf16[256,2048]{1,0:T(8,128)(2,1)} %collective-permute-done.11.refs_2_.refs_3_, ...), custom_call_target="tpu_custom_call" | custom-call | flops 42949672960 | tf_op jit(solution)/shard_map/two2/pallas_call | solution.py:117
  179.8 10.2 %two3.1.refs_4_ = bf16[256,2048]{1,0:T(8,128)(2,1)} custom-call(s32[1]{0:T(128)} %bitcast.index, bf16[256,4096]{1,0:T(8,128)(2,1)} %all-gather.6.cloned.1.call-done.refs_0_.refs_8_, bf16[4096,6656]{1,0:T(8,128)(2,1)} %weight.5, bf16[256,2048]{1,0:T(8,128)(2,1)} %collective-permute-done.9.refs_2_.refs_3_, ...), custom_call_target="tpu_custom_call" | custom-call | flops 42949672960 | tf_op jit(solution)/shard_map/two3/pallas_call | solution.py:117
  194.9 4.4 %collective-permute-start.17 = (bf16[256,1024]{1,0:T(8,128)(2,1)}, bf16[256,1024]{1,0:T(8,128)(2,1)}, u32[]{:S(2)}, u32[]{:S(2)}) collective-permute-start(bf16[256,1024]{1,0:T(8,128)(2,1)} %two0.1.refs_4_), channel_id=1, source_target_pairs={{0,4},{12,8},{1,5},{13,9},{2,6},{14,10},{3,7},{15,11},{16,20},{28,... | collective-permute-start | bytes 1572872 | tf_op jit(solution)/shard_map/send6/ppermute | solution.py:315
  199.2 6.2 %one0.1 = bf16[256,1024]{1,0:T(8,128)(2,1)} custom-call(s32[1]{0:T(128)} %bitcast.index, bf16[256,4096]{1,0:T(8,128)(2,1)} %all-gather.10.cloned.1.call-done.refs_0_.other.refs_9_, bf16[4096,6656]{1,0:T(8,128)(2,1)} %weight.5, bf16[256,1024]{1,0:T(8,128)(2,1)} %collective-permute-done.10.refs_2_, bf16[64,6656]{1,0:T(8,128)(2,1)} %copy-done.2, ...), custom_call_target="tpu_custom_call" | custom-call | flops 21474836480 | tf_op jit(solution)/shard_map/one0/pallas_call | solution.py:117
  205.5 5.7 %shard_map.94 = f32[256,64]{1,0:T(8,128)} custom-call(s32[2]{0:T(128)} %fusion.28.ids, bf16[256,6656]{1,0:T(8,128)(2,1)} %grad.1, bf16[4,64,6656]{2,1,0:T(8,128)(2,1)} %up.1), custom_call_target="tpu_custom_call" | custom-call | flops 8724152320 | tf_op jit(solution)/shard_map/pallas_call | solution.py:209
  215.8 4.7 %far_terms.1.refs_4_ = bf16[2,64,6656]{2,1,0:T(8,128)(2,1)} custom-call(f32[2,4]{1,0:T(2,128)} %add_convert_fusion.4.weights, f32[2]{0:T(128)} %broadcast_16_scale.2.scale, bf16[1,64,6656]{2,1,0:T(8,128)(2,1)} %bitcast.54, bf16[1,64,6656]{2,1,0:T(8,128)(2,1)} %bitcast.50, bf16[1,64,6656]{2,1,0:T(8,128)(2,1)} %bitcast.58, bf16[1,64,6656]{2,1,0:T(8,128)(2,1)} %bitcast.61), custom_call_target="tpu_custom_call" | custom-call | flops 136314880 | tf_op jit(solution)/shard_map/far_terms/pallas_call | solution.py:284
  221.3 6.5 %collective-permute-start.21 = (bf16[256,1024]{1,0:T(8,128)(2,1)S(1)}, bf16[256,1024]{1,0:T(8,128)(2,1)S(1)}, u32[]{:S(2)}, u32[]{:S(2)}) collective-permute-start(bf16[256,1024]{1,0:T(8,128)(2,1)S(1)} %copy-done.34), channel_id=1, source_target_pairs={{0,4},{12,8},{4,0},{8,12},{1,5},{13,9},{5,1},{9,13},{2,6},{14,10},... | collective-permute-start | bytes 1572872 | tf_op jit(solution)/shard_map/send8/ppermute | solution.py:324
  227.8 6.2 %late0.1.refs_1_ = bf16[256,1024]{1,0:T(8,128)(2,1)} custom-call(s32[1]{0:T(128)} %bitcast.index, bf16[256,4096]{1,0:T(8,128)(2,1)} %all-gather.8.cloned.1.call-done.refs_0_.one.refs_10_, bf16[4096,6656]{1,0:T(8,128)(2,1)} %weight.5, bf16[256,1024]{1,0:T(8,128)(2,1)} %collective-permute-done.17.refs_2_.refs_3_, ...), custom_call_target="tpu_custom_call" | custom-call | flops 21474836480 | tf_op jit(solution)/shard_map/late0/pallas_call | solution.py:117
  237.2 5.4 %collective-permute-start.19 = (bf16[256,2048]{1,0:T(8,128)(2,1)}, bf16[256,2048]{1,0:T(8,128)(2,1)}, u32[]{:S(2)}, u32[]{:S(2)}) collective-permute-start(bf16[256,2048]{1,0:T(8,128)(2,1)} %two2.1.refs_4_), channel_id=1, source_target_pairs={{0,4},{12,8},{1,5},{13,9},{2,6},{14,10},{3,7},{15,11},{16,20},{28,... | collective-permute-start | bytes 3145736 | tf_op jit(solution)/shard_map/send9/ppermute | solution.py:315
  242.6 12.0 %pair1.1 = (bf16[256,1536]{1,0:T(8,128)(2,1)}, bf16[256,1536]{1,0:T(8,128)(2,1)}) custom-call(bf16[256,4096]{1,0:T(8,128)(2,1)} %all-gather.8.cloned.1.call-done.refs_0_.one.refs_10_, bf16[256,4096]{1,0:T(8,128)(2,1)} %all-gather.10.cloned.1.call-done.refs_0_.other.refs_9_, bf16[4096,6656]{1,0:T(8,128)(2,1)} %weight.5, ...), custom_call_target="tpu_custom_call" | custom-call | flops 64424509440 | tf_op jit(solution)/shard_map/pair1/pallas_call | solution.py:154
  255.4 15.2 %collective-permute-start.23 = (bf16[256,2048]{1,0:T(8,128)(2,1)}, bf16[256,2048]{1,0:T(8,128)(2,1)}, u32[]{:S(2)}, u32[]{:S(2)}) collective-permute-start(bf16[256,2048]{1,0:T(8,128)(2,1)} %two3.1.refs_4_), channel_id=1, source_target_pairs={{0,4},{12,8},{1,5},{13,9},{2,6},{14,10},{3,7},{15,11},{16,20},{28,... | collective-permute-start | bytes 3145736 | tf_op jit(solution)/shard_map/send10/ppermute | solution.py:315
  270.6 4.4 %last_terms.1 = bf16[2,64,6656]{2,1,0:T(8,128)(2,1)} custom-call(f32[2,2]{1,0:T(2,128)} %get-tuple-element.149.weights, f32[2]{0:T(128)} %broadcast_16_scale.2.scale, bf16[1,64,6656]{2,1,0:T(8,128)(2,1)} %bitcast.55, bf16[1,64,6656]{2,1,0:T(8,128)(2,1)} %bitcast.51, bf16[2,64,6656]{2,1,0:T(8,128)(2,1)} %copy-done.7), custom_call_target="tpu_custom_call" | custom-call | flops 68157440 | tf_op jit(solution)/shard_map/last_terms/pallas_call | solution.py:284
  276.3 4.7 %near_terms.1.refs_1_ = bf16[2,64,6656]{2,1,0:T(8,128)(2,1)} custom-call(f32[2,4]{1,0:T(2,128)} %add_convert_fusion.5.weights, f32[2]{0:T(128)} %broadcast_16_scale.2.scale, bf16[1,64,6656]{2,1,0:T(8,128)(2,1)} %bitcast.56, bf16[1,64,6656]{2,1,0:T(8,128)(2,1)} %bitcast.52, bf16[1,64,6656]{2,1,0:T(8,128)(2,1)} %bitcast.59, bf16[1,64,6656]{2,1,0:T(8,128)(2,1)} %bitcast.62), custom_call_target="tpu_custom_call" | custom-call | flops 136314880 | tf_op jit(solution)/shard_map/near_terms/pallas_call | solution.py:284
  282.9 4.0 %collective-permute-start.27 = (bf16[256,1536]{1,0:T(8,128)(2,1)}, bf16[256,1536]{1,0:T(8,128)(2,1)}, u32[]{:S(2)}, u32[]{:S(2)}) collective-permute-start(bf16[256,1536]{1,0:T(8,128)(2,1)} %get-tuple-element.162), channel_id=1, source_target_pairs={{0,4},{12,8},{4,0},{8,12},{1,5},{13,9},{5,1},{9,13},{2,6},{14,10},... | collective-permute-start | bytes 2359304 | tf_op jit(solution)/shard_map/send11/ppermute | solution.py:324
  286.9 14.4 %pair2.1 = (bf16[256,2048]{1,0:T(8,128)(2,1)}, bf16[256,2048]{1,0:T(8,128)(2,1)}) custom-call(bf16[256,4096]{1,0:T(8,128)(2,1)} %all-gather.8.cloned.1.call-done.refs_0_.one.refs_10_, bf16[256,4096]{1,0:T(8,128)(2,1)} %all-gather.10.cloned.1.call-done.refs_0_.other.refs_9_, bf16[4096,6656]{1,0:T(8,128)(2,1)} %weight.5, ...), custom_call_target="tpu_custom_call" | custom-call | flops 85899345920 | tf_op jit(solution)/shard_map/pair2/pallas_call | solution.py:154
  305.3 14.4 %pair3.1 = (bf16[256,2048]{1,0:T(8,128)(2,1)}, bf16[256,2048]{1,0:T(8,128)(2,1)}) custom-call(bf16[256,4096]{1,0:T(8,128)(2,1)} %all-gather.8.cloned.1.call-done.refs_0_.one.refs_10_, bf16[256,4096]{1,0:T(8,128)(2,1)} %all-gather.10.cloned.1.call-done.refs_0_.other.refs_9_, bf16[4096,6656]{1,0:T(8,128)(2,1)} %weight.5, ...), custom_call_target="tpu_custom_call" | custom-call | flops 85899345920 | tf_op jit(solution)/shard_map/pair3/pallas_call | solution.py:154
  325.5 12.2 %collective-permute-done.27 = bf16[256,1536]{1,0:T(8,128)(2,1)} collective-permute-done((bf16[256,1536]{1,0:T(8,128)(2,1)}, bf16[256,1536]{1,0:T(8,128)(2,1)}, u32[]{:S(2)}, u32[]{:S(2)}) %collective-permute-start.27) | collective-permute-done | bytes 786464 | tf_op jit(solution)/shard_map/send11/ppermute | solution.py:324
  339.5 20.7 %collective-permute-done.25 = bf16[256,2048]{1,0:T(8,128)(2,1)} collective-permute-done((bf16[256,2048]{1,0:T(8,128)(2,1)}, bf16[256,2048]{1,0:T(8,128)(2,1)}, u32[]{:S(2)}, u32[]{:S(2)}) %collective-permute-start.25) | collective-permute-done | bytes 1048608 | tf_op jit(solution)/shard_map/send12/ppermute | solution.py:324
  360.2 6.0 %shard_map.96 = f32[2,64,6656]{2,1,0:T(8,128)} custom-call(f32[2,4]{1,0:T(2,128)} %add_select_fusion.weights, f32[2]{0:T(128)} %copy-done.23, bf16[1,64,6656]{2,1,0:T(8,128)(2,1)} %bitcast.57, bf16[1,64,6656]{2,1,0:T(8,128)(2,1)} %bitcast.53, bf16[1,64,6656]{2,1,0:T(8,128)(2,1)} %bitcast.60, bf16[1,64,6656]{2,1,0:T(8,128)(2,1)} %bitcast.63, ...), custom_call_target="tpu_custom_call" | custom-call | flops 136314880 | tf_op jit(solution)/shard_map/pallas_call | solution.py:284
  375.3 5.0 %collective-permute-done.31 = bf16[256,2048]{1,0:T(8,128)(2,1)} collective-permute-done((bf16[256,2048]{1,0:T(8,128)(2,1)}, bf16[256,2048]{1,0:T(8,128)(2,1)}, u32[]{:S(2)}, u32[]{:S(2)}) %collective-permute-start.31) | collective-permute-done | bytes 1048608 | tf_op jit(solution)/shard_map/send13/ppermute | solution.py:324
  (194 shorter events, 90.0 us)
Async XLA Ops:
  7.2 100.1 %all-gather.12.cloned.1.call-start = ((), (), s32[]{:S(2)}) async-start(), calls=%async_computation.6 | async-start | bytes 2621440 | tf_op jit(solution)/shard_map/all_gather | solution.py:329
  9.7 26.5 %collective-permute-start.2 = (bf16[64,4096]{1,0:T(8,128)(2,1)}, bf16[64,4096]{1,0:T(8,128)(2,1)}, u32[]{:S(2)}, u32[]{:S(2)}) collective-permute-start(bf16[64,4096]{1,0:T(8,128)(2,1)} %get-tuple-element.181), channel_id=1, source_target_pairs={{0,4},{4,0},{8,12},{12,8},{1,5},{5,1},{9,13},{13,9},{2,6},{6,2},{1... | collective-permute-start | bytes 1572872 | tf_op jit(solution)/shard_map/ppermute | solution.py:38
  12.7 23.8 %collective-permute-start.1 = (bf16[64,4096]{1,0:T(8,128)(2,1)S(1)}, bf16[64,4096]{1,0:T(8,128)(2,1)}, u32[]{:S(2)}, u32[]{:S(2)}) collective-permute-start(bf16[64,4096]{1,0:T(8,128)(2,1)S(1)} %get-tuple-element.182), channel_id=1, source_target_pairs={{0,8},{4,12},{8,0},{12,4},{1,9},{5,13},{9,1},{13,5},{2,10},{6,14},... | collective-permute-start | bytes 1572872 | tf_op jit(solution)/shard_map/ppermute | solution.py:38
  15.3 34.3 %collective-permute-start = (bf16[64,4096]{1,0:T(8,128)(2,1)S(1)}, bf16[64,4096]{1,0:T(8,128)(2,1)}, u32[]{:S(2)}, u32[]{:S(2)}) collective-permute-start(bf16[64,4096]{1,0:T(8,128)(2,1)S(1)} %get-tuple-element.92), channel_id=1, source_target_pairs={{0,12},{12,0},{1,13},{13,1},{2,14},{14,2},{3,15},{15,3},{16,28},{2... | collective-permute-start | bytes 1572872 | tf_op jit(solution)/shard_map/ppermute | solution.py:330
  52.3 83.0 %all-gather.6.cloned.1.call-start = ((), (), s32[]{:S(2)}) async-start(), calls=%async_computation.2 | async-start | bytes 2621440 | tf_op jit(solution)/shard_map/two_rows/all_gather | solution.py:327
  89.7 53.2 %reduce-scatter.2.cloned.1.call-start = ((), (), s32[]{:S(2)}) async-start(), calls=%async_computation.1 | async-start | bytes 163840 | tf_op jit(solution)/shard_map/forward/reduce_scatter | solution.py:427
  112.5 86.8 %all-gather.10.cloned.1.call-start = ((), (), s32[]{:S(2)}) async-start(), calls=%async_computation.4 | async-start | bytes 2621440 | tf_op jit(solution)/shard_map/one_rows/all_gather | solution.py:327
  113.1 114.7 %all-gather.8.cloned.1.call-start = ((), (), s32[]{:S(2)}) async-start(), calls=%async_computation.3 | async-start | bytes 2621440 | tf_op jit(solution)/shard_map/late_rows/all_gather | solution.py:327
  117.3 202.5 %all-reduce.3.cloned.1.call-start = ((), (), s32[]{:S(2)}) async-start(), calls=%async_computation.5 | async-start | bytes 1048576 | tf_op jit(solution)/shard_map/back_proj/psum | solution.py:487
  117.3 45.7 %collective-permute-start.11 = (bf16[256,2048]{1,0:T(8,128)(2,1)}, bf16[256,2048]{1,0:T(8,128)(2,1)}, u32[]{:S(2)}, u32[]{:S(2)}) collective-permute-start(bf16[256,2048]{1,0:T(8,128)(2,1)} %first2.1), channel_id=1, source_target_pairs={{0,4},{12,8},{1,5},{13,9},{2,6},{14,10},{3,7},{15,11},{16,20},{28,... | collective-permute-start | bytes 3145736 | tf_op jit(solution)/shard_map/send2/ppermute | solution.py:315
  133.0 45.2 %collective-permute-start.9 = (bf16[256,2048]{1,0:T(8,128)(2,1)}, bf16[256,2048]{1,0:T(8,128)(2,1)}, u32[]{:S(2)}, u32[]{:S(2)}) collective-permute-start(bf16[256,2048]{1,0:T(8,128)(2,1)} %first3.1.refs_4_), channel_id=1, source_target_pairs={{0,4},{12,8},{1,5},{13,9},{2,6},{14,10},{3,7},{15,11},{16,20},{28,... | collective-permute-start | bytes 3145736 | tf_op jit(solution)/shard_map/send3/ppermute | solution.py:315
  141.5 36.6 %collective-permute-start.10 = (bf16[256,1024]{1,0:T(8,128)(2,1)}, bf16[256,1024]{1,0:T(8,128)(2,1)}, u32[]{:S(2)}, u32[]{:S(2)}) collective-permute-start(bf16[256,1024]{1,0:T(8,128)(2,1)} %two0.1.refs_4_), channel_id=1, source_target_pairs={{4,8},{8,4},{5,9},{9,5},{6,10},{10,6},{7,11},{11,7},{20,24},{24,20... | collective-permute-start | bytes 1572872 | tf_op jit(solution)/shard_map/mid_two0/ppermute | solution.py:318
  151.8 43.1 %collective-permute-start.13 = (bf16[256,1536]{1,0:T(8,128)(2,1)}, bf16[256,1536]{1,0:T(8,128)(2,1)}, u32[]{:S(2)}, u32[]{:S(2)}) collective-permute-start(bf16[256,1536]{1,0:T(8,128)(2,1)} %two1.1), channel_id=1, source_target_pairs={{4,8},{8,4},{5,9},{9,5},{6,10},{10,6},{7,11},{11,7},{20,24},{24,20... | collective-permute-start | bytes 2359304 | tf_op jit(solution)/shard_map/mid_two1/ppermute | solution.py:318
  163.1 31.8 %collective-permute-start.12 = (bf16[64,6656]{1,0:T(8,128)(2,1)S(1)}, bf16[64,6656]{1,0:T(8,128)(2,1)S(1)}, u32[]{:S(2)}, u32[]{:S(2)}) collective-permute-start(bf16[64,6656]{1,0:T(8,128)(2,1)S(1)} %fusion.1), channel_id=1, source_target_pairs={{0,4},{12,8},{1,5},{13,9},{2,6},{14,10},{3,7},{15,11},{16,20},{28,... | collective-permute-start | bytes 2555912 | tf_op jit(solution)/shard_map/send4/ppermute | solution.py:315
  176.5 36.5 %collective-permute-start.15 = (bf16[256,2048]{1,0:T(8,128)(2,1)}, bf16[256,2048]{1,0:T(8,128)(2,1)}, u32[]{:S(2)}, u32[]{:S(2)}) collective-permute-start(bf16[256,2048]{1,0:T(8,128)(2,1)} %two2.1.refs_4_), channel_id=1, source_target_pairs={{4,8},{8,4},{5,9},{9,5},{6,10},{10,6},{7,11},{11,7},{20,24},{24,20... | collective-permute-start | bytes 3145736 | tf_op jit(solution)/shard_map/mid_two2/ppermute | solution.py:318
  178.1 34.9 %collective-permute-start.14 = (bf16[64,6656]{1,0:T(8,128)(2,1)S(1)}, bf16[64,6656]{1,0:T(8,128)(2,1)S(1)}, u32[]{:S(2)}, u32[]{:S(2)}) collective-permute-start(bf16[64,6656]{1,0:T(8,128)(2,1)S(1)} %copy-done), channel_id=1, source_target_pairs={{0,4},{12,8},{1,5},{13,9},{2,6},{14,10},{3,7},{15,11},{16,20},{28,... | collective-permute-start | bytes 2555912 | tf_op jit(solution)/shard_map/send5/ppermute | solution.py:315
  190.0 31.2 %collective-permute-start.18 = (bf16[256,2048]{1,0:T(8,128)(2,1)}, bf16[256,2048]{1,0:T(8,128)(2,1)}, u32[]{:S(2)}, u32[]{:S(2)}) collective-permute-start(bf16[256,2048]{1,0:T(8,128)(2,1)} %two3.1.refs_4_), channel_id=1, source_target_pairs={{4,8},{8,4},{5,9},{9,5},{6,10},{10,6},{7,11},{11,7},{20,24},{24,20... | collective-permute-start | bytes 3145736 | tf_op jit(solution)/shard_map/mid_two3/ppermute | solution.py:318
  194.9 26.4 %collective-permute-start.17 = (bf16[256,1024]{1,0:T(8,128)(2,1)}, bf16[256,1024]{1,0:T(8,128)(2,1)}, u32[]{:S(2)}, u32[]{:S(2)}) collective-permute-start(bf16[256,1024]{1,0:T(8,128)(2,1)} %two0.1.refs_4_), channel_id=1, source_target_pairs={{0,4},{12,8},{1,5},{13,9},{2,6},{14,10},{3,7},{15,11},{16,20},{28,... | collective-permute-start | bytes 1572872 | tf_op jit(solution)/shard_map/send6/ppermute | solution.py:315
  213.0 24.2 %collective-permute-start.16 = (bf16[256,1536]{1,0:T(8,128)(2,1)}, bf16[256,1536]{1,0:T(8,128)(2,1)}, u32[]{:S(2)}, u32[]{:S(2)}) collective-permute-start(bf16[256,1536]{1,0:T(8,128)(2,1)} %two1.1), channel_id=1, source_target_pairs={{0,4},{12,8},{1,5},{13,9},{2,6},{14,10},{3,7},{15,11},{16,20},{28,... | collective-permute-start | bytes 2359304 | tf_op jit(solution)/shard_map/send7/ppermute | solution.py:315
  220.5 34.9 %collective-permute-start.22 = (bf16[2,64,6656]{2,1,0:T(8,128)(2,1)}, bf16[2,64,6656]{2,1,0:T(8,128)(2,1)S(1)}, u32[]{:S(2)}, u32[]{:S(2)}) collective-permute-start(bf16[2,64,6656]{2,1,0:T(8,128)(2,1)} %far_terms.1.refs_4_), channel_id=1, source_target_pairs={{4,8},{8,4},{5,9},{9,5},{6,10},{10,6},{7,11},{11,7},{20,24},{24,20... | collective-permute-start | bytes 5111816 | tf_op jit(solution)/shard_map/far_terms/ppermute | solution.py:318
  221.3 34.1 %collective-permute-start.21 = (bf16[256,1024]{1,0:T(8,128)(2,1)S(1)}, bf16[256,1024]{1,0:T(8,128)(2,1)S(1)}, u32[]{:S(2)}, u32[]{:S(2)}) collective-permute-start(bf16[256,1024]{1,0:T(8,128)(2,1)S(1)} %copy-done.34), channel_id=1, source_target_pairs={{0,4},{12,8},{4,0},{8,12},{1,5},{13,9},{5,1},{9,13},{2,6},{14,10},... | collective-permute-start | bytes 1572872 | tf_op jit(solution)/shard_map/send8/ppermute | solution.py:324
  234.0 46.9 %collective-permute-start.20 = (bf16[256,1024]{1,0:T(8,128)(2,1)}, bf16[256,1024]{1,0:T(8,128)(2,1)S(1)}, u32[]{:S(2)}, u32[]{:S(2)}) collective-permute-start(bf16[256,1024]{1,0:T(8,128)(2,1)} %late0.1.refs_1_), channel_id=1, source_target_pairs={{4,8},{8,4},{5,9},{9,5},{6,10},{10,6},{7,11},{11,7},{20,24},{24,20... | collective-permute-start | bytes 1572872 | tf_op jit(solution)/shard_map/mid_late0/ppermute | solution.py:318
  237.2 45.6 %collective-permute-start.19 = (bf16[256,2048]{1,0:T(8,128)(2,1)}, bf16[256,2048]{1,0:T(8,128)(2,1)}, u32[]{:S(2)}, u32[]{:S(2)}) collective-permute-start(bf16[256,2048]{1,0:T(8,128)(2,1)} %two2.1.refs_4_), channel_id=1, source_target_pairs={{0,4},{12,8},{1,5},{13,9},{2,6},{14,10},{3,7},{15,11},{16,20},{28,... | collective-permute-start | bytes 3145736 | tf_op jit(solution)/shard_map/send9/ppermute | solution.py:315
  254.6 46.7 %collective-permute-start.24 = (bf16[256,1536]{1,0:T(8,128)(2,1)}, bf16[256,1536]{1,0:T(8,128)(2,1)S(1)}, u32[]{:S(2)}, u32[]{:S(2)}) collective-permute-start(bf16[256,1536]{1,0:T(8,128)(2,1)} %get-tuple-element.169), channel_id=1, source_target_pairs={{4,8},{8,4},{5,9},{9,5},{6,10},{10,6},{7,11},{11,7},{20,24},{24,20... | collective-permute-start | bytes 2359304 | tf_op jit(solution)/shard_map/pair1/ppermute | solution.py:318
  255.4 47.6 %collective-permute-start.23 = (bf16[256,2048]{1,0:T(8,128)(2,1)}, bf16[256,2048]{1,0:T(8,128)(2,1)}, u32[]{:S(2)}, u32[]{:S(2)}) collective-permute-start(bf16[256,2048]{1,0:T(8,128)(2,1)} %two3.1.refs_4_), channel_id=1, source_target_pairs={{0,4},{12,8},{1,5},{13,9},{2,6},{14,10},{3,7},{15,11},{16,20},{28,... | collective-permute-start | bytes 3145736 | tf_op jit(solution)/shard_map/send10/ppermute | solution.py:315
  275.0 64.4 %collective-permute-start.28 = (bf16[2,64,6656]{2,1,0:T(8,128)(2,1)}, bf16[2,64,6656]{2,1,0:T(8,128)(2,1)}, u32[]{:S(2)}, u32[]{:S(2)}) collective-permute-start(bf16[2,64,6656]{2,1,0:T(8,128)(2,1)} %last_terms.1), channel_id=1, source_target_pairs={{4,0},{8,12},{5,1},{9,13},{6,2},{10,14},{7,3},{11,15},{20,16},{24,... | collective-permute-start | bytes 5111816 | tf_op jit(solution)/shard_map/last_terms/ppermute | solution.py:321
  281.0 79.2 %collective-permute-start.26 = (bf16[2,64,6656]{2,1,0:T(8,128)(2,1)}, bf16[2,64,6656]{2,1,0:T(8,128)(2,1)}, u32[]{:S(2)}, u32[]{:S(2)}) collective-permute-start(bf16[2,64,6656]{2,1,0:T(8,128)(2,1)} %near_terms.1.refs_1_), channel_id=1, source_target_pairs={{4,8},{8,4},{5,9},{9,5},{6,10},{10,6},{7,11},{11,7},{20,24},{24,20... | collective-permute-start | bytes 5111816 | tf_op jit(solution)/shard_map/near_terms/ppermute | solution.py:318
  282.9 54.8 %collective-permute-start.27 = (bf16[256,1536]{1,0:T(8,128)(2,1)}, bf16[256,1536]{1,0:T(8,128)(2,1)}, u32[]{:S(2)}, u32[]{:S(2)}) collective-permute-start(bf16[256,1536]{1,0:T(8,128)(2,1)} %get-tuple-element.162), channel_id=1, source_target_pairs={{0,4},{12,8},{4,0},{8,12},{1,5},{13,9},{5,1},{9,13},{2,6},{14,10},... | collective-permute-start | bytes 2359304 | tf_op jit(solution)/shard_map/send11/ppermute | solution.py:324
  301.3 70.9 %collective-permute-start.29 = (bf16[256,2048]{1,0:T(8,128)(2,1)}, bf16[256,2048]{1,0:T(8,128)(2,1)}, u32[]{:S(2)}, u32[]{:S(2)}) collective-permute-start(bf16[256,2048]{1,0:T(8,128)(2,1)} %get-tuple-element.173.refs_1_), channel_id=1, source_target_pairs={{4,8},{8,4},{5,9},{9,5},{6,10},{10,6},{7,11},{11,7},{20,24},{24,20... | collective-permute-start | bytes 3145736 | tf_op jit(solution)/shard_map/pair2/ppermute | solution.py:318
  302.9 57.2 %collective-permute-start.25 = (bf16[256,2048]{1,0:T(8,128)(2,1)}, bf16[256,2048]{1,0:T(8,128)(2,1)}, u32[]{:S(2)}, u32[]{:S(2)}) collective-permute-start(bf16[256,2048]{1,0:T(8,128)(2,1)} %get-tuple-element.153), channel_id=1, source_target_pairs={{0,4},{12,8},{4,0},{8,12},{1,5},{13,9},{5,1},{9,13},{2,6},{14,10},... | collective-permute-start | bytes 3145736 | tf_op jit(solution)/shard_map/send12/ppermute | solution.py:324
  337.7 37.6 %collective-permute-start.30 = (bf16[256,2048]{1,0:T(8,128)(2,1)}, bf16[256,2048]{1,0:T(8,128)(2,1)}, u32[]{:S(2)}, u32[]{:S(2)}) collective-permute-start(bf16[256,2048]{1,0:T(8,128)(2,1)} %get-tuple-element.175), channel_id=1, source_target_pairs={{4,8},{8,4},{5,9},{9,5},{6,10},{10,6},{7,11},{11,7},{20,24},{24,20... | collective-permute-start | bytes 3145736 | tf_op jit(solution)/shard_map/pair3/ppermute | solution.py:318
  339.4 40.9 %collective-permute-start.31 = (bf16[256,2048]{1,0:T(8,128)(2,1)}, bf16[256,2048]{1,0:T(8,128)(2,1)}, u32[]{:S(2)}, u32[]{:S(2)}) collective-permute-start(bf16[256,2048]{1,0:T(8,128)(2,1)} %get-tuple-element.176), channel_id=1, source_target_pairs={{0,4},{12,8},{4,0},{8,12},{1,5},{13,9},{5,1},{9,13},{2,6},{14,10},... | collective-permute-start | bytes 3145736 | tf_op jit(solution)/shard_map/send13/ppermute | solution.py:324
  (43 other events, 554.5 us)
Sparse Core Ops, SparseCore 0:
  52.5 23.8 all-gather.11
  89.9 21.8 all-gather.5
  114.6 19.8 reduce-scatter.1
  136.0 20.8 all-gather.9
  158.3 22.9 all-gather.7
  213.1 92.9 all-reduce.2
